TPU v7x, 512 devices: a whole 4x4x16 slice. The times are simulated.
512 devices in a mesh: band: 8 (over x, core), dom: 64 (over y, z).
Axes of the slice: x: 4, y: 4, z: 16, core: 2. Of those that a mesh axis runs over, the one named last changes fastest.
Arguments:
- orbitals: float32 [64, 512, 16, 64], P('band', 'dom'), may hold values from -6 to 6
- spin_group: int32 [64], P('band'), may hold values from 0 to 1
- occupation: int32 [64], P('band'), may hold values from 1 to 16
- potential_guess: float32 [1024, 32, 128], P('dom'), may hold values from -6 to 6
Outputs:
- potential: float32 [1024, 32, 128], P('dom')
- magnetization: float32 [1024, 32, 128], P('dom')
All inputs are finite; a program needn't handle non-finite values.
Results may differ from a plain program's by a relative error of at most 0.00016.
Values sent between devices are 32-bit elements; how exact they have to be, the bound alone decides.
No kernel may reach another device: no remote copies, remote signals or barrier semaphores. Data moves between devices by JAX's collectives and lax.ppermute only.
A program may use at most 64 MiB of HBM per device.

v0:
```python
import jax
import jax.numpy as jnp
from jax import lax
from jax.sharding import PartitionSpec as P

SPINS = 2
DEN = 16
LEVELS = 5
NU = 2
COARSE_SWEEPS = 4


OMEGA = 2.0 / 3.0
SOURCE_SCALE = 0.6


def extended(block, sides, width):
    for axis, dim in sides:
        count = lax.axis_size(axis)
        forward = [(i, i + 1) for i in range(count - 1)]
        backward = [(target, source) for source, target in forward]
        low = lax.ppermute(
            lax.slice_in_dim(block, block.shape[dim] - width, None, axis=dim), axis, forward
        )
        high = lax.ppermute(lax.slice_in_dim(block, 0, width, axis=dim), axis, backward)
        block = jnp.concatenate([low, block, high], axis=dim)
    return block


def refine_from(coarse, padded, axis):
    count = coarse.shape[axis]
    lower = lax.slice_in_dim(padded, 0, count, axis=axis)
    upper = lax.slice_in_dim(padded, 2, count + 2, axis=axis)
    first = 0.75 * coarse + 0.25 * lower
    second = 0.75 * coarse + 0.25 * upper
    both = jnp.stack([first, second], axis=axis + 1)
    shape = list(coarse.shape)
    shape[axis] = 2 * count
    return both.reshape(shape)


def refine_local(coarse, axis):
    widths = [(0, 0)] * coarse.ndim
    widths[axis] = (1, 1)
    return refine_from(coarse, jnp.pad(coarse, widths), axis)


def refine_rest(coarse, padded):
    fine = refine_from(coarse, padded, 1)
    fine = refine_local(fine, 2)
    return refine_local(fine, 3)


def neighbour_sum(field, xpad):
    total = xpad[2:] + xpad[:-2]
    ypad = jnp.pad(field, ((0, 0), (1, 1), (0, 0)))
    total = total + ypad[:, 2:] + ypad[:, :-2]
    zpad = jnp.pad(field, ((0, 0), (0, 0), (1, 1)))
    return total + zpad[:, :, 2:] + zpad[:, :, :-2]


def sweep(field, right):
    xpad = extended(field, (("dom", 0),), 1)
    applied = 6.0 * field - neighbour_sum(field, xpad)
    return field + OMEGA * (right - applied) / 6.0


def leftover_of(field, right):
    xpad = extended(field, (("dom", 0),), 1)
    return right - (6.0 * field - neighbour_sum(field, xpad))


def restrict(field):
    a, b, c = field.shape
    return 0.5 * field.reshape(a // 2, 2, b // 2, 2, c // 2, 2).sum(axis=(1, 3, 5))


def prolong(field):
    a, b, c = field.shape
    spread = jnp.broadcast_to(field[:, None, :, None, :, None], (a, 2, b, 2, c, 2))
    return spread.reshape(2 * a, 2 * b, 2 * c)


def coarsest_solve(right):
    correction = OMEGA * right / 6.0
    for turn in range(COARSE_SWEEPS - 1):
        correction = sweep(correction, right)
    return correction


def vcycle(right, level):
    if level == LEVELS - 1:
        return coarsest_solve(right)
    correction = OMEGA * right / 6.0
    correction = sweep(correction, right)
    leftover = leftover_of(correction, right)
    correction = correction + prolong(vcycle(restrict(leftover), level + 1))
    for turn in range(NU):
        correction = sweep(correction, right)
    return correction


def on_device(orbitals, spin_group, occupation, potential_guess):
    channels = jnp.arange(SPINS, dtype=jnp.int32)[:, None]
    weights = (spin_group[None, :] == channels).astype(jnp.float32) * (
        occupation[None, :].astype(jnp.float32) * (0.125 / DEN)
    )
    squares = (orbitals * orbitals).reshape(orbitals.shape[0], -1)
    coarse = jnp.dot(
        weights, squares, precision=lax.Precision.HIGHEST, preferred_element_type=jnp.float32
    )
    coarse = coarse.reshape((SPINS,) + orbitals.shape[1:])
    padded = extended(coarse, (("dom", 1),), 1)
    fine = lax.psum(refine_rest(coarse, padded), "band")
    magnetization = fine[0] - fine[1]
    source = SOURCE_SCALE * (fine[0] + fine[1])
    guess_pad = extended(potential_guess, (("dom", 0),), 1)
    defect = source - (6.0 * potential_guess - neighbour_sum(potential_guess, guess_pad))
    potential = potential_guess + vcycle(defect, 0)
    return (potential, magnetization)


def solution(mesh):
    placed = (P("band", "dom", None, None), P("band"), P("band"), P("dom", None, None))
    return jax.shard_map(
        on_device,
        mesh=mesh,
        in_specs=placed,
        out_specs=(P("dom", None, None), P("dom", None, None)),
        check_vma=False,
    )
```

profile of v0, /device:TPU:24, one launch (start us, length us, event | category | flops | bytes accessed | tf_op | source)
XLA Modules:
  0.0 387.1 jit_solution(17413216513542498143)
XLA Ops:
  10.4 3.8 collective-permute-start
  14.2 9.7 %collective-permute-start.1 = (f32[2,1,16,64]{3,0,2,1:T(2,128)S(1)}, f32[2,1,16,64]{3,0,2,1:T(2,128)S(1)}, u32[]{:S(2)}, u32[]{:S(2)}) collective-permute-start(f32[2,1,16,64]{3,0,2,1:T(2,128)S(1)} %get-tuple-element.31), channel_id=1, source_target_pairs={{1,0},{2,1},{3,2},{4,3},{5,4},{6,5},{7,6},{8,7},{9,8},{10,9},{11,1... | collective-permute-start | bytes 24584 | tf_op jit(solution)/shard_map/ppermute | solution.py:25
  26.4 2.9 copy.86
  29.4 1.9 collective-permute-start.3
  31.3 6.3 %collective-permute-start.2 = (f32[1,32,128]{2,1,0:T(8,128)S(1)}, f32[1,32,128]{2,1,0:T(8,128)S(1)}, u32[]{:S(2)}, u32[]{:S(2)}) collective-permute-start(f32[1,32,128]{2,1,0:T(8,128)S(1)} %get-tuple-element.27), channel_id=1, source_target_pairs={{1,0},{2,1},{3,2},{4,3},{5,4},{6,5},{7,6},{8,7},{9,8},{10,9},{11,1... | collective-permute-start | bytes 49160 | tf_op jit(solution)/shard_map/ppermute | solution.py:25
  41.0 68.2 %all-reduce.44.cloned.1.call-done = f32[2,16,32,128]{2,1,3,0:T(8,128)} async-done(((f32[2,16,32,128]{2,1,3,0:T(8,128)}), f32[2,16,32,128]{2,1,3,0:T(8,128)}) %all-reduce.44.cloned.1.call-update) | async-done | bytes 524304 | tf_op jit(solution)/shard_map/psum | solution.py:114
  109.2 2.5 broadcast_multiply_fusion
  111.8 6.2 %collective-permute-start.4 = (f32[1,32,128]{1,0,2:T(1,128)S(1)}, f32[1,32,128]{1,0,2:T(1,128)S(1)}, u32[]{:S(2)}, u32[]{:S(2)}) collective-permute-start(f32[1,32,128]{1,0,2:T(1,128)S(1)} %get-tuple-element.18), channel_id=1, source_target_pairs={{1,0},{2,1},{3,2},{4,3},{5,4},{6,5},{7,6},{8,7},{9,8},{10,9},{11,1... | collective-permute-start | bytes 49160 | tf_op jit(solution)/shard_map/ppermute | solution.py:25
  118.0 1.9 collective-permute-start.5
  119.9 6.3 %collective-permute-done.5 = f32[1,32,128]{1,0,2:T(1,128)S(1)} collective-permute-done((f32[1,32,128]{1,0,2:T(1,128)S(1)}, f32[1,32,128]{1,0,2:T(1,128)S(1)}, u32[]{:S(2)}, u32[]{:S(2)}) %collective-permute-start.5) | collective-permute-done | bytes 16416 | tf_op jit(solution)/shard_map/ppermute | solution.py:22
  127.4 1.9 collective-permute-start.6
  129.3 3.9 %collective-permute-start.7 = (f32[1,32,128]{1,0,2:T(1,128)S(1)}, f32[1,32,128]{1,0,2:T(1,128)S(1)}, u32[]{:S(2)}, u32[]{:S(2)}) collective-permute-start(f32[1,32,128]{1,0,2:T(1,128)S(1)} %get-tuple-element.17), channel_id=1, source_target_pairs={{0,1},{1,2},{2,3},{3,4},{4,5},{5,6},{6,7},{7,8},{8,9},{9,10},{10,1... | collective-permute-start | bytes 49160 | tf_op jit(solution)/shard_map/ppermute | solution.py:22
  133.5 4.0 %collective-permute-done.7 = f32[1,32,128]{1,0,2:T(1,128)S(1)} collective-permute-done((f32[1,32,128]{1,0,2:T(1,128)S(1)}, f32[1,32,128]{1,0,2:T(1,128)S(1)}, u32[]{:S(2)}, u32[]{:S(2)}) %collective-permute-start.7) | collective-permute-done | bytes 16416 | tf_op jit(solution)/shard_map/ppermute | solution.py:22
  141.0 18.1 %reshape.89 = f32[8,2,16,2,64,2]{5,4,3,2,1,0:T(8,128)} reshape(f32[16,32,128]{2,1,0:T(8,128)S(1)} %copy.92) | data formatting | bytes 524288 | tf_op jit(solution)/shard_map/reshape | solution.py:75
  159.1 7.0 %reduce_sum.43 = f32[8,16,64]{2,1,0:T(8,128)S(1)} reduce(f32[8,2,16,2,64,2]{5,4,3,2,1,0:T(8,128)} %reshape.89, f32[]{:T(128)} %constant.76.clone.1), dimensions={1,3,5}, to_apply=%region_1.2 | reduce | flops 57344 | bytes 294916 | tf_op jit(solution)/shard_map/reduce_sum | solution.py:75
  166.1 1.9 collective-permute-start.8
  168.0 3.9 %collective-permute-start.9 = (f32[1,16,64]{2,1,0:T(8,128)S(1)}, f32[1,16,64]{2,1,0:T(8,128)S(1)}, u32[]{:S(2)}, u32[]{:S(2)}) collective-permute-start(f32[1,16,64]{2,1,0:T(8,128)S(1)} %get-tuple-element.39), channel_id=1, source_target_pairs={{0,1},{1,2},{2,3},{3,4},{4,5},{5,6},{6,7},{7,8},{8,9},{9,10},{10,1... | collective-permute-start | bytes 12296 | tf_op jit(solution)/shard_map/ppermute | solution.py:22
  172.0 3.7 collective-permute-done.9
  175.8 1.9 collective-permute-start.10
  177.7 4.1 %collective-permute-start.11 = (f32[1,16,64]{2,1,0:T(8,128)S(1)}, f32[1,16,64]{2,1,0:T(8,128)S(1)}, u32[]{:S(2)}, u32[]{:S(2)}) collective-permute-start(f32[1,16,64]{2,1,0:T(8,128)S(1)} %get-tuple-element.37), channel_id=1, source_target_pairs={{0,1},{1,2},{2,3},{3,4},{4,5},{5,6},{6,7},{7,8},{8,9},{9,10},{10,1... | collective-permute-start | bytes 12296 | tf_op jit(solution)/shard_map/ppermute | solution.py:22
  181.9 3.5 collective-permute-done.11
  185.5 3.5 reshape.90
  190.8 1.9 collective-permute-start.12
  192.8 3.9 %collective-permute-start.13 = (f32[1,8,32]{2,1,0:T(8,128)S(1)}, f32[1,8,32]{2,1,0:T(8,128)S(1)}, u32[]{:S(2)}, u32[]{:S(2)}) collective-permute-start(f32[1,8,32]{2,1,0:T(8,128)S(1)} %get-tuple-element.47), channel_id=1, source_target_pairs={{0,1},{1,2},{2,3},{3,4},{4,5},{5,6},{6,7},{7,8},{8,9},{9,10},{10,1... | collective-permute-start | bytes 3080 | tf_op jit(solution)/shard_map/ppermute | solution.py:22
  196.7 3.7 collective-permute-done.13
  200.5 1.9 collective-permute-start.14
  202.4 3.9 %collective-permute-start.15 = (f32[1,8,32]{2,1,0:T(8,128)S(1)}, f32[1,8,32]{2,1,0:T(8,128)S(1)}, u32[]{:S(2)}, u32[]{:S(2)}) collective-permute-start(f32[1,8,32]{2,1,0:T(8,128)S(1)} %get-tuple-element.45), channel_id=1, source_target_pairs={{0,1},{1,2},{2,3},{3,4},{4,5},{5,6},{6,7},{7,8},{8,9},{9,10},{10,1... | collective-permute-start | bytes 3080 | tf_op jit(solution)/shard_map/ppermute | solution.py:22
  206.3 3.7 collective-permute-done.15
  213.0 1.9 collective-permute-start.16
  214.9 3.9 %collective-permute-start.17 = (f32[1,4,16]{2,1,0:T(4,128)S(1)}, f32[1,4,16]{2,1,0:T(4,128)S(1)}, u32[]{:S(2)}, u32[]{:S(2)}) collective-permute-start(f32[1,4,16]{2,1,0:T(4,128)S(1)} %get-tuple-element.55), channel_id=1, source_target_pairs={{0,1},{1,2},{2,3},{3,4},{4,5},{5,6},{6,7},{7,8},{8,9},{9,10},{10,1... | collective-permute-start | bytes 776 | tf_op jit(solution)/shard_map/ppermute | solution.py:22
  218.8 3.6 collective-permute-done.17
  225.2 3.9 %collective-permute-start.19 = (f32[1,4,16]{2,1,0:T(4,128)S(1)}, f32[1,4,16]{2,1,0:T(4,128)S(1)}, u32[]{:S(2)}, u32[]{:S(2)}) collective-permute-start(f32[1,4,16]{2,1,0:T(4,128)S(1)} %get-tuple-element.53), channel_id=1, source_target_pairs={{0,1},{1,2},{2,3},{3,4},{4,5},{5,6},{6,7},{7,8},{8,9},{9,10},{10,1... | collective-permute-start | bytes 776 | tf_op jit(solution)/shard_map/ppermute | solution.py:22
  229.1 3.6 collective-permute-done.19
  233.7 1.9 collective-permute-start.21
  235.6 6.0 %collective-permute-start.20 = (f32[1,2,8]{2,1,0:T(2,128)S(1)}, f32[1,2,8]{2,1,0:T(2,128)S(1)}, u32[]{:S(2)}, u32[]{:S(2)}) collective-permute-start(f32[1,2,8]{2,1,0:T(2,128)S(1)} %multiply_bitcast_fusion), channel_id=1, source_target_pairs={{1,0},{2,1},{3,2},{4,3},{5,4},{6,5},{7,6},{8,7},{9,8},{10,9},{11,1... | collective-permute-start | bytes 200 | tf_op jit(solution)/shard_map/ppermute | solution.py:25
  245.0 6.3 %collective-permute-start.22 = (f32[1,2,8]{2,1,0:T(2,128)S(1)}, f32[1,2,8]{2,1,0:T(2,128)S(1)}, u32[]{:S(2)}, u32[]{:S(2)}) collective-permute-start(f32[1,2,8]{2,1,0:T(2,128)S(1)} %fusion.170), channel_id=1, source_target_pairs={{1,0},{2,1},{3,2},{4,3},{5,4},{6,5},{7,6},{8,7},{9,8},{10,9},{11,1... | collective-permute-start | bytes 200 | tf_op jit(solution)/shard_map/ppermute | solution.py:25
  254.5 6.3 %collective-permute-start.24 = (f32[1,2,8]{2,1,0:T(2,128)S(1)}, f32[1,2,8]{2,1,0:T(2,128)S(1)}, u32[]{:S(2)}, u32[]{:S(2)}) collective-permute-start(f32[1,2,8]{2,1,0:T(2,128)S(1)} %fusion.172), channel_id=1, source_target_pairs={{1,0},{2,1},{3,2},{4,3},{5,4},{6,5},{7,6},{8,7},{9,8},{10,9},{11,1... | collective-permute-start | bytes 200 | tf_op jit(solution)/shard_map/ppermute | solution.py:25
  262.4 6.3 %collective-permute-start.26 = (f32[1,4,16]{2,1,0:T(4,128)S(1)}, f32[1,4,16]{2,1,0:T(4,128)S(1)}, u32[]{:S(2)}, u32[]{:S(2)}) collective-permute-start(f32[1,4,16]{2,1,0:T(4,128)S(1)} %get-tuple-element.50), channel_id=1, source_target_pairs={{1,0},{2,1},{3,2},{4,3},{5,4},{6,5},{7,6},{8,7},{9,8},{10,9},{11,1... | collective-permute-start | bytes 776 | tf_op jit(solution)/shard_map/ppermute | solution.py:25
  268.6 1.9 collective-permute-start.27
  270.6 5.6 %collective-permute-done.27 = f32[1,4,16]{2,1,0:T(4,128)S(1)} collective-permute-done((f32[1,4,16]{2,1,0:T(4,128)S(1)}, f32[1,4,16]{2,1,0:T(4,128)S(1)}, u32[]{:S(2)}, u32[]{:S(2)}) %collective-permute-start.27) | collective-permute-done | bytes 288 | tf_op jit(solution)/shard_map/ppermute | solution.py:22
  278.9 3.9 %collective-permute-start.29 = (f32[1,4,16]{2,1,0:T(4,128)S(1)}, f32[1,4,16]{2,1,0:T(4,128)S(1)}, u32[]{:S(2)}, u32[]{:S(2)}) collective-permute-start(f32[1,4,16]{2,1,0:T(4,128)S(1)} %get-tuple-element.49), channel_id=1, source_target_pairs={{0,1},{1,2},{2,3},{3,4},{4,5},{5,6},{6,7},{7,8},{8,9},{9,10},{10,1... | collective-permute-start | bytes 776 | tf_op jit(solution)/shard_map/ppermute | solution.py:22
  282.9 3.6 collective-permute-done.29
  290.8 3.9 %collective-permute-start.31 = (f32[1,8,32]{2,1,0:T(8,128)S(1)}, f32[1,8,32]{2,1,0:T(8,128)S(1)}, u32[]{:S(2)}, u32[]{:S(2)}) collective-permute-start(f32[1,8,32]{2,1,0:T(8,128)S(1)} %get-tuple-element.43), channel_id=1, source_target_pairs={{0,1},{1,2},{2,3},{3,4},{4,5},{5,6},{6,7},{7,8},{8,9},{9,10},{10,1... | collective-permute-start | bytes 3080 | tf_op jit(solution)/shard_map/ppermute | solution.py:22
  294.7 3.7 collective-permute-done.31
  298.5 1.9 collective-permute-start.32
  300.4 3.9 %collective-permute-start.33 = (f32[1,8,32]{2,1,0:T(8,128)S(1)}, f32[1,8,32]{2,1,0:T(8,128)S(1)}, u32[]{:S(2)}, u32[]{:S(2)}) collective-permute-start(f32[1,8,32]{2,1,0:T(8,128)S(1)} %get-tuple-element.41), channel_id=1, source_target_pairs={{0,1},{1,2},{2,3},{3,4},{4,5},{5,6},{6,7},{7,8},{8,9},{9,10},{10,1... | collective-permute-start | bytes 3080 | tf_op jit(solution)/shard_map/ppermute | solution.py:22
  304.3 3.7 collective-permute-done.33
  309.8 3.2 reshape.93
  313.0 1.9 collective-permute-start.34
  314.9 3.9 %collective-permute-start.35 = (f32[1,16,64]{2,1,0:T(8,128)S(1)}, f32[1,16,64]{2,1,0:T(8,128)S(1)}, u32[]{:S(2)}, u32[]{:S(2)}) collective-permute-start(f32[1,16,64]{2,1,0:T(8,128)S(1)} %get-tuple-element.35), channel_id=1, source_target_pairs={{0,1},{1,2},{2,3},{3,4},{4,5},{5,6},{6,7},{7,8},{8,9},{9,10},{10,1... | collective-permute-start | bytes 12296 | tf_op jit(solution)/shard_map/ppermute | solution.py:22
  318.9 3.7 collective-permute-done.35
  322.7 1.9 collective-permute-start.36
  324.7 3.9 %collective-permute-start.37 = (f32[1,16,64]{2,1,0:T(8,128)S(1)}, f32[1,16,64]{2,1,0:T(8,128)S(1)}, u32[]{:S(2)}, u32[]{:S(2)}) collective-permute-start(f32[1,16,64]{2,1,0:T(8,128)S(1)} %get-tuple-element.33), channel_id=1, source_target_pairs={{0,1},{1,2},{2,3},{3,4},{4,5},{5,6},{6,7},{7,8},{8,9},{9,10},{10,1... | collective-permute-start | bytes 12296 | tf_op jit(solution)/shard_map/ppermute | solution.py:22
  328.6 3.7 collective-permute-done.37
  332.4 6.5 %broadcast_in_dim.39 = f32[8,2,16,2,64,2]{5,4,3,2,1,0:T(8,128)} broadcast(f32[8,16,64]{2,1,0:T(8,128)S(1)} %fusion.78), dimensions={0,2,4} | broadcast | bytes 294912 | tf_op jit(solution)/shard_map/broadcast_in_dim | solution.py:80
  338.9 12.6 %reshape.94 = f32[16,32,128]{2,1,0:T(8,128)S(1)} reshape(f32[8,2,16,2,64,2]{5,4,3,2,1,0:T(8,128)} %broadcast_in_dim.39) | data formatting | bytes 524288 | tf_op jit(solution)/shard_map/reshape | solution.py:81
  354.4 2.1 collective-permute-start.38
  356.4 3.9 %collective-permute-start.39 = (f32[1,32,128]{1,0,2:T(1,128)S(1)}, f32[1,32,128]{1,0,2:T(1,128)S(1)}, u32[]{:S(2)}, u32[]{:S(2)}) collective-permute-start(f32[1,32,128]{1,0,2:T(1,128)S(1)} %get-tuple-element.15), channel_id=1, source_target_pairs={{0,1},{1,2},{2,3},{3,4},{4,5},{5,6},{6,7},{7,8},{8,9},{9,10},{10,1... | collective-permute-start | bytes 49160 | tf_op jit(solution)/shard_map/ppermute | solution.py:22
  360.7 4.0 %collective-permute-done.39 = f32[1,32,128]{1,0,2:T(1,128)S(1)} collective-permute-done((f32[1,32,128]{1,0,2:T(1,128)S(1)}, f32[1,32,128]{1,0,2:T(1,128)S(1)}, u32[]{:S(2)}, u32[]{:S(2)}) %collective-permute-start.39) | collective-permute-done | bytes 16416 | tf_op jit(solution)/shard_map/ppermute | solution.py:22
  365.8 1.9 collective-permute-start.40
  367.7 3.9 %collective-permute-start.41 = (f32[1,32,128]{1,0,2:T(1,128)S(1)}, f32[1,32,128]{1,0,2:T(1,128)S(1)}, u32[]{:S(2)}, u32[]{:S(2)}) collective-permute-start(f32[1,32,128]{1,0,2:T(1,128)S(1)} %get-tuple-element.13), channel_id=1, source_target_pairs={{0,1},{1,2},{2,3},{3,4},{4,5},{5,6},{6,7},{7,8},{8,9},{9,10},{10,1... | collective-permute-start | bytes 49160 | tf_op jit(solution)/shard_map/ppermute | solution.py:22
  372.8 2.3 copy.96
  376.0 1.9 fusion.9
  377.9 2.3 copy.95
  (117 shorter events, 45.9 us)
Async XLA Ops:
  7.2 2.4 copy-start.3
  7.2 102.0 %all-reduce.44.cloned.1.call-start = ((), (), s32[]{:S(2)}) async-start(), calls=%async_computation | async-start | bytes 4194304 | tf_op jit(solution)/shard_map/psum | solution.py:114
  10.4 13.5 %collective-permute-start = (f32[2,1,16,64]{3,0,2,1:T(2,128)S(1)}, f32[2,1,16,64]{3,0,2,1:T(2,128)S(1)}, u32[]{:S(2)}, u32[]{:S(2)}) collective-permute-start(f32[2,1,16,64]{3,0,2,1:T(2,128)S(1)} %get-tuple-element.30), channel_id=1, source_target_pairs={{0,1},{1,2},{2,3},{3,4},{4,5},{5,6},{6,7},{7,8},{8,9},{9,10},{10,1... | collective-permute-start | bytes 24584 | tf_op jit(solution)/shard_map/ppermute | solution.py:22
  14.2 11.1 %collective-permute-start.1 = (f32[2,1,16,64]{3,0,2,1:T(2,128)S(1)}, f32[2,1,16,64]{3,0,2,1:T(2,128)S(1)}, u32[]{:S(2)}, u32[]{:S(2)}) collective-permute-start(f32[2,1,16,64]{3,0,2,1:T(2,128)S(1)} %get-tuple-element.31), channel_id=1, source_target_pairs={{1,0},{2,1},{3,2},{4,3},{5,4},{6,5},{7,6},{8,7},{9,8},{10,9},{11,1... | collective-permute-start | bytes 24584 | tf_op jit(solution)/shard_map/ppermute | solution.py:25
  26.4 3.0 copy-start.1
  29.4 8.8 %collective-permute-start.3 = (f32[1,32,128]{2,1,0:T(8,128)S(1)}, f32[1,32,128]{2,1,0:T(8,128)S(1)}, u32[]{:S(2)}, u32[]{:S(2)}) collective-permute-start(f32[1,32,128]{2,1,0:T(8,128)S(1)} %get-tuple-element.26), channel_id=1, source_target_pairs={{0,1},{1,2},{2,3},{3,4},{4,5},{5,6},{6,7},{7,8},{8,9},{9,10},{10,1... | collective-permute-start | bytes 49160 | tf_op jit(solution)/shard_map/ppermute | solution.py:22
  31.3 7.7 %collective-permute-start.2 = (f32[1,32,128]{2,1,0:T(8,128)S(1)}, f32[1,32,128]{2,1,0:T(8,128)S(1)}, u32[]{:S(2)}, u32[]{:S(2)}) collective-permute-start(f32[1,32,128]{2,1,0:T(8,128)S(1)} %get-tuple-element.27), channel_id=1, source_target_pairs={{1,0},{2,1},{3,2},{4,3},{5,4},{6,5},{7,6},{8,7},{9,8},{10,9},{11,1... | collective-permute-start | bytes 49160 | tf_op jit(solution)/shard_map/ppermute | solution.py:25
  111.8 8.2 %collective-permute-start.4 = (f32[1,32,128]{1,0,2:T(1,128)S(1)}, f32[1,32,128]{1,0,2:T(1,128)S(1)}, u32[]{:S(2)}, u32[]{:S(2)}) collective-permute-start(f32[1,32,128]{1,0,2:T(1,128)S(1)} %get-tuple-element.18), channel_id=1, source_target_pairs={{1,0},{2,1},{3,2},{4,3},{5,4},{6,5},{7,6},{8,7},{9,8},{10,9},{11,1... | collective-permute-start | bytes 49160 | tf_op jit(solution)/shard_map/ppermute | solution.py:25
  118.0 8.3 %collective-permute-start.5 = (f32[1,32,128]{1,0,2:T(1,128)S(1)}, f32[1,32,128]{1,0,2:T(1,128)S(1)}, u32[]{:S(2)}, u32[]{:S(2)}) collective-permute-start(f32[1,32,128]{1,0,2:T(1,128)S(1)} %get-tuple-element.19), channel_id=1, source_target_pairs={{0,1},{1,2},{2,3},{3,4},{4,5},{5,6},{6,7},{7,8},{8,9},{9,10},{10,1... | collective-permute-start | bytes 49160 | tf_op jit(solution)/shard_map/ppermute | solution.py:22
  127.4 6.2 %collective-permute-start.6 = (f32[1,32,128]{1,0,2:T(1,128)S(1)}, f32[1,32,128]{1,0,2:T(1,128)S(1)}, u32[]{:S(2)}, u32[]{:S(2)}) collective-permute-start(f32[1,32,128]{1,0,2:T(1,128)S(1)} %get-tuple-element.16), channel_id=1, source_target_pairs={{1,0},{2,1},{3,2},{4,3},{5,4},{6,5},{7,6},{8,7},{9,8},{10,9},{11,1... | collective-permute-start | bytes 49160 | tf_op jit(solution)/shard_map/ppermute | solution.py:25
  129.3 8.3 %collective-permute-start.7 = (f32[1,32,128]{1,0,2:T(1,128)S(1)}, f32[1,32,128]{1,0,2:T(1,128)S(1)}, u32[]{:S(2)}, u32[]{:S(2)}) collective-permute-start(f32[1,32,128]{1,0,2:T(1,128)S(1)} %get-tuple-element.17), channel_id=1, source_target_pairs={{0,1},{1,2},{2,3},{3,4},{4,5},{5,6},{6,7},{7,8},{8,9},{9,10},{10,1... | collective-permute-start | bytes 49160 | tf_op jit(solution)/shard_map/ppermute | solution.py:22
  166.1 5.9 %collective-permute-start.8 = (f32[1,16,64]{2,1,0:T(8,128)S(1)}, f32[1,16,64]{2,1,0:T(8,128)S(1)}, u32[]{:S(2)}, u32[]{:S(2)}) collective-permute-start(f32[1,16,64]{2,1,0:T(8,128)S(1)} %get-tuple-element.38), channel_id=1, source_target_pairs={{1,0},{2,1},{3,2},{4,3},{5,4},{6,5},{7,6},{8,7},{9,8},{10,9},{11,1... | collective-permute-start | bytes 12296 | tf_op jit(solution)/shard_map/ppermute | solution.py:25
  168.0 7.7 %collective-permute-start.9 = (f32[1,16,64]{2,1,0:T(8,128)S(1)}, f32[1,16,64]{2,1,0:T(8,128)S(1)}, u32[]{:S(2)}, u32[]{:S(2)}) collective-permute-start(f32[1,16,64]{2,1,0:T(8,128)S(1)} %get-tuple-element.39), channel_id=1, source_target_pairs={{0,1},{1,2},{2,3},{3,4},{4,5},{5,6},{6,7},{7,8},{8,9},{9,10},{10,1... | collective-permute-start | bytes 12296 | tf_op jit(solution)/shard_map/ppermute | solution.py:22
  175.8 6.0 %collective-permute-start.10 = (f32[1,16,64]{2,1,0:T(8,128)S(1)}, f32[1,16,64]{2,1,0:T(8,128)S(1)}, u32[]{:S(2)}, u32[]{:S(2)}) collective-permute-start(f32[1,16,64]{2,1,0:T(8,128)S(1)} %get-tuple-element.36), channel_id=1, source_target_pairs={{1,0},{2,1},{3,2},{4,3},{5,4},{6,5},{7,6},{8,7},{9,8},{10,9},{11,1... | collective-permute-start | bytes 12296 | tf_op jit(solution)/shard_map/ppermute | solution.py:25
  177.7 7.7 %collective-permute-start.11 = (f32[1,16,64]{2,1,0:T(8,128)S(1)}, f32[1,16,64]{2,1,0:T(8,128)S(1)}, u32[]{:S(2)}, u32[]{:S(2)}) collective-permute-start(f32[1,16,64]{2,1,0:T(8,128)S(1)} %get-tuple-element.37), channel_id=1, source_target_pairs={{0,1},{1,2},{2,3},{3,4},{4,5},{5,6},{6,7},{7,8},{8,9},{9,10},{10,1... | collective-permute-start | bytes 12296 | tf_op jit(solution)/shard_map/ppermute | solution.py:22
  190.8 5.9 %collective-permute-start.12 = (f32[1,8,32]{2,1,0:T(8,128)S(1)}, f32[1,8,32]{2,1,0:T(8,128)S(1)}, u32[]{:S(2)}, u32[]{:S(2)}) collective-permute-start(f32[1,8,32]{2,1,0:T(8,128)S(1)} %get-tuple-element.46), channel_id=1, source_target_pairs={{1,0},{2,1},{3,2},{4,3},{5,4},{6,5},{7,6},{8,7},{9,8},{10,9},{11,1... | collective-permute-start | bytes 3080 | tf_op jit(solution)/shard_map/ppermute | solution.py:25
  192.8 7.6 %collective-permute-start.13 = (f32[1,8,32]{2,1,0:T(8,128)S(1)}, f32[1,8,32]{2,1,0:T(8,128)S(1)}, u32[]{:S(2)}, u32[]{:S(2)}) collective-permute-start(f32[1,8,32]{2,1,0:T(8,128)S(1)} %get-tuple-element.47), channel_id=1, source_target_pairs={{0,1},{1,2},{2,3},{3,4},{4,5},{5,6},{6,7},{7,8},{8,9},{9,10},{10,1... | collective-permute-start | bytes 3080 | tf_op jit(solution)/shard_map/ppermute | solution.py:22
  200.5 9.5 %copy-start.2 = (f32[4,8,32]{2,1,0:T(8,128)}, f32[4,8,32]{2,1,0:T(8,128)S(1)}, u32[]{:S(2)}) copy-start(f32[4,8,32]{2,1,0:T(8,128)S(1)} %fusion.90) | copy-start | bytes 12292
  200.5 5.9 %collective-permute-start.14 = (f32[1,8,32]{2,1,0:T(8,128)S(1)}, f32[1,8,32]{2,1,0:T(8,128)S(1)}, u32[]{:S(2)}, u32[]{:S(2)}) collective-permute-start(f32[1,8,32]{2,1,0:T(8,128)S(1)} %get-tuple-element.44), channel_id=1, source_target_pairs={{1,0},{2,1},{3,2},{4,3},{5,4},{6,5},{7,6},{8,7},{9,8},{10,9},{11,1... | collective-permute-start | bytes 3080 | tf_op jit(solution)/shard_map/ppermute | solution.py:25
  202.4 7.6 %collective-permute-start.15 = (f32[1,8,32]{2,1,0:T(8,128)S(1)}, f32[1,8,32]{2,1,0:T(8,128)S(1)}, u32[]{:S(2)}, u32[]{:S(2)}) collective-permute-start(f32[1,8,32]{2,1,0:T(8,128)S(1)} %get-tuple-element.45), channel_id=1, source_target_pairs={{0,1},{1,2},{2,3},{3,4},{4,5},{5,6},{6,7},{7,8},{8,9},{9,10},{10,1... | collective-permute-start | bytes 3080 | tf_op jit(solution)/shard_map/ppermute | solution.py:22
  213.0 5.8 %collective-permute-start.16 = (f32[1,4,16]{2,1,0:T(4,128)S(1)}, f32[1,4,16]{2,1,0:T(4,128)S(1)}, u32[]{:S(2)}, u32[]{:S(2)}) collective-permute-start(f32[1,4,16]{2,1,0:T(4,128)S(1)} %get-tuple-element.54), channel_id=1, source_target_pairs={{1,0},{2,1},{3,2},{4,3},{5,4},{6,5},{7,6},{8,7},{9,8},{10,9},{11,1... | collective-permute-start | bytes 776 | tf_op jit(solution)/shard_map/ppermute | solution.py:25
  214.9 7.6 %collective-permute-start.17 = (f32[1,4,16]{2,1,0:T(4,128)S(1)}, f32[1,4,16]{2,1,0:T(4,128)S(1)}, u32[]{:S(2)}, u32[]{:S(2)}) collective-permute-start(f32[1,4,16]{2,1,0:T(4,128)S(1)} %get-tuple-element.55), channel_id=1, source_target_pairs={{0,1},{1,2},{2,3},{3,4},{4,5},{5,6},{6,7},{7,8},{8,9},{9,10},{10,1... | collective-permute-start | bytes 776 | tf_op jit(solution)/shard_map/ppermute | solution.py:22
  223.3 5.8 %collective-permute-start.18 = (f32[1,4,16]{2,1,0:T(4,128)S(1)}, f32[1,4,16]{2,1,0:T(4,128)S(1)}, u32[]{:S(2)}, u32[]{:S(2)}) collective-permute-start(f32[1,4,16]{2,1,0:T(4,128)S(1)} %get-tuple-element.52), channel_id=1, source_target_pairs={{1,0},{2,1},{3,2},{4,3},{5,4},{6,5},{7,6},{8,7},{9,8},{10,9},{11,1... | collective-permute-start | bytes 776 | tf_op jit(solution)/shard_map/ppermute | solution.py:25
  225.2 7.6 %collective-permute-start.19 = (f32[1,4,16]{2,1,0:T(4,128)S(1)}, f32[1,4,16]{2,1,0:T(4,128)S(1)}, u32[]{:S(2)}, u32[]{:S(2)}) collective-permute-start(f32[1,4,16]{2,1,0:T(4,128)S(1)} %get-tuple-element.53), channel_id=1, source_target_pairs={{0,1},{1,2},{2,3},{3,4},{4,5},{5,6},{6,7},{7,8},{8,9},{9,10},{10,1... | collective-permute-start | bytes 776 | tf_op jit(solution)/shard_map/ppermute | solution.py:22
  233.7 8.0 %collective-permute-start.21 = (f32[1,2,8]{2,1,0:T(2,128)S(1)}, f32[1,2,8]{2,1,0:T(2,128)S(1)}, u32[]{:S(2)}, u32[]{:S(2)}) collective-permute-start(f32[1,2,8]{2,1,0:T(2,128)S(1)} %multiply_bitcast_fusion), channel_id=1, source_target_pairs={{0,1},{1,2},{2,3},{3,4},{4,5},{5,6},{6,7},{7,8},{8,9},{9,10},{10,1... | collective-permute-start | bytes 200 | tf_op jit(solution)/shard_map/ppermute | solution.py:22
  235.6 7.3 %collective-permute-start.20 = (f32[1,2,8]{2,1,0:T(2,128)S(1)}, f32[1,2,8]{2,1,0:T(2,128)S(1)}, u32[]{:S(2)}, u32[]{:S(2)}) collective-permute-start(f32[1,2,8]{2,1,0:T(2,128)S(1)} %multiply_bitcast_fusion), channel_id=1, source_target_pairs={{1,0},{2,1},{3,2},{4,3},{5,4},{6,5},{7,6},{8,7},{9,8},{10,9},{11,1... | collective-permute-start | bytes 200 | tf_op jit(solution)/shard_map/ppermute | solution.py:25
  243.0 8.2 %collective-permute-start.23 = (f32[1,2,8]{2,1,0:T(2,128)S(1)}, f32[1,2,8]{2,1,0:T(2,128)S(1)}, u32[]{:S(2)}, u32[]{:S(2)}) collective-permute-start(f32[1,2,8]{2,1,0:T(2,128)S(1)} %fusion.170), channel_id=1, source_target_pairs={{0,1},{1,2},{2,3},{3,4},{4,5},{5,6},{6,7},{7,8},{8,9},{9,10},{10,1... | collective-permute-start | bytes 200 | tf_op jit(solution)/shard_map/ppermute | solution.py:22
  245.0 7.6 %collective-permute-start.22 = (f32[1,2,8]{2,1,0:T(2,128)S(1)}, f32[1,2,8]{2,1,0:T(2,128)S(1)}, u32[]{:S(2)}, u32[]{:S(2)}) collective-permute-start(f32[1,2,8]{2,1,0:T(2,128)S(1)} %fusion.170), channel_id=1, source_target_pairs={{1,0},{2,1},{3,2},{4,3},{5,4},{6,5},{7,6},{8,7},{9,8},{10,9},{11,1... | collective-permute-start | bytes 200 | tf_op jit(solution)/shard_map/ppermute | solution.py:25
  252.6 8.2 %collective-permute-start.25 = (f32[1,2,8]{2,1,0:T(2,128)S(1)}, f32[1,2,8]{2,1,0:T(2,128)S(1)}, u32[]{:S(2)}, u32[]{:S(2)}) collective-permute-start(f32[1,2,8]{2,1,0:T(2,128)S(1)} %fusion.172), channel_id=1, source_target_pairs={{0,1},{1,2},{2,3},{3,4},{4,5},{5,6},{6,7},{7,8},{8,9},{9,10},{10,1... | collective-permute-start | bytes 200 | tf_op jit(solution)/shard_map/ppermute | solution.py:22
  254.5 7.6 %collective-permute-start.24 = (f32[1,2,8]{2,1,0:T(2,128)S(1)}, f32[1,2,8]{2,1,0:T(2,128)S(1)}, u32[]{:S(2)}, u32[]{:S(2)}) collective-permute-start(f32[1,2,8]{2,1,0:T(2,128)S(1)} %fusion.172), channel_id=1, source_target_pairs={{1,0},{2,1},{3,2},{4,3},{5,4},{6,5},{7,6},{8,7},{9,8},{10,9},{11,1... | collective-permute-start | bytes 200 | tf_op jit(solution)/shard_map/ppermute | solution.py:25
  262.4 8.2 %collective-permute-start.26 = (f32[1,4,16]{2,1,0:T(4,128)S(1)}, f32[1,4,16]{2,1,0:T(4,128)S(1)}, u32[]{:S(2)}, u32[]{:S(2)}) collective-permute-start(f32[1,4,16]{2,1,0:T(4,128)S(1)} %get-tuple-element.50), channel_id=1, source_target_pairs={{1,0},{2,1},{3,2},{4,3},{5,4},{6,5},{7,6},{8,7},{9,8},{10,9},{11,1... | collective-permute-start | bytes 776 | tf_op jit(solution)/shard_map/ppermute | solution.py:25
  268.6 7.6 %collective-permute-start.27 = (f32[1,4,16]{2,1,0:T(4,128)S(1)}, f32[1,4,16]{2,1,0:T(4,128)S(1)}, u32[]{:S(2)}, u32[]{:S(2)}) collective-permute-start(f32[1,4,16]{2,1,0:T(4,128)S(1)} %get-tuple-element.51), channel_id=1, source_target_pairs={{0,1},{1,2},{2,3},{3,4},{4,5},{5,6},{6,7},{7,8},{8,9},{9,10},{10,1... | collective-permute-start | bytes 776 | tf_op jit(solution)/shard_map/ppermute | solution.py:22
  277.0 5.8 %collective-permute-start.28 = (f32[1,4,16]{2,1,0:T(4,128)S(1)}, f32[1,4,16]{2,1,0:T(4,128)S(1)}, u32[]{:S(2)}, u32[]{:S(2)}) collective-permute-start(f32[1,4,16]{2,1,0:T(4,128)S(1)} %get-tuple-element.48), channel_id=1, source_target_pairs={{1,0},{2,1},{3,2},{4,3},{5,4},{6,5},{7,6},{8,7},{9,8},{10,9},{11,1... | collective-permute-start | bytes 776 | tf_op jit(solution)/shard_map/ppermute | solution.py:25
  278.9 7.6 %collective-permute-start.29 = (f32[1,4,16]{2,1,0:T(4,128)S(1)}, f32[1,4,16]{2,1,0:T(4,128)S(1)}, u32[]{:S(2)}, u32[]{:S(2)}) collective-permute-start(f32[1,4,16]{2,1,0:T(4,128)S(1)} %get-tuple-element.49), channel_id=1, source_target_pairs={{0,1},{1,2},{2,3},{3,4},{4,5},{5,6},{6,7},{7,8},{8,9},{9,10},{10,1... | collective-permute-start | bytes 776 | tf_op jit(solution)/shard_map/ppermute | solution.py:22
  288.9 5.8 %collective-permute-start.30 = (f32[1,8,32]{2,1,0:T(8,128)S(1)}, f32[1,8,32]{2,1,0:T(8,128)S(1)}, u32[]{:S(2)}, u32[]{:S(2)}) collective-permute-start(f32[1,8,32]{2,1,0:T(8,128)S(1)} %get-tuple-element.42), channel_id=1, source_target_pairs={{1,0},{2,1},{3,2},{4,3},{5,4},{6,5},{7,6},{8,7},{9,8},{10,9},{11,1... | collective-permute-start | bytes 3080 | tf_op jit(solution)/shard_map/ppermute | solution.py:25
  290.8 7.6 %collective-permute-start.31 = (f32[1,8,32]{2,1,0:T(8,128)S(1)}, f32[1,8,32]{2,1,0:T(8,128)S(1)}, u32[]{:S(2)}, u32[]{:S(2)}) collective-permute-start(f32[1,8,32]{2,1,0:T(8,128)S(1)} %get-tuple-element.43), channel_id=1, source_target_pairs={{0,1},{1,2},{2,3},{3,4},{4,5},{5,6},{6,7},{7,8},{8,9},{9,10},{10,1... | collective-permute-start | bytes 3080 | tf_op jit(solution)/shard_map/ppermute | solution.py:22
  298.5 5.8 %collective-permute-start.32 = (f32[1,8,32]{2,1,0:T(8,128)S(1)}, f32[1,8,32]{2,1,0:T(8,128)S(1)}, u32[]{:S(2)}, u32[]{:S(2)}) collective-permute-start(f32[1,8,32]{2,1,0:T(8,128)S(1)} %get-tuple-element.40), channel_id=1, source_target_pairs={{1,0},{2,1},{3,2},{4,3},{5,4},{6,5},{7,6},{8,7},{9,8},{10,9},{11,1... | collective-permute-start | bytes 3080 | tf_op jit(solution)/shard_map/ppermute | solution.py:25
  300.4 7.6 %collective-permute-start.33 = (f32[1,8,32]{2,1,0:T(8,128)S(1)}, f32[1,8,32]{2,1,0:T(8,128)S(1)}, u32[]{:S(2)}, u32[]{:S(2)}) collective-permute-start(f32[1,8,32]{2,1,0:T(8,128)S(1)} %get-tuple-element.41), channel_id=1, source_target_pairs={{0,1},{1,2},{2,3},{3,4},{4,5},{5,6},{6,7},{7,8},{8,9},{9,10},{10,1... | collective-permute-start | bytes 3080 | tf_op jit(solution)/shard_map/ppermute | solution.py:22
  313.0 5.9 %collective-permute-start.34 = (f32[1,16,64]{2,1,0:T(8,128)S(1)}, f32[1,16,64]{2,1,0:T(8,128)S(1)}, u32[]{:S(2)}, u32[]{:S(2)}) collective-permute-start(f32[1,16,64]{2,1,0:T(8,128)S(1)} %get-tuple-element.34), channel_id=1, source_target_pairs={{1,0},{2,1},{3,2},{4,3},{5,4},{6,5},{7,6},{8,7},{9,8},{10,9},{11,1... | collective-permute-start | bytes 12296 | tf_op jit(solution)/shard_map/ppermute | solution.py:25
  314.9 7.7 %collective-permute-start.35 = (f32[1,16,64]{2,1,0:T(8,128)S(1)}, f32[1,16,64]{2,1,0:T(8,128)S(1)}, u32[]{:S(2)}, u32[]{:S(2)}) collective-permute-start(f32[1,16,64]{2,1,0:T(8,128)S(1)} %get-tuple-element.35), channel_id=1, source_target_pairs={{0,1},{1,2},{2,3},{3,4},{4,5},{5,6},{6,7},{7,8},{8,9},{9,10},{10,1... | collective-permute-start | bytes 12296 | tf_op jit(solution)/shard_map/ppermute | solution.py:22
  322.7 5.9 %collective-permute-start.36 = (f32[1,16,64]{2,1,0:T(8,128)S(1)}, f32[1,16,64]{2,1,0:T(8,128)S(1)}, u32[]{:S(2)}, u32[]{:S(2)}) collective-permute-start(f32[1,16,64]{2,1,0:T(8,128)S(1)} %get-tuple-element.32), channel_id=1, source_target_pairs={{1,0},{2,1},{3,2},{4,3},{5,4},{6,5},{7,6},{8,7},{9,8},{10,9},{11,1... | collective-permute-start | bytes 12296 | tf_op jit(solution)/shard_map/ppermute | solution.py:25
  324.7 7.7 %collective-permute-start.37 = (f32[1,16,64]{2,1,0:T(8,128)S(1)}, f32[1,16,64]{2,1,0:T(8,128)S(1)}, u32[]{:S(2)}, u32[]{:S(2)}) collective-permute-start(f32[1,16,64]{2,1,0:T(8,128)S(1)} %get-tuple-element.33), channel_id=1, source_target_pairs={{0,1},{1,2},{2,3},{3,4},{4,5},{5,6},{6,7},{7,8},{8,9},{9,10},{10,1... | collective-permute-start | bytes 12296 | tf_op jit(solution)/shard_map/ppermute | solution.py:22
  354.3 17.4 %copy-start = (f32[2,16,32,128]{2,1,3,0:T(8,128)S(1)}, f32[2,16,32,128]{2,1,3,0:T(8,128)}, u32[]{:S(2)}) copy-start(f32[2,16,32,128]{2,1,3,0:T(8,128)} %all-reduce.44.cloned.1.call-done) | copy-start | bytes 1572868
  354.4 6.3 %collective-permute-start.38 = (f32[1,32,128]{1,0,2:T(1,128)S(1)}, f32[1,32,128]{1,0,2:T(1,128)S(1)}, u32[]{:S(2)}, u32[]{:S(2)}) collective-permute-start(f32[1,32,128]{1,0,2:T(1,128)S(1)} %get-tuple-element.14), channel_id=1, source_target_pairs={{1,0},{2,1},{3,2},{4,3},{5,4},{6,5},{7,6},{8,7},{9,8},{10,9},{11,1... | collective-permute-start | bytes 49160 | tf_op jit(solution)/shard_map/ppermute | solution.py:25
  356.4 8.3 %collective-permute-start.39 = (f32[1,32,128]{1,0,2:T(1,128)S(1)}, f32[1,32,128]{1,0,2:T(1,128)S(1)}, u32[]{:S(2)}, u32[]{:S(2)}) collective-permute-start(f32[1,32,128]{1,0,2:T(1,128)S(1)} %get-tuple-element.15), channel_id=1, source_target_pairs={{0,1},{1,2},{2,3},{3,4},{4,5},{5,6},{6,7},{7,8},{8,9},{9,10},{10,1... | collective-permute-start | bytes 49160 | tf_op jit(solution)/shard_map/ppermute | solution.py:22
  365.8 9.3 %collective-permute-start.40 = (f32[1,32,128]{1,0,2:T(1,128)S(1)}, f32[1,32,128]{1,0,2:T(1,128)S(1)}, u32[]{:S(2)}, u32[]{:S(2)}) collective-permute-start(f32[1,32,128]{1,0,2:T(1,128)S(1)} %get-tuple-element.12), channel_id=1, source_target_pairs={{1,0},{2,1},{3,2},{4,3},{5,4},{6,5},{7,6},{8,7},{9,8},{10,9},{11,1... | collective-permute-start | bytes 49160 | tf_op jit(solution)/shard_map/ppermute | solution.py:25
  367.7 8.3 %collective-permute-start.41 = (f32[1,32,128]{1,0,2:T(1,128)S(1)}, f32[1,32,128]{1,0,2:T(1,128)S(1)}, u32[]{:S(2)}, u32[]{:S(2)}) collective-permute-start(f32[1,32,128]{1,0,2:T(1,128)S(1)} %get-tuple-element.13), channel_id=1, source_target_pairs={{0,1},{1,2},{2,3},{3,4},{4,5},{5,6},{6,7},{7,8},{8,9},{9,10},{10,1... | collective-permute-start | bytes 49160 | tf_op jit(solution)/shard_map/ppermute | solution.py:22
Sparse Core Ops, SparseCore 0:
  29.5 79.6 all-reduce.43
where the time goes:
time: 389 us; the launch traced here: 387 us
  starting transfers between devices  145 us (37%)
  waiting for transfers between devices  136 us (35%)
  local copies, waits for them, and re-layouts  61.4 us (16%)
  other arithmetic  29.3 us (8%)
  between operations  14.9 us (4%)
    ppermute x21, starting transfers between devices, extended(): lax.ppermute(lax.slice_in_dim(block, 0, width, axis=dim), axis, backward)  74.1 us
    ppermute x21, starting transfers between devices, extended(): lax.ppermute(lax.slice_in_dim(block, block.shape[dim] - width, None, axis...  70.4 us
    psum x1, waiting for transfers between devices, on_device(): fine = lax.psum(refine_rest(coarse, padded), 'band')  68.2 us
    ppermute x21, waiting for transfers between devices, extended(): lax.ppermute(lax.slice_in_dim(block, block.shape[dim] - width, None, axis...  61.3 us
    reshape x3, local copies, waits for them, and re-layouts, restrict(): field.reshape(a // 2, 2, b // 2, 2, c // 2, 2).sum(axis=(1, 3, 5))  22.4 us
    reshape x4, local copies, waits for them, and re-layouts, prolong(): return spread.reshape(2 * a, 2 * b, 2 * c)  18 us
    reduce_sum x5, other arithmetic, restrict(): field.reshape(a // 2, 2, b // 2, 2, c // 2, 2).sum(axis=(1, 3, 5))  10.4 us
    broadcast_in_dim x5, local copies, waits for them, and re-layouts, prolong(): jnp.broadcast_to(field[:, None, :, None, :, None], (a, 2, b, 2, c, 2))  8.38 us
  transfers between devices with their start and end apart: 43, of which 24 were waited for; matrix products, arithmetic and copies ran while one was open for 2% of the time, Pallas kernels for 0%

commit v1 on v0

v1 whole, which is shorter than its diff:
```python
import functools

import jax
import jax.numpy as jnp
from jax import lax
from jax.experimental import pallas as pl
from jax.experimental.pallas import tpu as pltpu
from jax.sharding import PartitionSpec as P

DEN = 16
BANDS = 8
DOMS = 64
REACH = 7
ALPHA = 1.0 / 9.0
SOURCE_SCALE = 0.6
F32 = jnp.float32


def lanes_of(shape):
    return lax.broadcasted_iota(jnp.int32, shape, len(shape) - 1)


def rows_of(shape):
    return lax.broadcasted_iota(jnp.int32, shape, len(shape) - 2)


def sides_z(v, step):
    lane = lanes_of(v.shape)
    ax = v.ndim - 1
    left = jnp.where(lane >= step, pltpu.roll(v, step, ax), 0.0)
    right = jnp.where(lane < 128 - step, pltpu.roll(v, 128 - step, ax), 0.0)
    return left + right


def from_below(v, step=1):
    return jnp.where(rows_of(v.shape) >= step, pltpu.roll(v, step, v.ndim - 2), 0.0)


def from_above(v, step=1):
    return jnp.where(rows_of(v.shape) < 8 - step, pltpu.roll(v, 8 - step, v.ndim - 2), 0.0)


def sides_y(v, step):
    if v.ndim == 2:
        return from_below(v, step) + from_above(v, step)
    parts = [v[q] for q in range(v.shape[0])]
    n = len(parts)
    out = []
    for q in range(n):
        lower = parts[q - 1] if q > 0 else from_below(parts[n - 1])
        upper = parts[q + 1] if q < n - 1 else from_above(parts[0])
        out.append(lower + upper)
    return jnp.stack(out, axis=0)


def smooth(low, v, high, zstep, ystep=1):
    around = sides_y(v, ystep) + sides_z(v, zstep)
    if low is not None:
        around = around + low
    if high is not None:
        around = around + high
    return v * (1.0 / 3.0) + around * ALPHA


def pair_z(v, step):
    lane = lanes_of(v.shape)
    ax = v.ndim - 1
    other = jnp.where((lane & step) == 0, pltpu.roll(v, 128 - step, ax), pltpu.roll(v, step, ax))
    return v + other


def pair_y(v, step):
    row = rows_of(v.shape)
    ax = v.ndim - 2
    other = jnp.where((row & step) == 0, pltpu.roll(v, 8 - step, ax), pltpu.roll(v, step, ax))
    return v + other


def run_T(src, planes, zstep, ystep=1, mask=None):
    out = {}
    for k in planes:
        v = src.get(k)
        low, high = src.get(k - 1), src.get(k + 1)
        if v is None:
            edge = low if low is not None else high
            got = edge * ALPHA
        else:
            got = smooth(low, v, high, zstep, ystep)
        out[k] = got if mask is None else mask(k, got)
    return out


class Held:
    def __init__(self, ref, first):
        self.ref, self.first, self.have = ref, first, set()

    def put(self, k, value):
        self.ref[k - self.first] = value
        self.have.add(k)

    def get(self, k):
        return self.ref[k - self.first] if k in self.have else None

    def __getitem__(self, k):
        return self.ref[k - self.first]


def hold_T(src, held, planes, zstep, mask):
    for k in planes:
        v = src.get(k)
        low, high = src.get(k - 1), src.get(k + 1)
        if v is None:
            got = (low if low is not None else high) * ALPHA
        else:
            got = smooth(low, v, high, zstep)
        held.put(k, mask(k, got))


def density_kernel(spin_ref, occ_ref, orb_ref, out_ref):
    weights = []
    for k in range(8):
        weight = occ_ref[k].astype(F32) * (0.125 / DEN)
        up = spin_ref[k] == 0
        weights.append((jnp.where(up, weight, 0.0), jnp.where(up, 0.0, weight)))
    for x in range(8):
        up, down = 0.0, 0.0
        for k in range(8):
            square = orb_ref[k, x] * orb_ref[k, x]
            up = up + weights[k][0] * square
            down = down + weights[k][1] * square
        both = jnp.concatenate([up, down], axis=-1)
        for copy in range(BANDS):
            out_ref[copy, pl.ds(16 * x, 16), :] = both


def density(spin_group, occupation, orbitals):
    smem = pl.BlockSpec(memory_space=pltpu.SMEM)
    vmem = pl.BlockSpec(memory_space=pltpu.VMEM)
    return pl.pallas_call(
        density_kernel,
        out_shape=jax.ShapeDtypeStruct((BANDS, 128, 128), F32),
        in_specs=[smem, smem, vmem],
        out_specs=vmem,
        compiler_params=pltpu.CompilerParams(vmem_limit_bytes=32 * 2**20),
        name="density",
    )(spin_group, occupation, orbitals)


def refine_matrix():
    row = lax.broadcasted_iota(jnp.int32, (128, 256), 0)
    col = lax.broadcasted_iota(jnp.int32, (128, 256), 1)
    cell, spin = row & 63, row >> 6
    fine, half = col & 127, col >> 7
    own = fine >> 1
    other = jnp.where((fine & 1) == 0, own - 1, own + 1)
    value = jnp.where(cell == own, 0.75, jnp.where(cell == other, 0.25, 0.0))
    return jnp.where((spin == 1) & (half == 1), -value, value)


def refine_y(pair):
    first, second = pair
    return jnp.stack(
        [
            0.75 * first + 0.25 * from_below(second),
            0.75 * first + 0.25 * second,
            0.75 * second + 0.25 * first,
            0.75 * second + 0.25 * from_above(first),
        ],
        axis=0,
    )


def refine_x(coarse, k):
    i = k // 2
    other = i - 1 if k % 2 == 0 else i + 1
    total = None
    for j, factor in ((i, 0.75), (other, 0.25)):
        if 0 <= j < 8:
            term = factor * coarse[j]
            total = term if total is None else total + term
    return total


def local_kernel(
    flag_ref, part_ref, guess_ref,
    far_ref, low_ref, high_ref, own0_ref, own1_ref, mag_ref,
    sum_ref, wide_ref, d_ref, t_ref, r_ref, t1_ref,
):
    low_flag, high_flag = flag_ref[0], flag_ref[1]

    def masked(last):
        def mask(k, v):
            if k < 0:
                return v * low_flag
            if k > last:
                return v * high_flag
            return v
        return mask

    inside0, inside1 = masked(15), masked(7)

    for x in range(8):
        rows = pl.ds(16 * x, 16)
        total = part_ref[0, rows, :]
        for band in range(1, BANDS):
            total = total + part_ref[band, rows, :]
        sum_ref[rows, :] = total
    wide = jnp.dot(
        sum_ref[...], refine_matrix(),
        precision=lax.Precision.HIGHEST, preferred_element_type=F32,
    )
    wide_ref[0], wide_ref[1] = wide[:, :128], wide[:, 128:]
    plus, minus = [], []
    for x in range(8):
        pairs = [[wide_ref[half, pl.ds(16 * x + p, 8, stride=2), :] for p in range(2)] for half in range(2)]
        plus.append(SOURCE_SCALE * refine_y(pairs[0]))
        minus.append(refine_y(pairs[1]))

    def guess(k):
        if not 0 <= k < 16:
            return None
        return jnp.stack([guess_ref[k, pl.ds(q, 8, stride=4), :] for q in range(4)], axis=0)

    d = Held(d_ref, -1)
    for k in range(-1, 17):
        v, low, high = guess(k), guess(k - 1), guess(k + 1)
        around = None
        if v is not None:
            around = sides_y(v, 1) + sides_z(v, 1)
        for side in (low, high):
            if side is not None:
                around = side if around is None else around + side
        applied = 6.0 * v - around if v is not None else -around
        d.put(k, inside0(k, refine_x(plus, k) - applied))
        mag = refine_x(minus, k)
        if 0 <= k < 16:
            for q in range(4):
                mag_ref[k, pl.ds(q, 8, stride=4), :] = mag[q]
        else:
            (low_ref if k < 0 else high_ref)[pl.ds(22, 4)] = mag

    t, r = Held(t_ref, -2), Held(r_ref, -3)
    hold_T(d, t, range(-2, 18), 1, inside0)
    hold_T(t, r, range(-3, 19), 1, inside0)

    def geometric(b, t, r, k, zstep):
        low, v, high = r.get(k - 1), r.get(k), r.get(k + 1)
        if v is None:
            last = (low if low is not None else high) * ALPHA
        else:
            last = smooth(low, v, high, zstep)
        for term in (r.get(k), t.get(k), b.get(k)):
            if term is not None:
                last = last + term
        return last * ALPHA

    for k in range(16):
        own0_ref[k] = geometric(d, t, r, k, 1)
    for k in range(4):
        low_ref[pl.ds(4 * k, 4)] = geometric(d, t, r, k - 4, 1)
        high_ref[pl.ds(4 * k, 4)] = geometric(d, t, r, k + 16, 1)

    b1 = {}
    for k in range(-2, 10):
        total = None
        for fine in (2 * k, 2 * k + 1):
            v = r.get(fine)
            if v is not None:
                total = v if total is None else total + v
        total = jnp.stack([total[0] + total[1], total[2] + total[3]], axis=0)
        b1[k] = 0.5 * pair_z(total, 1)
    t1 = run_T(b1, range(-3, 11), 2, mask=inside1)
    r1 = Held(t1_ref, -4)
    hold_T(t1, r1, range(-4, 12), 2, inside1)
    f1 = {k: geometric(b1, t1, r1, k, 2) for k in range(-5, 13)}
    for k in range(-1, 9):
        own1_ref[k + 1] = f1[k]
    even = (lanes_of((8, 128)) & 1) == 0
    for pair in range(3):
        for q in range(2):
            low_ref[16 + 2 * pair + q] = jnp.where(even, f1[2 * pair - 5][q], f1[2 * pair - 4][q])
            high_ref[16 + 2 * pair + q] = jnp.where(even, f1[2 * pair + 7][q], f1[2 * pair + 8][q])

    lane = lanes_of((8, 128)) & 3
    for group in range(2):
        packed = None
        for p in range(4):
            k = 4 * group + p - 2
            v = r1[2 * k] + r1[2 * k + 1]
            v = 0.5 * pair_z(v[0] + v[1], 2)
            packed = v if packed is None else jnp.where(lane == p, v, packed)
        far_ref[pl.ds(8 * group, 8), :] = packed


def local_part(flags, parts, guess):
    smem = pl.BlockSpec(memory_space=pltpu.SMEM)
    vmem = pl.BlockSpec(memory_space=pltpu.VMEM)
    shape = lambda *s: jax.ShapeDtypeStruct(s, F32)
    return pl.pallas_call(
        local_kernel,
        out_shape=(
            shape(16, 128), shape(26, 8, 128), shape(26, 8, 128),
            shape(16, 4, 8, 128), shape(10, 2, 8, 128), shape(16, 32, 128),
        ),
        in_specs=[smem, vmem, vmem],
        out_specs=(vmem,) * 6,
        scratch_shapes=[
            pltpu.VMEM((128, 128), F32), pltpu.VMEM((2, 128, 128), F32),
            pltpu.VMEM((18, 4, 8, 128), F32), pltpu.VMEM((20, 4, 8, 128), F32),
            pltpu.VMEM((22, 4, 8, 128), F32), pltpu.VMEM((16, 2, 8, 128), F32),
        ],
        compiler_params=pltpu.CompilerParams(vmem_limit_bytes=32 * 2**20),
        name="local",
    )(flags, parts, guess)


def final_kernel(
    place_ref, far_ref, mine_ref, low_ref, high_ref, own0_ref, own1_ref, mag_ref, guess_ref,
    pot_out, mag_out,
    b2_ref, t2_ref, r2_ref, p1_ref,
):
    dom = place_ref[0]

    def masked(count):
        first, last = -dom * count, (DOMS - dom) * count
        def mask(k, v):
            if 0 <= k < count:
                return v
            ok = (k >= first) & (k < last)
            return jnp.where(ok, v, 0.0)
        return mask

    lane = lanes_of((8, 128)) & 3
    def message(i):
        shift = i - REACH
        if shift == 0:
            return mine_ref, 0, None
        return far_ref, (0 if shift < 0 else 16), abs(shift)

    def vector(i, half):
        ref, row, member = message(i)
        rows = pl.ds(row + 8 * half, 8)
        return ref[rows, :] if member is None else ref[member, rows, :]

    b2, t2, r2 = Held(b2_ref, -30), Held(t2_ref, -25), Held(r2_ref, -24)
    for i in range(16):
        packed = None
        for part in ((i, 0), (i - 1, 1)):
            if 0 <= part[0] < 15:
                v = vector(*part)
                packed = v if packed is None else packed + v
        for p in range(4):
            only = jnp.where(lane == p, packed, 0.0)
            only = only + pltpu.roll(only, 1 if p % 2 == 0 else 127, 1)
            only = only + pltpu.roll(only, 2 if p < 2 else 126, 1)
            b2.put(4 * (i - REACH) - 2 + p, only)
    inside2, inside3, inside4 = masked(4), masked(2), masked(1)
    hold_T(b2, t2, range(-25, 29), 4, inside2)
    hold_T(t2, r2, range(-24, 28), 4, lambda k, v: v)

    b3 = {}
    for k in range(-12, 14):
        v = pair_y(pair_z(r2[2 * k] + r2[2 * k + 1], 4), 1)
        b3[k] = inside3(k, 0.5 * v)
    t3 = run_T(b3, range(-11, 13), 8, 2, inside3)
    r3 = run_T(t3, range(-10, 12), 8, 2)

    b4 = {}
    for k in range(-5, 6):
        v = pair_y(pair_z(r3[2 * k] + r3[2 * k + 1], 8), 2)
        b4[k] = inside4(k, 0.5 * v)
    t4 = run_T(b4, range(-4, 5), 16, 4, inside4)
    r4 = run_T(t4, range(-3, 4), 16, 4, inside4)
    u4 = run_T(r4, range(-2, 3), 16, 4)
    e4 = {k: ALPHA * (b4[k] + t4[k] + r4[k] + u4[k]) for k in range(-2, 3)}
    e4 = {k: inside4(k, v) for k, v in e4.items()}

    v3 = {k: ALPHA * t3[k] + e4[k // 2] for k in range(-4, 6)}
    v3 = run_T(v3, range(-3, 5), 8, 2, inside3)
    w3 = run_T(v3, range(-2, 4), 8, 2)
    e3 = {k: inside3(k, w3[k] + ALPHA * (b3[k] + t3[k] + r3[k])) for k in range(-2, 4)}

    v2 = {k: ALPHA * t2[k] + e3[k // 2] for k in range(-4, 8)}
    v2 = run_T(v2, range(-3, 7), 4, 1, inside2)
    w2 = run_T(v2, range(-2, 6), 4, 1)
    e2 = {k: inside2(k, w2[k] + ALPHA * (b2[k] + t2[k] + r2[k])) for k in range(-2, 6)}

    inside1, inside0 = masked(8), masked(16)
    spread = {k: jnp.stack([e2[k // 2]] * 2, axis=0) for k in range(-4, 12)}
    v1 = run_T(spread, range(-2, 10), 2, 1, inside1)
    w1 = run_T(v1, range(-1, 9), 2, 1)
    even = (lanes_of((8, 128)) & 1) == 0
    extra = {}
    for ref, first in ((low_ref, -1), (high_ref, 3)):
        for pair in range(3):
            both = [ref[16 + 2 * pair + q] for q in range(2)]
            one = jnp.stack([jnp.where(even, v, pltpu.roll(v, 1, 1)) for v in both], axis=0)
            two = jnp.stack([jnp.where(even, pltpu.roll(v, 127, 1), v) for v in both], axis=0)
            for k, v in ((first + 2 * pair, one), (first + 2 * pair + 1, two)):
                extra[k] = extra[k] + v if k in extra else v
    e1 = {}
    for k in range(-1, 9):
        e1[k] = inside1(k, w1[k] + own1_ref[k + 1] + extra[k])

    def prolonged(k):
        v = e1[k // 2]
        return jnp.stack([v[0], v[0], v[1], v[1]], axis=0)

    p1 = Held(p1_ref, -1)
    wide = {k: prolonged(k) for k in range(-2, 18)}
    hold_T(wide, p1, range(-1, 17), 1, inside0)
    for k in range(16):
        v = smooth(p1[k - 1], p1[k], p1[k + 1], 1) + own0_ref[k]
        if k < 4:
            v = v + low_ref[pl.ds(4 * k, 4)]
        if k >= 12:
            v = v + high_ref[pl.ds(4 * (k - 12), 4)]
        for q in range(4):
            rows = pl.ds(q, 8, stride=4)
            pot_out[k, rows, :] = guess_ref[k, rows, :] + v[q]
    mag_out[...] = mag_ref[...]
    for q in range(4):
        rows = pl.ds(q, 8, stride=4)
        mag_out[0, rows, :] = mag_ref[0, rows, :] + low_ref[22 + q]
        mag_out[15, rows, :] = mag_ref[15, rows, :] + high_ref[22 + q]


def final_part(place, far, mine, low, high, own0, own1, mag, guess):
    smem = pl.BlockSpec(memory_space=pltpu.SMEM)
    vmem = pl.BlockSpec(memory_space=pltpu.VMEM)
    shape = lambda *s: jax.ShapeDtypeStruct(s, F32)
    return pl.pallas_call(
        final_kernel,
        out_shape=(shape(16, 32, 128), shape(16, 32, 128)),
        in_specs=[smem] + [vmem] * 8,
        out_specs=(vmem, vmem),
        scratch_shapes=[
            pltpu.VMEM((64, 8, 128), F32), pltpu.VMEM((54, 8, 128), F32),
            pltpu.VMEM((52, 8, 128), F32), pltpu.VMEM((18, 4, 8, 128), F32),
        ],
        compiler_params=pltpu.CompilerParams(vmem_limit_bytes=32 * 2**20),
        name="final",
    )(place, far, mine, low, high, own0, own1, mag, guess)


def on_device(orbitals, spin_group, occupation, potential_guess):
    dom = lax.axis_index("dom")
    flags = jnp.stack([dom > 0, dom < DOMS - 1]).astype(F32)
    place = dom.astype(jnp.int32)[None]
    parts = lax.all_to_all(density(spin_group, occupation, orbitals), "band", 0, 0)
    far, to_low, to_high, own0, own1, mag = local_part(flags, parts, potential_guess)

    ups = [(k * DOMS + d, k * DOMS + d + k) for k in range(1, BANDS) for d in range(DOMS - k)]
    downs = [(target, source) for source, target in ups]
    from_low = lax.ppermute(far, ("band", "dom"), ups)
    from_high = lax.ppermute(far, ("band", "dom"), downs)
    near_low = lax.ppermute(to_high, "dom", [(d, d + 1) for d in range(DOMS - 1)])
    near_high = lax.ppermute(to_low, "dom", [(d + 1, d) for d in range(DOMS - 1)])
    both = jnp.concatenate([from_low, from_high], axis=0)
    everyone = lax.all_to_all(jnp.broadcast_to(both[None], (BANDS, 32, 128)), "band", 0, 0)
    return final_part(
        place, everyone, far, near_low, near_high, own0, own1, mag, potential_guess
    )


def solution(mesh):
    placed = (P("band", "dom", None, None), P("band"), P("band"), P("dom", None, None))
    return jax.shard_map(
        on_device,
        mesh=mesh,
        in_specs=placed,
        out_specs=(P("dom", None, None), P("dom", None, None)),
        check_vma=False,
    )
```

time: 389 us -> 66.3 us (0.17)
  the two profiles are of different devices: /device:TPU:24 before, /device:TPU:26 now
where the time goes in v1:
time: 66.3 us; the launch traced here: 65.9 us
  starting transfers between devices  38.5 us (58%)
  waiting for transfers between devices  17.7 us (27%)
  Pallas kernels  5.82 us (9%)
  local copies, waits for them, and re-layouts  3.02 us (5%)
  between operations  0.69 us (1%)
    ppermute x1, starting transfers between devices, on_device(): from_high = lax.ppermute(far, ('band', 'dom'), downs)  12 us
    all_to_all x1, starting transfers between devices, on_device(): lax.all_to_all(jnp.broadcast_to(both[None], (BANDS, 32, 128)), 'band', 0, 0)  11.7 us
    all_to_all x1, waiting for transfers between devices, on_device(): lax.all_to_all(density(spin_group, occupation, orbitals), 'band', 0, 0)  8.82 us
    ppermute x1, waiting for transfers between devices, on_device(): from_low = lax.ppermute(far, ('band', 'dom'), ups)  6.61 us
    all_to_all x1, starting transfers between devices, on_device(): lax.all_to_all(density(spin_group, occupation, orbitals), 'band', 0, 0)  4.96 us
    ppermute x1, starting transfers between devices, on_device(): lax.ppermute(to_low, 'dom', [(d + 1, d) for d in range(DOMS - 1)])  4.96 us
    ppermute x1, starting transfers between devices, on_device(): lax.ppermute(to_high, 'dom', [(d, d + 1) for d in range(DOMS - 1)])  2.98 us
    pallas_call x1, Pallas kernels, final_part(): pl.pallas_call(final_kernel, out_shape=(shape(16, 32, 128), shape(16, 32,...  2.56 us
  transfers between devices with their start and end apart: 6, of which 4 were waited for; matrix products, arithmetic and copies ran while one was open for 0% of the time, Pallas kernels for 0%

profile of v1, /device:TPU:26, one launch (start us, length us, event | category | flops | bytes accessed | tf_op | source)
XLA Modules:
  0.0 65.9 jit_solution(8632427042729590153)
XLA Ops:
  0.6 0.0 copy-start.1
  0.6 1.0 %copy-done.1 = f32[8,8,16,64]{3,2,1,0:T(8,128)S(1)} copy-done((f32[8,8,16,64]{3,2,1,0:T(8,128)S(1)}, f32[8,8,16,64]{3,2,1,0:T(8,128)}, u32[]{:S(2)}) %copy-start.1) | copy-done | bytes 262168
  1.7 0.0 copy-start.2
  1.7 0.7 copy-done.2
  2.3 0.0 copy-start.3
  2.3 0.7 copy-done.3
  3.0 1.5 %density.1 = f32[8,128,128]{2,1,0:T(8,128)} custom-call(s32[8]{0:T(128)S(1)} %copy-done.2, s32[8]{0:T(128)S(1)} %copy-done.3, f32[8,8,16,64]{3,2,1,0:T(8,128)S(1)} %copy-done.1), custom_call_target="tpu_custom_call" | custom-call | tf_op jit(solution)/shard_map/density/pallas_call | solution.py:139
  4.5 0.0 copy-start
  4.5 5.0 %all-to-all-start = ((f32[8,128,128]{2,1,0:T(8,128)}), f32[8,128,128]{2,1,0:T(8,128)S(1)}, u32[]{:S(2)}, u32[]{:S(2)}) async-start(f32[8,128,128]{2,1,0:T(8,128)} %density.1), calls=%async_computation | async-start | bytes 1048576 | tf_op jit(solution)/shard_map/all_to_all | solution.py:450
  9.4 0.1 add_convert_fusion.flag_ref
  9.5 8.8 %all-to-all-done.part_ref = f32[8,128,128]{2,1,0:T(8,128)S(1)} async-done(((f32[8,128,128]{2,1,0:T(8,128)}), f32[8,128,128]{2,1,0:T(8,128)S(1)}, u32[]{:S(2)}, u32[]{:S(2)}) %all-to-all-start) | async-done | bytes 524320 | tf_op jit(solution)/shard_map/all_to_all | solution.py:450
  18.3 0.0 copy-done
  18.3 1.8 %local.1 = (f32[16,128]{1,0:T(8,128)S(1)}, f32[26,8,128]{2,1,0:T(8,128)S(1)}, f32[26,8,128]{2,1,0:T(8,128)S(1)}, f32[16,4,8,128]{3,2,1,0:T(8,128)S(1)}, f32[10,2...) custom-call(f32[2]{0:T(128)S(1)} %add_convert_fusion.flag_ref, f32[8,128,128]{2,1,0:T(8,128)S(1)} %all-to-all-done.part_ref, ...), custom_call_target="tpu_custom_call" | custom-call | tf_op jit(solution)/shard_map/local/pallas_call | solution.py:299
  20.1 12.0 %collective-permute-start.1 = (f32[16,128]{1,0:T(8,128)S(1)}, f32[16,128]{1,0:T(8,128)S(1)}, u32[]{:S(2)}, u32[]{:S(2)}) collective-permute-start(f32[16,128]{1,0:T(8,128)S(1)} %get-tuple-element.8.mine_ref), channel_id=1, source_target_pairs={{65,64},{66,65},{67,66},{68,67},{69,68},{70,69},{71,70},{72,71},{7... | collective-permute-start | bytes 24584 | tf_op jit(solution)/shard_map/ppermute | solution.py:456
  32.1 1.9 %collective-permute-start = (f32[16,128]{1,0:T(8,128)S(1)}, f32[16,128]{1,0:T(8,128)S(1)}, u32[]{:S(2)}, u32[]{:S(2)}) collective-permute-start(f32[16,128]{1,0:T(8,128)S(1)} %get-tuple-element.8.mine_ref), channel_id=1, source_target_pairs={{64,65},{65,66},{66,67},{67,68},{68,69},{69,70},{70,71},{71,72},{7... | collective-permute-start | bytes 24584 | tf_op jit(solution)/shard_map/ppermute | solution.py:455
  34.1 0.0 collective-permute-done.1
  34.1 6.6 %collective-permute-done = f32[16,128]{1,0:T(8,128)S(1)} collective-permute-done((f32[16,128]{1,0:T(8,128)S(1)}, f32[16,128]{1,0:T(8,128)S(1)}, u32[]{:S(2)}, u32[]{:S(2)}) %collective-permute-start) | collective-permute-done | bytes 8224 | tf_op jit(solution)/shard_map/ppermute | solution.py:455
  40.7 0.7 %broadcast_in_dim.10 = f32[8,32,128]{2,1,0:T(8,128)} broadcast(f32[32,128]{1,0:T(8,128)S(1)} %pad_maximum_fusion), dimensions={1,2} | broadcast | bytes 147456 | tf_op jit(solution)/shard_map/broadcast_in_dim | solution.py:460
  41.4 11.7 %all-to-all-start.1 = ((f32[8,32,128]{2,1,0:T(8,128)}), f32[8,32,128]{2,1,0:T(8,128)S(1)}, u32[]{:S(2)}, u32[]{:S(2)}) async-start(f32[8,32,128]{2,1,0:T(8,128)} %broadcast_in_dim.10), calls=%async_computation.1 | async-start | bytes 262144 | tf_op jit(solution)/shard_map/all_to_all | solution.py:460
  53.1 3.0 %collective-permute-start.2 = (f32[26,8,128]{2,1,0:T(8,128)S(1)}, f32[26,8,128]{2,1,0:T(8,128)S(1)}, u32[]{:S(2)}, u32[]{:S(2)}) collective-permute-start(f32[26,8,128]{2,1,0:T(8,128)S(1)} %get-tuple-element.9), channel_id=1, source_target_pairs={{0,1},{1,2},{2,3},{3,4},{4,5},{5,6},{6,7},{7,8},{8,9},{9,10},{10,1... | collective-permute-start | bytes 319496 | tf_op jit(solution)/shard_map/ppermute | solution.py:457
  56.1 5.0 %collective-permute-start.3 = (f32[26,8,128]{2,1,0:T(8,128)S(1)}, f32[26,8,128]{2,1,0:T(8,128)S(1)}, u32[]{:S(2)}, u32[]{:S(2)}) collective-permute-start(f32[26,8,128]{2,1,0:T(8,128)S(1)} %get-tuple-element.10), channel_id=1, source_target_pairs={{1,0},{2,1},{3,2},{4,3},{5,4},{6,5},{7,6},{8,7},{9,8},{10,9},{11,1... | collective-permute-start | bytes 319496 | tf_op jit(solution)/shard_map/ppermute | solution.py:458
  61.0 1.1 %collective-permute-done.2.low_ref = f32[26,8,128]{2,1,0:T(8,128)S(1)} collective-permute-done((f32[26,8,128]{2,1,0:T(8,128)S(1)}, f32[26,8,128]{2,1,0:T(8,128)S(1)}, u32[]{:S(2)}, u32[]{:S(2)}) %collective-permute-start.2) | collective-permute-done | bytes 106528 | tf_op jit(solution)/shard_map/ppermute | solution.py:457
  62.1 1.2 %collective-permute-done.3.high_ref = f32[26,8,128]{2,1,0:T(8,128)S(1)} collective-permute-done((f32[26,8,128]{2,1,0:T(8,128)S(1)}, f32[26,8,128]{2,1,0:T(8,128)S(1)}, u32[]{:S(2)}, u32[]{:S(2)}) %collective-permute-start.3) | collective-permute-done | bytes 106528 | tf_op jit(solution)/shard_map/ppermute | solution.py:458
  63.3 0.0 all-to-all-done.1.far_ref
  63.3 2.6 %final.1 = (f32[16,32,128]{2,1,0:T(8,128)}, f32[16,32,128]{2,1,0:T(8,128)}) custom-call(s32[1]{0:T(128)} %bitcast.place_ref, f32[8,32,128]{2,1,0:T(8,128)S(1)} %all-to-all-done.1.far_ref, f32[16,128]{1,0:T(8,128)S(1)} %get-tuple-element.8.mine_ref, f32[26,8,128]{2,1,0:T(8,128)S(1)} %collective-permute-done.2.low_ref, ...), custom_call_target="tpu_custom_call" | custom-call | tf_op jit(solution)/shard_map/final/pallas_call | solution.py:432
  (1 shorter events, 0.0 us)
Async XLA Ops:
  0.6 1.0 %copy-start.1 = (f32[8,8,16,64]{3,2,1,0:T(8,128)S(1)}, f32[8,8,16,64]{3,2,1,0:T(8,128)}, u32[]{:S(2)}) copy-start(f32[8,8,16,64]{3,2,1,0:T(8,128)} %orb_ref.1) | copy-start | bytes 786436
  1.7 0.7 copy-start.2
  2.3 0.7 copy-start.3
  4.5 13.9 %copy-start = (f32[16,32,128]{2,1,0:T(8,128)S(1)}, f32[16,32,128]{2,1,0:T(8,128)}, u32[]{:S(2)}) copy-start(f32[16,32,128]{2,1,0:T(8,128)} %guess_ref.3) | copy-start | bytes 786436
  4.5 13.9 %all-to-all-start = ((f32[8,128,128]{2,1,0:T(8,128)}), f32[8,128,128]{2,1,0:T(8,128)S(1)}, u32[]{:S(2)}, u32[]{:S(2)}) async-start(f32[8,128,128]{2,1,0:T(8,128)} %density.1), calls=%async_computation | async-start | bytes 1048576 | tf_op jit(solution)/shard_map/all_to_all | solution.py:450
  20.1 14.0 %collective-permute-start.1 = (f32[16,128]{1,0:T(8,128)S(1)}, f32[16,128]{1,0:T(8,128)S(1)}, u32[]{:S(2)}, u32[]{:S(2)}) collective-permute-start(f32[16,128]{1,0:T(8,128)S(1)} %get-tuple-element.8.mine_ref), channel_id=1, source_target_pairs={{65,64},{66,65},{67,66},{68,67},{69,68},{70,69},{71,70},{72,71},{7... | collective-permute-start | bytes 24584 | tf_op jit(solution)/shard_map/ppermute | solution.py:456
  32.1 8.6 %collective-permute-start = (f32[16,128]{1,0:T(8,128)S(1)}, f32[16,128]{1,0:T(8,128)S(1)}, u32[]{:S(2)}, u32[]{:S(2)}) collective-permute-start(f32[16,128]{1,0:T(8,128)S(1)} %get-tuple-element.8.mine_ref), channel_id=1, source_target_pairs={{64,65},{65,66},{66,67},{67,68},{68,69},{69,70},{70,71},{71,72},{7... | collective-permute-start | bytes 24584 | tf_op jit(solution)/shard_map/ppermute | solution.py:455
  41.4 21.9 %all-to-all-start.1 = ((f32[8,32,128]{2,1,0:T(8,128)}), f32[8,32,128]{2,1,0:T(8,128)S(1)}, u32[]{:S(2)}, u32[]{:S(2)}) async-start(f32[8,32,128]{2,1,0:T(8,128)} %broadcast_in_dim.10), calls=%async_computation.1 | async-start | bytes 262144 | tf_op jit(solution)/shard_map/all_to_all | solution.py:460
  53.1 9.0 %collective-permute-start.2 = (f32[26,8,128]{2,1,0:T(8,128)S(1)}, f32[26,8,128]{2,1,0:T(8,128)S(1)}, u32[]{:S(2)}, u32[]{:S(2)}) collective-permute-start(f32[26,8,128]{2,1,0:T(8,128)S(1)} %get-tuple-element.9), channel_id=1, source_target_pairs={{0,1},{1,2},{2,3},{3,4},{4,5},{5,6},{6,7},{7,8},{8,9},{9,10},{10,1... | collective-permute-start | bytes 319496 | tf_op jit(solution)/shard_map/ppermute | solution.py:457
  56.1 7.2 %collective-permute-start.3 = (f32[26,8,128]{2,1,0:T(8,128)S(1)}, f32[26,8,128]{2,1,0:T(8,128)S(1)}, u32[]{:S(2)}, u32[]{:S(2)}) collective-permute-start(f32[26,8,128]{2,1,0:T(8,128)S(1)} %get-tuple-element.10), channel_id=1, source_target_pairs={{1,0},{2,1},{3,2},{4,3},{5,4},{6,5},{7,6},{8,7},{9,8},{10,9},{11,1... | collective-permute-start | bytes 319496 | tf_op jit(solution)/shard_map/ppermute | solution.py:458

commit v2 on v1

--- a/solution.py
+++ b/solution.py
@@ -11,6 +11,7 @@
 BANDS = 8
 DOMS = 64
 REACH = 7
+RING = 16
 ALPHA = 1.0 / 9.0
 SOURCE_SCALE = 0.6
 F32 = jnp.float32
@@ -116,31 +117,44 @@
         held.put(k, mask(k, got))
 
 
-def density_kernel(spin_ref, occ_ref, orb_ref, out_ref):
-    weights = []
+def density_kernel(spin_hbm, occ_hbm, orb_hbm, out_ref, spin_ref, occ_ref, orb_ref, sems):
+    copies = [
+        pltpu.make_async_copy(spin_hbm, spin_ref, sems.at[8]),
+        pltpu.make_async_copy(occ_hbm, occ_ref, sems.at[9]),
+    ]
+    copies += [pltpu.make_async_copy(orb_hbm.at[k], orb_ref.at[k], sems.at[k]) for k in range(8)]
+    for copy in copies:
+        copy.start()
+    copies[0].wait()
+    copies[1].wait()
+    ups, downs = [0.0] * 8, [0.0] * 8
     for k in range(8):
         weight = occ_ref[k].astype(F32) * (0.125 / DEN)
         up = spin_ref[k] == 0
-        weights.append((jnp.where(up, weight, 0.0), jnp.where(up, 0.0, weight)))
+        up, down = jnp.where(up, weight, 0.0), jnp.where(up, 0.0, weight)
+        copies[2 + k].wait()
+        for x in range(8):
+            square = orb_ref[k, x] * orb_ref[k, x]
+            ups[x] = ups[x] + up * square
+            downs[x] = downs[x] + down * square
     for x in range(8):
-        up, down = 0.0, 0.0
-        for k in range(8):
-            square = orb_ref[k, x] * orb_ref[k, x]
-            up = up + weights[k][0] * square
-            down = down + weights[k][1] * square
-        both = jnp.concatenate([up, down], axis=-1)
+        both = jnp.concatenate([ups[x], downs[x]], axis=-1)
         for copy in range(BANDS):
             out_ref[copy, pl.ds(16 * x, 16), :] = both
 
 
 def density(spin_group, occupation, orbitals):
-    smem = pl.BlockSpec(memory_space=pltpu.SMEM)
+    anywhere = pl.BlockSpec(memory_space=pl.ANY)
     vmem = pl.BlockSpec(memory_space=pltpu.VMEM)
     return pl.pallas_call(
         density_kernel,
         out_shape=jax.ShapeDtypeStruct((BANDS, 128, 128), F32),
-        in_specs=[smem, smem, vmem],
+        in_specs=[anywhere] * 3,
         out_specs=vmem,
+        scratch_shapes=[
+            pltpu.SMEM((8,), jnp.int32), pltpu.SMEM((8,), jnp.int32),
+            pltpu.VMEM((8, 8, 16, 64), F32), pltpu.SemaphoreType.DMA((10,)),
+        ],
         compiler_params=pltpu.CompilerParams(vmem_limit_bytes=32 * 2**20),
         name="density",
     )(spin_group, occupation, orbitals)
@@ -289,7 +303,8 @@
             v = r1[2 * k] + r1[2 * k + 1]
             v = 0.5 * pair_z(v[0] + v[1], 2)
             packed = v if packed is None else jnp.where(lane == p, v, packed)
-        far_ref[pl.ds(8 * group, 8), :] = packed
+        for copy in range(RING):
+            far_ref[copy, pl.ds(8 * group, 8), :] = packed
 
 
 def local_part(flags, parts, guess):
@@ -299,7 +314,7 @@
     return pl.pallas_call(
         local_kernel,
         out_shape=(
-            shape(16, 128), shape(26, 8, 128), shape(26, 8, 128),
+            shape(RING, 16, 128), shape(26, 8, 128), shape(26, 8, 128),
             shape(16, 4, 8, 128), shape(10, 2, 8, 128), shape(16, 32, 128),
         ),
         in_specs=[smem, vmem, vmem],
@@ -331,16 +346,20 @@
         return mask
 
     lane = lanes_of((8, 128)) & 3
-    def message(i):
-        shift = i - REACH
-        if shift == 0:
-            return mine_ref, 0, None
-        return far_ref, (0 if shift < 0 else 16), abs(shift)
+    core = place_ref[1]
+    ring, spot = dom // RING, dom % RING
+    even_first = RING * ring
+    odd_first = even_first + jnp.where(spot >= RING // 2, RING // 2, -(RING // 2))
 
     def vector(i, half):
-        ref, row, member = message(i)
-        rows = pl.ds(row + 8 * half, 8)
-        return ref[rows, :] if member is None else ref[member, rows, :]
+        wanted = dom - REACH + i
+        at = wanted - even_first
+        in_even = (at >= 0) & (at < RING)
+        at = jnp.clip(jnp.where(in_even, at, wanted - odd_first), 0, RING - 1)
+        rows = pl.ds(8 * half, 8)
+        held = in_even == (core == 0)
+        v = jnp.where(held, mine_ref[at, rows, :], far_ref[at, rows, :])
+        return jnp.where((wanted >= 0) & (wanted < DOMS), v, 0.0)
 
     b2, t2, r2 = Held(b2_ref, -30), Held(t2_ref, -25), Held(r2_ref, -24)
     for i in range(16):
@@ -446,20 +465,21 @@
 def on_device(orbitals, spin_group, occupation, potential_guess):
     dom = lax.axis_index("dom")
     flags = jnp.stack([dom > 0, dom < DOMS - 1]).astype(F32)
-    place = dom.astype(jnp.int32)[None]
+    core = lax.axis_index("band") % 2
+    place = jnp.stack([dom, core]).astype(jnp.int32)
     parts = lax.all_to_all(density(spin_group, occupation, orbitals), "band", 0, 0)
     far, to_low, to_high, own0, own1, mag = local_part(flags, parts, potential_guess)
 
-    ups = [(k * DOMS + d, k * DOMS + d + k) for k in range(1, BANDS) for d in range(DOMS - k)]
-    downs = [(target, source) for source, target in ups]
-    from_low = lax.ppermute(far, ("band", "dom"), ups)
-    from_high = lax.ppermute(far, ("band", "dom"), downs)
+    rings = [
+        [b * DOMS + (first + 8 * (b % 2) + i) % DOMS for i in range(RING)]
+        for b in range(BANDS) for first in range(0, DOMS, RING)
+    ]
+    mine = lax.all_to_all(far, ("band", "dom"), 0, 0, axis_index_groups=rings)
     near_low = lax.ppermute(to_high, "dom", [(d, d + 1) for d in range(DOMS - 1)])
     near_high = lax.ppermute(to_low, "dom", [(d + 1, d) for d in range(DOMS - 1)])
-    both = jnp.concatenate([from_low, from_high], axis=0)
-    everyone = lax.all_to_all(jnp.broadcast_to(both[None], (BANDS, 32, 128)), "band", 0, 0)
+    other = lax.ppermute(mine, "band", [(b, b ^ 1) for b in range(BANDS)])
     return final_part(
-        place, everyone, far, near_low, near_high, own0, own1, mag, potential_guess
+        place, other, mine, near_low, near_high, own0, own1, mag, potential_guess
     )
 
 

time: 66.3 us -> 65.6 us (0.989)
  the two profiles are of different devices: /device:TPU:26 before, /device:TPU:1 now
where the time goes in v2:
time: 65.6 us; the launch traced here: 65.2 us
  blocking collectives  22 us (34%)
  starting transfers between devices  19.2 us (29%)
  waiting for transfers between devices  14.2 us (22%)
  Pallas kernels  6.66 us (10%)
  local copies, waits for them, and re-layouts  2.35 us (4%)
  between operations  0.7 us (1%)
    all_to_all x1, blocking collectives, on_device(): mine = lax.all_to_all(far, ('band', 'dom'), 0, 0, axis_index_groups=rings)  22 us
    all_to_all x1, starting transfers between devices, on_device(): lax.all_to_all(density(spin_group, occupation, orbitals), 'band', 0, 0)  10.4 us
    all_to_all x1, waiting for transfers between devices, on_device(): lax.all_to_all(density(spin_group, occupation, orbitals), 'band', 0, 0)  9.42 us
    ppermute x1, starting transfers between devices, on_device(): other = lax.ppermute(mine, 'band', [(b, b ^ 1) for b in range(BANDS)])  4.43 us
    ppermute x1, waiting for transfers between devices, on_device(): lax.ppermute(to_low, 'dom', [(d + 1, d) for d in range(DOMS - 1)])  3.8 us
    pallas_call x1, Pallas kernels, final_part(): pl.pallas_call(final_kernel, out_shape=(shape(16, 32, 128), shape(16, 32,...  3.11 us
    ppermute x1, starting transfers between devices, on_device(): lax.ppermute(to_high, 'dom', [(d, d + 1) for d in range(DOMS - 1)])  3.02 us
    unnamed x8, local copies, waits for them, and re-layouts  2.35 us
  transfers between devices with their start and end apart: 4, of which 3 were waited for; matrix products, arithmetic and copies ran while one was open for 0% of the time, Pallas kernels for 0%

profile of v2, /device:TPU:1, one launch (start us, length us, event | category | flops | bytes accessed | tf_op | source)
XLA Modules:
  0.0 65.2 jit_solution(16144667635976149559)
XLA Ops:
  0.6 0.0 copy-start.1
  0.6 1.0 %copy-done.1 = f32[8,8,16,64]{3,2,1,0:T(8,128)S(1)} copy-done((f32[8,8,16,64]{3,2,1,0:T(8,128)S(1)}, f32[8,8,16,64]{3,2,1,0:T(8,128)}, u32[]{:S(2)}) %copy-start.1) | copy-done | bytes 262168
  1.7 0.0 copy-start.2
  1.7 0.7 %copy-done.2 = s32[8]{0:T(128)S(1)} copy-done((s32[8]{0:T(128)S(1)}, s32[8]{0:T(128)}, u32[]{:S(2)}) %copy-start.2) | copy-done | bytes 56
  2.3 0.0 copy-start.3
  2.3 0.7 %copy-done.3 = s32[8]{0:T(128)S(1)} copy-done((s32[8]{0:T(128)S(1)}, s32[8]{0:T(128)}, u32[]{:S(2)}) %copy-start.3) | copy-done | bytes 56
  3.0 1.8 %density.1 = f32[8,128,128]{2,1,0:T(8,128)} custom-call(s32[8]{0:T(128)S(1)} %copy-done.2, s32[8]{0:T(128)S(1)} %copy-done.3, f32[8,8,16,64]{3,2,1,0:T(8,128)S(1)} %copy-done.1), custom_call_target="tpu_custom_call" | custom-call | tf_op jit(solution)/shard_map/density/pallas_call | solution.py:149
  4.8 0.0 copy-start
  4.8 10.4 %all-to-all-start = ((f32[8,128,128]{2,1,0:T(8,128)}), f32[8,128,128]{2,1,0:T(8,128)S(1)}, u32[]{:S(2)}, u32[]{:S(2)}) async-start(f32[8,128,128]{2,1,0:T(8,128)} %density.1), calls=%async_computation | async-start | bytes 1048576 | tf_op jit(solution)/shard_map/all_to_all | solution.py:470
  15.2 0.1 add_convert_fusion.flag_ref
  15.3 9.4 %all-to-all-done.part_ref = f32[8,128,128]{2,1,0:T(8,128)S(1)} async-done(((f32[8,128,128]{2,1,0:T(8,128)}), f32[8,128,128]{2,1,0:T(8,128)S(1)}, u32[]{:S(2)}, u32[]{:S(2)}) %all-to-all-start) | async-done | bytes 524320 | tf_op jit(solution)/shard_map/all_to_all | solution.py:470
  24.7 0.0 copy-done
  24.7 1.8 %local.1 = (f32[16,16,128]{2,1,0:T(8,128)S(1)}, f32[26,8,128]{2,1,0:T(8,128)S(1)}, f32[26,8,128]{2,1,0:T(8,128)S(1)}, f32[16,4,8,128]{3,2,1,0:T(8,128)S(1)}, f32...) custom-call(f32[2]{0:T(128)S(1)} %add_convert_fusion.flag_ref, f32[8,128,128]{2,1,0:T(8,128)S(1)} %all-to-all-done.part_ref, ...), custom_call_target="tpu_custom_call" | custom-call | tf_op jit(solution)/shard_map/local/pallas_call | solution.py:314
  26.5 22.0 %all_to_all.10.mine_ref = f32[16,16,128]{2,1,0:T(8,128)S(1)} all-to-all(f32[16,16,128]{2,1,0:T(8,128)S(1)} %get-tuple-element.8), channel_id=1, replica_groups={{0,1,2,3,4,5,6,7,8,9,10,11,12,13,14,15},{16,17,18,19,20,21,22,23,24,25,..., dimensions={0} | all-to-all | bytes 262144 | tf_op jit(solution)/shard_map/all_to_all | solution.py:477
  48.4 4.4 %collective-permute-start = (f32[16,16,128]{2,1,0:T(8,128)S(1)}, f32[16,16,128]{2,1,0:T(8,128)S(1)}, u32[]{:S(2)}, u32[]{:S(2)}) collective-permute-start(f32[16,16,128]{2,1,0:T(8,128)S(1)} %all_to_all.10.mine_ref), channel_id=1, source_target_pairs={{0,64},{64,0},{128,192},{192,128},{256,320},{320,256},{384,448},{4... | collective-permute-start | bytes 393224 | tf_op jit(solution)/shard_map/ppermute | solution.py:480
  52.9 3.0 %collective-permute-start.1 = (f32[26,8,128]{2,1,0:T(8,128)S(1)}, f32[26,8,128]{2,1,0:T(8,128)S(1)}, u32[]{:S(2)}, u32[]{:S(2)}) collective-permute-start(f32[26,8,128]{2,1,0:T(8,128)S(1)} %get-tuple-element.9), channel_id=1, source_target_pairs={{0,1},{1,2},{2,3},{3,4},{4,5},{5,6},{6,7},{7,8},{8,9},{9,10},{10,1... | collective-permute-start | bytes 319496 | tf_op jit(solution)/shard_map/ppermute | solution.py:478
  55.9 1.3 %collective-permute-start.2 = (f32[26,8,128]{2,1,0:T(8,128)S(1)}, f32[26,8,128]{2,1,0:T(8,128)S(1)}, u32[]{:S(2)}, u32[]{:S(2)}) collective-permute-start(f32[26,8,128]{2,1,0:T(8,128)S(1)} %get-tuple-element.10), channel_id=1, source_target_pairs={{1,0},{2,1},{3,2},{4,3},{5,4},{6,5},{7,6},{8,7},{9,8},{10,9},{11,1... | collective-permute-start | bytes 319496 | tf_op jit(solution)/shard_map/ppermute | solution.py:479
  57.2 0.1 pad_add_fusion.place_ref
  57.3 1.0 %collective-permute-done.1.low_ref = f32[26,8,128]{2,1,0:T(8,128)S(1)} collective-permute-done((f32[26,8,128]{2,1,0:T(8,128)S(1)}, f32[26,8,128]{2,1,0:T(8,128)S(1)}, u32[]{:S(2)}, u32[]{:S(2)}) %collective-permute-start.1) | collective-permute-done | bytes 106528 | tf_op jit(solution)/shard_map/ppermute | solution.py:478
  58.3 3.8 %collective-permute-done.2.high_ref = f32[26,8,128]{2,1,0:T(8,128)S(1)} collective-permute-done((f32[26,8,128]{2,1,0:T(8,128)S(1)}, f32[26,8,128]{2,1,0:T(8,128)S(1)}, u32[]{:S(2)}, u32[]{:S(2)}) %collective-permute-start.2) | collective-permute-done | bytes 106528 | tf_op jit(solution)/shard_map/ppermute | solution.py:479
  62.1 0.0 collective-permute-done.far_ref
  62.1 3.1 %final.1 = (f32[16,32,128]{2,1,0:T(8,128)}, f32[16,32,128]{2,1,0:T(8,128)}) custom-call(s32[2]{0:T(128)S(1)} %pad_add_fusion.place_ref, f32[16,16,128]{2,1,0:T(8,128)S(1)} %collective-permute-done.far_ref, f32[16,16,128]{2,1,0:T(8,128)S(1)} %all_to_all.10.mine_ref, f32[26,8,128]{2,1,0:T(8,128)S(1)} %collective-permute-done.1.low_ref, ...), custom_call_target="tpu_custom_call" | custom-call | tf_op jit(solution)/shard_map/final/pallas_call | solution.py:451
Async XLA Ops:
  0.6 1.0 %copy-start.1 = (f32[8,8,16,64]{3,2,1,0:T(8,128)S(1)}, f32[8,8,16,64]{3,2,1,0:T(8,128)}, u32[]{:S(2)}) copy-start(f32[8,8,16,64]{3,2,1,0:T(8,128)} %orb_hbm.1) | copy-start | bytes 786436
  1.7 0.7 %copy-start.2 = (s32[8]{0:T(128)S(1)}, s32[8]{0:T(128)}, u32[]{:S(2)}) copy-start(s32[8]{0:T(128)} %spin_hbm.1) | copy-start | bytes 100
  2.3 0.7 %copy-start.3 = (s32[8]{0:T(128)S(1)}, s32[8]{0:T(128)}, u32[]{:S(2)}) copy-start(s32[8]{0:T(128)} %occ_hbm.1) | copy-start | bytes 100
  4.8 19.9 %copy-start = (f32[16,32,128]{2,1,0:T(8,128)S(1)}, f32[16,32,128]{2,1,0:T(8,128)}, u32[]{:S(2)}) copy-start(f32[16,32,128]{2,1,0:T(8,128)} %guess_ref.3) | copy-start | bytes 786436
  4.8 19.9 %all-to-all-start = ((f32[8,128,128]{2,1,0:T(8,128)}), f32[8,128,128]{2,1,0:T(8,128)S(1)}, u32[]{:S(2)}, u32[]{:S(2)}) async-start(f32[8,128,128]{2,1,0:T(8,128)} %density.1), calls=%async_computation | async-start | bytes 1048576 | tf_op jit(solution)/shard_map/all_to_all | solution.py:470
  48.4 13.6 %collective-permute-start = (f32[16,16,128]{2,1,0:T(8,128)S(1)}, f32[16,16,128]{2,1,0:T(8,128)S(1)}, u32[]{:S(2)}, u32[]{:S(2)}) collective-permute-start(f32[16,16,128]{2,1,0:T(8,128)S(1)} %all_to_all.10.mine_ref), channel_id=1, source_target_pairs={{0,64},{64,0},{128,192},{192,128},{256,320},{320,256},{384,448},{4... | collective-permute-start | bytes 393224 | tf_op jit(solution)/shard_map/ppermute | solution.py:480
  52.9 5.4 %collective-permute-start.1 = (f32[26,8,128]{2,1,0:T(8,128)S(1)}, f32[26,8,128]{2,1,0:T(8,128)S(1)}, u32[]{:S(2)}, u32[]{:S(2)}) collective-permute-start(f32[26,8,128]{2,1,0:T(8,128)S(1)} %get-tuple-element.9), channel_id=1, source_target_pairs={{0,1},{1,2},{2,3},{3,4},{4,5},{5,6},{6,7},{7,8},{8,9},{9,10},{10,1... | collective-permute-start | bytes 319496 | tf_op jit(solution)/shard_map/ppermute | solution.py:478
  55.9 6.2 %collective-permute-start.2 = (f32[26,8,128]{2,1,0:T(8,128)S(1)}, f32[26,8,128]{2,1,0:T(8,128)S(1)}, u32[]{:S(2)}, u32[]{:S(2)}) collective-permute-start(f32[26,8,128]{2,1,0:T(8,128)S(1)} %get-tuple-element.10), channel_id=1, source_target_pairs={{1,0},{2,1},{3,2},{4,3},{5,4},{6,5},{7,6},{8,7},{9,8},{10,9},{11,1... | collective-permute-start | bytes 319496 | tf_op jit(solution)/shard_map/ppermute | solution.py:479

commit v3 on v2

--- a/solution.py
+++ b/solution.py
@@ -117,7 +117,7 @@
         held.put(k, mask(k, got))
 
 
-def density_kernel(spin_hbm, occ_hbm, orb_hbm, out_ref, spin_ref, occ_ref, orb_ref, sems):
+def density_kernel(spin_hbm, occ_hbm, orb_hbm, out_hbm, spin_ref, occ_ref, orb_ref, own_ref, sems):
     copies = [
         pltpu.make_async_copy(spin_hbm, spin_ref, sems.at[8]),
         pltpu.make_async_copy(occ_hbm, occ_ref, sems.at[9]),
@@ -138,24 +138,27 @@
             ups[x] = ups[x] + up * square
             downs[x] = downs[x] + down * square
     for x in range(8):
-        both = jnp.concatenate([ups[x], downs[x]], axis=-1)
-        for copy in range(BANDS):
-            out_ref[copy, pl.ds(16 * x, 16), :] = both
+        own_ref[pl.ds(16 * x, 16), :] = jnp.concatenate([ups[x], downs[x]], axis=-1)
+    copies = [pltpu.make_async_copy(own_ref, out_hbm.at[b], sems.at[b]) for b in range(BANDS)]
+    for copy in copies:
+        copy.start()
+    for copy in copies:
+        copy.wait()
 
 
 def density(spin_group, occupation, orbitals):
-    anywhere = pl.BlockSpec(memory_space=pl.ANY)
-    vmem = pl.BlockSpec(memory_space=pltpu.VMEM)
+    hbm = pl.BlockSpec(memory_space=pltpu.HBM)
     return pl.pallas_call(
         density_kernel,
         out_shape=jax.ShapeDtypeStruct((BANDS, 128, 128), F32),
-        in_specs=[anywhere] * 3,
-        out_specs=vmem,
+        in_specs=[hbm] * 3,
+        out_specs=hbm,
         scratch_shapes=[
             pltpu.SMEM((8,), jnp.int32), pltpu.SMEM((8,), jnp.int32),
-            pltpu.VMEM((8, 8, 16, 64), F32), pltpu.SemaphoreType.DMA((10,)),
+            pltpu.VMEM((8, 8, 16, 64), F32), pltpu.VMEM((128, 128), F32),
+            pltpu.SemaphoreType.DMA((10,)),
         ],
-        compiler_params=pltpu.CompilerParams(vmem_limit_bytes=32 * 2**20),
+        compiler_params=pltpu.CompilerParams(vmem_limit_bytes=60 * 2**20),
         name="density",
     )(spin_group, occupation, orbitals)
 
@@ -197,8 +200,8 @@
 
 def local_kernel(
     flag_ref, part_ref, guess_ref,
-    far_ref, low_ref, high_ref, own0_ref, own1_ref, mag_ref,
-    sum_ref, wide_ref, d_ref, t_ref, r_ref, t1_ref,
+    far_hbm, low_ref, high_ref, own0_ref, own1_ref, mag_ref,
+    sum_ref, wide_ref, d_ref, t_ref, r_ref, t1_ref, far_ref, sems,
 ):
     low_flag, high_flag = flag_ref[0], flag_ref[1]
 
@@ -303,8 +306,12 @@
             v = r1[2 * k] + r1[2 * k + 1]
             v = 0.5 * pair_z(v[0] + v[1], 2)
             packed = v if packed is None else jnp.where(lane == p, v, packed)
-        for copy in range(RING):
-            far_ref[copy, pl.ds(8 * group, 8), :] = packed
+        far_ref[pl.ds(8 * group, 8), :] = packed
+    copies = [pltpu.make_async_copy(far_ref, far_hbm.at[i], sems.at[i]) for i in range(RING)]
+    for copy in copies:
+        copy.start()
+    for copy in copies:
+        copy.wait()
 
 
 def local_part(flags, parts, guess):
@@ -318,11 +325,12 @@
             shape(16, 4, 8, 128), shape(10, 2, 8, 128), shape(16, 32, 128),
         ),
         in_specs=[smem, vmem, vmem],
-        out_specs=(vmem,) * 6,
+        out_specs=(pl.BlockSpec(memory_space=pltpu.HBM),) + (vmem,) * 5,
         scratch_shapes=[
             pltpu.VMEM((128, 128), F32), pltpu.VMEM((2, 128, 128), F32),
             pltpu.VMEM((18, 4, 8, 128), F32), pltpu.VMEM((20, 4, 8, 128), F32),
             pltpu.VMEM((22, 4, 8, 128), F32), pltpu.VMEM((16, 2, 8, 128), F32),
+            pltpu.VMEM((16, 128), F32), pltpu.SemaphoreType.DMA((RING,)),
         ],
         compiler_params=pltpu.CompilerParams(vmem_limit_bytes=32 * 2**20),
         name="local",
@@ -477,6 +485,7 @@
     mine = lax.all_to_all(far, ("band", "dom"), 0, 0, axis_index_groups=rings)
     near_low = lax.ppermute(to_high, "dom", [(d, d + 1) for d in range(DOMS - 1)])
     near_high = lax.ppermute(to_low, "dom", [(d + 1, d) for d in range(DOMS - 1)])
+    mine, near_low, near_high = lax.optimization_barrier((mine, near_low, near_high))
     other = lax.ppermute(mine, "band", [(b, b ^ 1) for b in range(BANDS)])
     return final_part(
         place, other, mine, near_low, near_high, own0, own1, mag, potential_guess

time: 65.6 us -> 56 us (0.85)
  blocking collectives: 22 us -> 0 us
  starting transfers between devices: 19.2 us -> 32.4 us
  local copies, waits for them, and re-layouts: 2.35 us -> 0.01 us
  Pallas kernels: 6.66 us -> 7.71 us
    all_to_all x1 -> x0, blocking collectives: 22 us -> none  [on_device(): mine = lax.all_to_all(far, ('band', 'dom'), 0, 0, axis_index_groups=rings)]
    all_to_all x0 -> x1, starting transfers between devices: none -> 16.3 us  [on_device(): mine = lax.all_to_all(far, ('band', 'dom'), 0, 0, axis_index_groups=rings)]
    unnamed x8 -> x2, local copies, waits for them, and re-layouts: 2.35 us -> 0.01 us
    ppermute x1, starting transfers between devices: 4.43 us -> 2.29 us  [on_device(): other = lax.ppermute(mine, 'band', [(b, b ^ 1) for b in range(BANDS)])]
    ppermute x1, waiting for transfers between devices: 3.8 us -> 2 us  [on_device(): lax.ppermute(to_low, 'dom', [(d + 1, d) for d in range(DOMS - 1)])]
    ppermute x1, waiting for transfers between devices: 0.99 us -> 2.32 us  [on_device(): lax.ppermute(to_high, 'dom', [(d, d + 1) for d in range(DOMS - 1)])]
    ppermute x1, waiting for transfers between devices: 0.01 us -> 0.88 us  [on_device(): other = lax.ppermute(mine, 'band', [(b, b ^ 1) for b in range(BANDS)])]
    ppermute x1, starting transfers between devices: 3.02 us -> 2.18 us  [on_device(): lax.ppermute(to_high, 'dom', [(d, d + 1) for d in range(DOMS - 1)])]
  transfers between devices with their start and end apart: 4 -> 5, of which waited for: 3 -> 4; matrix products, arithmetic and copies ran while one was open for 0% -> 0% of each run, Pallas kernels for 0% -> 0%
where the time goes in v3:
time: 56 us; the launch traced here: 55.6 us
  starting transfers between devices  32.4 us (58%)
  waiting for transfers between devices  14.6 us (26%)
  Pallas kernels  7.71 us (14%)
  between operations  0.69 us (1%)
    all_to_all x1, starting transfers between devices, on_device(): mine = lax.all_to_all(far, ('band', 'dom'), 0, 0, axis_index_groups=rings)  16.3 us
    all_to_all x1, starting transfers between devices, on_device(): lax.all_to_all(density(spin_group, occupation, orbitals), 'band', 0, 0)  10.4 us
    all_to_all x1, waiting for transfers between devices, on_device(): lax.all_to_all(density(spin_group, occupation, orbitals), 'band', 0, 0)  9.42 us
    pallas_call x1, Pallas kernels, final_part(): pl.pallas_call(final_kernel, out_shape=(shape(16, 32, 128), shape(16, 32,...  3.11 us
    pallas_call x1, Pallas kernels, local_part(): pl.pallas_call(local_kernel, out_shape=(shape(RING, 16, 128), shape(26, 8...  2.56 us
    ppermute x1, waiting for transfers between devices, on_device(): lax.ppermute(to_high, 'dom', [(d, d + 1) for d in range(DOMS - 1)])  2.32 us
    ppermute x1, starting transfers between devices, on_device(): other = lax.ppermute(mine, 'band', [(b, b ^ 1) for b in range(BANDS)])  2.29 us
    ppermute x1, starting transfers between devices, on_device(): lax.ppermute(to_high, 'dom', [(d, d + 1) for d in range(DOMS - 1)])  2.18 us
  transfers between devices with their start and end apart: 5, of which 4 were waited for; matrix products, arithmetic and copies ran while one was open for 0% of the time, Pallas kernels for 0%

profile of v3, /device:TPU:1, one launch (start us, length us, event | category | flops | bytes accessed | tf_op | source)
XLA Modules:
  0.0 55.6 jit_solution(1427157534856219405)
XLA Ops:
  0.6 2.0 %density.1 = f32[8,128,128]{2,1,0:T(8,128)} custom-call(s32[8]{0:T(128)} %spin_hbm.1, s32[8]{0:T(128)} %occ_hbm.1, f32[8,8,16,64]{3,2,1,0:T(8,128)} %orb_hbm.1), custom_call_target="tpu_custom_call" | custom-call | tf_op jit(solution)/shard_map/density/pallas_call | solution.py:151
  2.7 0.0 copy-start
  2.7 10.4 %all-to-all-start = ((f32[8,128,128]{2,1,0:T(8,128)}), f32[8,128,128]{2,1,0:T(8,128)S(1)}, u32[]{:S(2)}, u32[]{:S(2)}) async-start(f32[8,128,128]{2,1,0:T(8,128)} %density.1), calls=%async_computation | async-start | bytes 1048576 | tf_op jit(solution)/shard_map/all_to_all | solution.py:478
  13.1 0.1 add_convert_fusion.flag_ref
  13.2 9.4 %all-to-all-done.part_ref = f32[8,128,128]{2,1,0:T(8,128)S(1)} async-done(((f32[8,128,128]{2,1,0:T(8,128)}), f32[8,128,128]{2,1,0:T(8,128)S(1)}, u32[]{:S(2)}, u32[]{:S(2)}) %all-to-all-start) | async-done | bytes 524320 | tf_op jit(solution)/shard_map/all_to_all | solution.py:478
  22.6 0.0 copy-done
  22.6 2.6 %local.1 = (f32[16,16,128]{2,1,0:T(8,128)}, f32[26,8,128]{2,1,0:T(8,128)S(1)}, f32[26,8,128]{2,1,0:T(8,128)S(1)}, f32[16,4,8,128]{3,2,1,0:T(8,128)S(1)}, f32[10,...) custom-call(f32[2]{0:T(128)S(1)} %add_convert_fusion.flag_ref, f32[8,128,128]{2,1,0:T(8,128)S(1)} %all-to-all-done.part_ref, ...), custom_call_target="tpu_custom_call" | custom-call | tf_op jit(solution)/shard_map/local/pallas_call | solution.py:321
  25.2 16.3 %all-to-all-start.1 = ((f32[16,16,128]{2,1,0:T(8,128)}), f32[16,16,128]{2,1,0:T(8,128)S(1)}, u32[]{:S(2)}, u32[]{:S(2)}) async-start(f32[16,16,128]{2,1,0:T(8,128)} %get-tuple-element.11), calls=%async_computation.1 | async-start | bytes 262144 | tf_op jit(solution)/shard_map/all_to_all | solution.py:485
  41.4 2.2 %collective-permute-start = (f32[26,8,128]{2,1,0:T(8,128)S(1)}, f32[26,8,128]{2,1,0:T(8,128)S(1)}, u32[]{:S(2)}, u32[]{:S(2)}) collective-permute-start(f32[26,8,128]{2,1,0:T(8,128)S(1)} %get-tuple-element.12), channel_id=1, source_target_pairs={{0,1},{1,2},{2,3},{3,4},{4,5},{5,6},{6,7},{7,8},{8,9},{9,10},{10,1... | collective-permute-start | bytes 319496 | tf_op jit(solution)/shard_map/ppermute | solution.py:486
  43.6 1.3 %collective-permute-start.1 = (f32[26,8,128]{2,1,0:T(8,128)S(1)}, f32[26,8,128]{2,1,0:T(8,128)S(1)}, u32[]{:S(2)}, u32[]{:S(2)}) collective-permute-start(f32[26,8,128]{2,1,0:T(8,128)S(1)} %get-tuple-element.13), channel_id=1, source_target_pairs={{1,0},{2,1},{3,2},{4,3},{5,4},{6,5},{7,6},{8,7},{9,8},{10,9},{11,1... | collective-permute-start | bytes 319496 | tf_op jit(solution)/shard_map/ppermute | solution.py:487
  44.9 2.3 %collective-permute-done.low_ref = f32[26,8,128]{2,1,0:T(8,128)S(1)} collective-permute-done((f32[26,8,128]{2,1,0:T(8,128)S(1)}, f32[26,8,128]{2,1,0:T(8,128)S(1)}, u32[]{:S(2)}, u32[]{:S(2)}) %collective-permute-start) | collective-permute-done | bytes 106528 | tf_op jit(solution)/shard_map/ppermute | solution.py:486
  47.3 2.0 %collective-permute-done.1.high_ref = f32[26,8,128]{2,1,0:T(8,128)S(1)} collective-permute-done((f32[26,8,128]{2,1,0:T(8,128)S(1)}, f32[26,8,128]{2,1,0:T(8,128)S(1)}, u32[]{:S(2)}, u32[]{:S(2)}) %collective-permute-start.1) | collective-permute-done | bytes 106528 | tf_op jit(solution)/shard_map/ppermute | solution.py:487
  49.3 0.0 all-to-all-done.1.mine_ref
  49.3 2.3 %collective-permute-start.2 = (f32[16,16,128]{2,1,0:T(8,128)S(1)}, f32[16,16,128]{2,1,0:T(8,128)S(1)}, u32[]{:S(2)}, u32[]{:S(2)}) collective-permute-start(f32[16,16,128]{2,1,0:T(8,128)S(1)} %all-to-all-done.1.mine_ref), channel_id=1, source_target_pairs={{0,64},{64,0},{128,192},{192,128},{256,320},{320,256},{384,448},{4... | collective-permute-start | bytes 393224 | tf_op jit(solution)/shard_map/ppermute | solution.py:489
  51.6 0.1 pad_add_fusion.place_ref
  51.6 0.9 %collective-permute-done.2.far_ref = f32[16,16,128]{2,1,0:T(8,128)S(1)} collective-permute-done((f32[16,16,128]{2,1,0:T(8,128)S(1)}, f32[16,16,128]{2,1,0:T(8,128)S(1)}, u32[]{:S(2)}, u32[]{:S(2)}) %collective-permute-start.2) | collective-permute-done | bytes 131104 | tf_op jit(solution)/shard_map/ppermute | solution.py:489
  52.5 3.1 %final.1 = (f32[16,32,128]{2,1,0:T(8,128)}, f32[16,32,128]{2,1,0:T(8,128)}) custom-call(s32[2]{0:T(128)S(1)} %pad_add_fusion.place_ref, f32[16,16,128]{2,1,0:T(8,128)S(1)} %collective-permute-done.2.far_ref, f32[16,16,128]{2,1,0:T(8,128)S(1)} %all-to-all-done.1.mine_ref, f32[26,8,128]{2,1,0:T(8,128)S(1)} %collective-permute-done.low_ref, ...), custom_call_target="tpu_custom_call" | custom-call | tf_op jit(solution)/shard_map/final/pallas_call | solution.py:459
Async XLA Ops:
  2.7 19.9 %copy-start = (f32[16,32,128]{2,1,0:T(8,128)S(1)}, f32[16,32,128]{2,1,0:T(8,128)}, u32[]{:S(2)}) copy-start(f32[16,32,128]{2,1,0:T(8,128)} %guess_ref.3) | copy-start | bytes 786436
  2.7 19.9 %all-to-all-start = ((f32[8,128,128]{2,1,0:T(8,128)}), f32[8,128,128]{2,1,0:T(8,128)S(1)}, u32[]{:S(2)}, u32[]{:S(2)}) async-start(f32[8,128,128]{2,1,0:T(8,128)} %density.1), calls=%async_computation | async-start | bytes 1048576 | tf_op jit(solution)/shard_map/all_to_all | solution.py:478
  25.2 24.1 %all-to-all-start.1 = ((f32[16,16,128]{2,1,0:T(8,128)}), f32[16,16,128]{2,1,0:T(8,128)S(1)}, u32[]{:S(2)}, u32[]{:S(2)}) async-start(f32[16,16,128]{2,1,0:T(8,128)} %get-tuple-element.11), calls=%async_computation.1 | async-start | bytes 262144 | tf_op jit(solution)/shard_map/all_to_all | solution.py:485
  41.4 5.8 %collective-permute-start = (f32[26,8,128]{2,1,0:T(8,128)S(1)}, f32[26,8,128]{2,1,0:T(8,128)S(1)}, u32[]{:S(2)}, u32[]{:S(2)}) collective-permute-start(f32[26,8,128]{2,1,0:T(8,128)S(1)} %get-tuple-element.12), channel_id=1, source_target_pairs={{0,1},{1,2},{2,3},{3,4},{4,5},{5,6},{6,7},{7,8},{8,9},{9,10},{10,1... | collective-permute-start | bytes 319496 | tf_op jit(solution)/shard_map/ppermute | solution.py:486
  43.6 5.6 %collective-permute-start.1 = (f32[26,8,128]{2,1,0:T(8,128)S(1)}, f32[26,8,128]{2,1,0:T(8,128)S(1)}, u32[]{:S(2)}, u32[]{:S(2)}) collective-permute-start(f32[26,8,128]{2,1,0:T(8,128)S(1)} %get-tuple-element.13), channel_id=1, source_target_pairs={{1,0},{2,1},{3,2},{4,3},{5,4},{6,5},{7,6},{8,7},{9,8},{10,9},{11,1... | collective-permute-start | bytes 319496 | tf_op jit(solution)/shard_map/ppermute | solution.py:487
  49.3 3.3 %collective-permute-start.2 = (f32[16,16,128]{2,1,0:T(8,128)S(1)}, f32[16,16,128]{2,1,0:T(8,128)S(1)}, u32[]{:S(2)}, u32[]{:S(2)}) collective-permute-start(f32[16,16,128]{2,1,0:T(8,128)S(1)} %all-to-all-done.1.mine_ref), channel_id=1, source_target_pairs={{0,64},{64,0},{128,192},{192,128},{256,320},{320,256},{384,448},{4... | collective-permute-start | bytes 393224 | tf_op jit(solution)/shard_map/ppermute | solution.py:489

commit v4 on v3

v4 whole, which is shorter than its diff:
```python
import functools

import jax
import jax.numpy as jnp
from jax import lax
from jax.experimental import pallas as pl
from jax.experimental.pallas import tpu as pltpu
from jax.sharding import PartitionSpec as P

DEN = 16
BANDS = 8
DOMS = 64
REACH = 7
RING = 16
ALPHA = 1.0 / 9.0
SOURCE_SCALE = 0.6
F32 = jnp.float32


def lanes_of(shape):
    return lax.broadcasted_iota(jnp.int32, shape, len(shape) - 1)


def rows_of(shape):
    return lax.broadcasted_iota(jnp.int32, shape, len(shape) - 2)


def sides_z(v, step):
    lane = lanes_of(v.shape)
    ax = v.ndim - 1
    left = jnp.where(lane >= step, pltpu.roll(v, step, ax), 0.0)
    right = jnp.where(lane < 128 - step, pltpu.roll(v, 128 - step, ax), 0.0)
    return left + right


def from_below(v, step=1):
    return jnp.where(rows_of(v.shape) >= step, pltpu.roll(v, step, v.ndim - 2), 0.0)


def from_above(v, step=1):
    return jnp.where(rows_of(v.shape) < 8 - step, pltpu.roll(v, 8 - step, v.ndim - 2), 0.0)


def sides_y(v, step):
    if v.ndim == 2:
        return from_below(v, step) + from_above(v, step)
    parts = [v[q] for q in range(v.shape[0])]
    n = len(parts)
    out = []
    for q in range(n):
        lower = parts[q - 1] if q > 0 else from_below(parts[n - 1])
        upper = parts[q + 1] if q < n - 1 else from_above(parts[0])
        out.append(lower + upper)
    return jnp.stack(out, axis=0)


def smooth(low, v, high, zstep, ystep=1):
    around = sides_y(v, ystep) + sides_z(v, zstep)
    if low is not None:
        around = around + low
    if high is not None:
        around = around + high
    return v * (1.0 / 3.0) + around * ALPHA


def pair_z(v, step):
    lane = lanes_of(v.shape)
    ax = v.ndim - 1
    other = jnp.where((lane & step) == 0, pltpu.roll(v, 128 - step, ax), pltpu.roll(v, step, ax))
    return v + other


def pair_y(v, step):
    row = rows_of(v.shape)
    ax = v.ndim - 2
    other = jnp.where((row & step) == 0, pltpu.roll(v, 8 - step, ax), pltpu.roll(v, step, ax))
    return v + other


def run_T(src, planes, zstep, ystep=1, mask=None):
    out = {}
    for k in planes:
        v = src.get(k)
        low, high = src.get(k - 1), src.get(k + 1)
        if v is None:
            edge = low if low is not None else high
            got = edge * ALPHA
        else:
            got = smooth(low, v, high, zstep, ystep)
        out[k] = got if mask is None else mask(k, got)
    return out


class Held:
    def __init__(self, ref, first):
        self.ref, self.first, self.have = ref, first, set()

    def put(self, k, value):
        self.ref[k - self.first] = value
        self.have.add(k)

    def get(self, k):
        return self.ref[k - self.first] if k in self.have else None

    def __getitem__(self, k):
        return self.ref[k - self.first]


def hold_T(src, held, planes, zstep, mask):
    for k in planes:
        v = src.get(k)
        low, high = src.get(k - 1), src.get(k + 1)
        if v is None:
            got = (low if low is not None else high) * ALPHA
        else:
            got = smooth(low, v, high, zstep)
        held.put(k, mask(k, got))


def refine_matrix(rows, columns):
    row = lax.broadcasted_iota(jnp.int32, (rows, columns), 0)
    col = lax.broadcasted_iota(jnp.int32, (rows, columns), 1)
    cell, spin = row & 63, row >> 6
    fine, half = col & 127, col >> 7
    own = fine >> 1
    other = jnp.where((fine & 1) == 0, own - 1, own + 1)
    value = jnp.where(cell == own, 0.75, jnp.where(cell == other, 0.25, 0.0))
    return jnp.where((spin == 1) & (half == 1), -value, value)


def refine_y(pair):
    first, second = pair
    return jnp.stack(
        [
            0.75 * first + 0.25 * from_below(second),
            0.75 * first + 0.25 * second,
            0.75 * second + 0.25 * first,
            0.75 * second + 0.25 * from_above(first),
        ],
        axis=0,
    )


def refine_x(coarse, k):
    i = k // 2
    other = i - 1 if k % 2 == 0 else i + 1
    total = None
    for j, factor in ((i, 0.75), (other, 0.25)):
        if 0 <= j < 8:
            term = factor * coarse[j]
            total = term if total is None else total + term
    return total


def refine_z(coarse, columns):
    return jnp.dot(
        coarse, refine_matrix(coarse.shape[1], columns),
        precision=lax.Precision.HIGHEST, preferred_element_type=F32,
    )


def masks(dom):
    low_flag = jnp.where(dom > 0, 1.0, 0.0).astype(F32)
    high_flag = jnp.where(dom < DOMS - 1, 1.0, 0.0).astype(F32)

    def masked(last):
        def mask(k, v):
            if k < 0:
                return v * low_flag
            if k > last:
                return v * high_flag
            return v
        return mask

    return masked(15), masked(7)


def guess_planes(guess_ref):
    def guess(k):
        if not 0 <= k < 16:
            return None
        return jnp.stack([guess_ref[k, pl.ds(q, 8, stride=4), :] for q in range(4)], axis=0)
    return guess


def restricted(r, k):
    total = None
    for fine in (2 * k, 2 * k + 1):
        v = r.get(fine)
        if v is not None:
            total = v if total is None else total + v
    total = jnp.stack([total[0] + total[1], total[2] + total[3]], axis=0)
    return 0.5 * pair_z(total, 1)


def geometric(b, t, r, k, zstep):
    low, v, high = r.get(k - 1), r.get(k), r.get(k + 1)
    if v is None:
        last = (low if low is not None else high) * ALPHA
    else:
        last = smooth(low, v, high, zstep)
    for term in (r.get(k), t.get(k), b.get(k)):
        if term is not None:
            last = last + term
    return last * ALPHA


def copy_all(source, target, count, sems):
    copies = [pltpu.make_async_copy(source, target.at[i], sems.at[i]) for i in range(count)]
    for copy in copies:
        copy.start()
    return copies


def density_kernel(
    spin_hbm, occ_hbm, orb_hbm, part_hbm, spin_ref, occ_ref, orb_ref, own_ref, sems,
):
    loads = [
        pltpu.make_async_copy(spin_hbm, spin_ref, sems.at[8]),
        pltpu.make_async_copy(occ_hbm, occ_ref, sems.at[9]),
    ]
    loads += [pltpu.make_async_copy(orb_hbm.at[k], orb_ref.at[k], sems.at[k]) for k in range(8)]
    for load in loads:
        load.start()
    loads[0].wait()
    loads[1].wait()
    ups, downs = [0.0] * 8, [0.0] * 8
    for k in range(8):
        weight = occ_ref[k].astype(F32) * (0.125 / DEN)
        up = spin_ref[k] == 0
        up, down = jnp.where(up, weight, 0.0), jnp.where(up, 0.0, weight)
        loads[2 + k].wait()
        for x in range(8):
            square = orb_ref[k, x] * orb_ref[k, x]
            ups[x] = ups[x] + up * square
            downs[x] = downs[x] + down * square
    for x in range(8):
        own_ref[pl.ds(16 * x, 16), :] = jnp.concatenate([ups[x], downs[x]], axis=-1)
    for copy in copy_all(own_ref, part_hbm, BANDS, sems):
        copy.wait()


def density(spin_group, occupation, orbitals):
    hbm = pl.BlockSpec(memory_space=pltpu.HBM)
    return pl.pallas_call(
        density_kernel,
        out_shape=jax.ShapeDtypeStruct((BANDS, 128, 128), F32),
        in_specs=[hbm] * 3,
        out_specs=hbm,
        scratch_shapes=[
            pltpu.SMEM((8,), jnp.int32), pltpu.SMEM((8,), jnp.int32),
            pltpu.VMEM((8, 8, 16, 64), F32), pltpu.VMEM((128, 128), F32),
            pltpu.SemaphoreType.DMA((10,)),
        ],
        compiler_params=pltpu.CompilerParams(vmem_limit_bytes=60 * 2**20),
        name="density",
    )(spin_group, occupation, orbitals)


def guess_kernel(guess_ref, out_ref):
    inside0, _ = masks(lax.axis_index("dom"))
    guess = guess_planes(guess_ref)
    for k in range(-1, 17):
        v, low, high = guess(k), guess(k - 1), guess(k + 1)
        around = None
        if v is not None:
            around = sides_y(v, 1) + sides_z(v, 1)
        for side in (low, high):
            if side is not None:
                around = side if around is None else around + side
        out_ref[k + 1] = inside0(k, around - 6.0 * v if v is not None else around)


def guess_part(guess):
    vmem = pl.BlockSpec(memory_space=pltpu.VMEM)
    return pl.pallas_call(
        guess_kernel,
        out_shape=jax.ShapeDtypeStruct((18, 4, 8, 128), F32),
        in_specs=[vmem],
        out_specs=vmem,
        compiler_params=pltpu.CompilerParams(vmem_limit_bytes=32 * 2**20),
        cost_estimate=pl.CostEstimate(flops=10**6, bytes_accessed=2**19, transcendentals=0),
        name="guess",
    )(guess)


def far_kernel(
    part_ref, applied_ref, far_hbm, minus_ref, d_ref, t_ref, r_ref, b1_ref, t1_ref, r1_ref,
    sum_ref, wide_ref, far_ref, sems,
):
    inside0, inside1 = masks(lax.axis_index("dom"))
    for x in range(8):
        rows = pl.ds(16 * x, 16)
        total = part_ref[0, rows, :]
        for band in range(1, BANDS):
            total = total + part_ref[band, rows, :]
        sum_ref[rows, :] = total
    wide = refine_z(sum_ref[...], 256)
    wide_ref[...] = wide[:, :128]
    minus_ref[...] = wide[:, 128:]
    plus = []
    for x in range(8):
        pair = [wide_ref[pl.ds(16 * x + p, 8, stride=2), :] for p in range(2)]
        plus.append(SOURCE_SCALE * refine_y(pair))
    d, t, r = Held(d_ref, -1), Held(t_ref, -2), Held(r_ref, -3)
    for k in range(-1, 17):
        d.put(k, inside0(k, refine_x(plus, k)) + applied_ref[k + 1])
    hold_T(d, t, range(-2, 18), 1, inside0)
    hold_T(t, r, range(-3, 19), 1, inside0)
    b1, t1, r1 = Held(b1_ref, -2), Held(t1_ref, -3), Held(r1_ref, -4)
    for k in range(-2, 10):
        b1.put(k, restricted(r, k))
    hold_T(b1, t1, range(-3, 11), 2, inside1)
    hold_T(t1, r1, range(-4, 12), 2, inside1)
    lane = lanes_of((8, 128)) & 3
    for group in range(2):
        packed = None
        for p in range(4):
            k = 4 * group + p - 2
            v = r1[2 * k] + r1[2 * k + 1]
            v = 0.5 * pair_z(v[0] + v[1], 2)
            packed = v if packed is None else jnp.where(lane == p, v, packed)
        far_ref[pl.ds(8 * group, 8), :] = packed
    for copy in copy_all(far_ref, far_hbm, RING, sems):
        copy.wait()


def far_part(parts, applied):
    vmem = pl.BlockSpec(memory_space=pltpu.VMEM)
    shape = lambda *s: jax.ShapeDtypeStruct(s, F32)
    return pl.pallas_call(
        far_kernel,
        out_shape=(
            shape(RING, 16, 128), shape(128, 128),
            shape(18, 4, 8, 128), shape(20, 4, 8, 128), shape(22, 4, 8, 128),
            shape(12, 2, 8, 128), shape(14, 2, 8, 128), shape(16, 2, 8, 128),
        ),
        in_specs=[vmem, vmem],
        out_specs=(pl.BlockSpec(memory_space=pltpu.HBM),) + (vmem,) * 7,
        scratch_shapes=[
            pltpu.VMEM((128, 128), F32), pltpu.VMEM((128, 128), F32),
            pltpu.VMEM((16, 128), F32), pltpu.SemaphoreType.DMA((RING,)),
        ],
        compiler_params=pltpu.CompilerParams(vmem_limit_bytes=32 * 2**20),
        name="far",
    )(parts, applied)


class Given(Held):
    def __init__(self, ref, first):
        super().__init__(ref, first)
        self.have = set(range(first, first + ref.shape[0]))


def near_kernel(
    guess_ref, minus_ref, d_ref, t_ref, r_ref, b1_ref, t1_ref, r1_ref,
    low_ref, high_ref, own0_ref, own1_ref, mag_ref,
):
    d, t, r = Given(d_ref, -1), Given(t_ref, -2), Given(r_ref, -3)
    b1, t1, r1 = Given(b1_ref, -2), Given(t1_ref, -3), Given(r1_ref, -4)
    minus = []
    for x in range(8):
        minus.append(refine_y([minus_ref[pl.ds(16 * x + p, 8, stride=2), :] for p in range(2)]))
    guess = guess_planes(guess_ref)
    for k in range(4):
        low_ref[pl.ds(4 * k, 4)] = geometric(d, t, r, k - 4, 1)
        high_ref[pl.ds(4 * k, 4)] = geometric(d, t, r, k + 16, 1)
    low_ref[pl.ds(22, 4)] = refine_x(minus, -1)
    high_ref[pl.ds(22, 4)] = refine_x(minus, 16)
    f1 = {k: geometric(b1, t1, r1, k, 2) for k in range(-5, 13)}
    for k in range(-1, 9):
        own1_ref[k + 1] = f1[k]
    even = (lanes_of((8, 128)) & 1) == 0
    for pair in range(3):
        for q in range(2):
            low_ref[16 + 2 * pair + q] = jnp.where(even, f1[2 * pair - 5][q], f1[2 * pair - 4][q])
            high_ref[16 + 2 * pair + q] = jnp.where(even, f1[2 * pair + 7][q], f1[2 * pair + 8][q])
    for k in range(16):
        own0_ref[k] = geometric(d, t, r, k, 1) + guess(k)
        mag_ref[k] = refine_x(minus, k)


def near_part(guess, *held):
    vmem = pl.BlockSpec(memory_space=pltpu.VMEM)
    shape = lambda *s: jax.ShapeDtypeStruct(s, F32)
    return pl.pallas_call(
        near_kernel,
        out_shape=(
            shape(26, 8, 128), shape(26, 8, 128),
            shape(16, 4, 8, 128), shape(10, 2, 8, 128), shape(16, 4, 8, 128),
        ),
        in_specs=[vmem] * 8,
        out_specs=(vmem,) * 5,
        compiler_params=pltpu.CompilerParams(vmem_limit_bytes=32 * 2**20),
        cost_estimate=pl.CostEstimate(flops=10**6, bytes_accessed=2**20, transcendentals=0),
        name="near",
    )(guess, *held)


def edge_kernel(low_ref, high_ref, own0_ref, own1_ref, mag_ref, base0_ref, base1_ref, mag_out):
    even = (lanes_of((8, 128)) & 1) == 0
    extra = {}
    for ref, first in ((low_ref, -1), (high_ref, 3)):
        for pair in range(3):
            both = [ref[16 + 2 * pair + q] for q in range(2)]
            one = jnp.stack([jnp.where(even, v, pltpu.roll(v, 1, 1)) for v in both], axis=0)
            two = jnp.stack([jnp.where(even, pltpu.roll(v, 127, 1), v) for v in both], axis=0)
            for k, v in ((first + 2 * pair, one), (first + 2 * pair + 1, two)):
                extra[k] = extra[k] + v if k in extra else v
    for k in range(-1, 9):
        base1_ref[k + 1] = own1_ref[k + 1] + extra[k]
    for k in range(16):
        v, mag = own0_ref[k], mag_ref[k]
        if k < 4:
            v = v + low_ref[pl.ds(4 * k, 4)]
        if k >= 12:
            v = v + high_ref[pl.ds(4 * (k - 12), 4)]
        base0_ref[k] = v
        if k == 0:
            mag = mag + low_ref[pl.ds(22, 4)]
        if k == 15:
            mag = mag + high_ref[pl.ds(22, 4)]
        for q in range(4):
            mag_out[k, pl.ds(q, 8, stride=4), :] = mag[q]


def edge_part(low, high, own0, own1, mag):
    vmem = pl.BlockSpec(memory_space=pltpu.VMEM)
    shape = lambda *s: jax.ShapeDtypeStruct(s, F32)
    return pl.pallas_call(
        edge_kernel,
        out_shape=(shape(16, 4, 8, 128), shape(10, 2, 8, 128), shape(16, 32, 128)),
        in_specs=[vmem] * 5,
        out_specs=(vmem,) * 3,
        compiler_params=pltpu.CompilerParams(vmem_limit_bytes=32 * 2**20),
        name="edge",
    )(low, high, own0, own1, mag)


def final_kernel(
    far_ref, mine_ref, base0_ref, base1_ref, pot_out,
    b2_ref, t2_ref, r2_ref, p1_ref,
):
    dom = lax.axis_index("dom")

    def masked(count):
        first, last = -dom * count, (DOMS - dom) * count
        def mask(k, v):
            if 0 <= k < count:
                return v
            ok = (k >= first) & (k < last)
            return jnp.where(ok, v, 0.0)
        return mask

    lane = lanes_of((8, 128)) & 3
    core = lax.axis_index("band") % 2
    ring, spot = dom // RING, dom % RING
    even_first = RING * ring
    odd_first = even_first + jnp.where(spot >= RING // 2, RING // 2, -(RING // 2))

    def vector(i, half):
        wanted = dom - REACH + i
        at = wanted - even_first
        in_even = (at >= 0) & (at < RING)
        at = jnp.clip(jnp.where(in_even, at, wanted - odd_first), 0, RING - 1)
        rows = pl.ds(8 * half, 8)
        held = in_even == (core == 0)
        v = jnp.where(held, mine_ref[at, rows, :], far_ref[at, rows, :])
        return jnp.where((wanted >= 0) & (wanted < DOMS), v, 0.0)

    b2, t2, r2 = Held(b2_ref, -30), Held(t2_ref, -25), Held(r2_ref, -24)
    for i in range(16):
        packed = None
        for part in ((i, 0), (i - 1, 1)):
            if 0 <= part[0] < 15:
                v = vector(*part)
                packed = v if packed is None else packed + v
        for p in range(4):
            only = jnp.where(lane == p, packed, 0.0)
            only = only + pltpu.roll(only, 1 if p % 2 == 0 else 127, 1)
            only = only + pltpu.roll(only, 2 if p < 2 else 126, 1)
            b2.put(4 * (i - REACH) - 2 + p, only)
    inside2, inside3, inside4 = masked(4), masked(2), masked(1)
    hold_T(b2, t2, range(-25, 29), 4, inside2)
    hold_T(t2, r2, range(-24, 28), 4, lambda k, v: v)

    b3 = {}
    for k in range(-12, 14):
        v = pair_y(pair_z(r2[2 * k] + r2[2 * k + 1], 4), 1)
        b3[k] = inside3(k, 0.5 * v)
    t3 = run_T(b3, range(-11, 13), 8, 2, inside3)
    r3 = run_T(t3, range(-10, 12), 8, 2)

    b4 = {}
    for k in range(-5, 6):
        v = pair_y(pair_z(r3[2 * k] + r3[2 * k + 1], 8), 2)
        b4[k] = inside4(k, 0.5 * v)
    t4 = run_T(b4, range(-4, 5), 16, 4, inside4)
    r4 = run_T(t4, range(-3, 4), 16, 4, inside4)
    u4 = run_T(r4, range(-2, 3), 16, 4)
    e4 = {k: ALPHA * (b4[k] + t4[k] + r4[k] + u4[k]) for k in range(-2, 3)}
    e4 = {k: inside4(k, v) for k, v in e4.items()}

    v3 = {k: ALPHA * t3[k] + e4[k // 2] for k in range(-4, 6)}
    v3 = run_T(v3, range(-3, 5), 8, 2, inside3)
    w3 = run_T(v3, range(-2, 4), 8, 2)
    e3 = {k: inside3(k, w3[k] + ALPHA * (b3[k] + t3[k] + r3[k])) for k in range(-2, 4)}

    v2 = {k: ALPHA * t2[k] + e3[k // 2] for k in range(-4, 8)}
    v2 = run_T(v2, range(-3, 7), 4, 1, inside2)
    w2 = run_T(v2, range(-2, 6), 4, 1)
    e2 = {k: inside2(k, w2[k] + ALPHA * (b2[k] + t2[k] + r2[k])) for k in range(-2, 6)}

    inside1, inside0 = masked(8), masked(16)
    spread = {k: jnp.stack([e2[k // 2]] * 2, axis=0) for k in range(-4, 12)}
    v1 = run_T(spread, range(-2, 10), 2, 1, inside1)
    w1 = run_T(v1, range(-1, 9), 2, 1)
    e1 = {k: inside1(k, w1[k] + base1_ref[k + 1]) for k in range(-1, 9)}

    def prolonged(k):
        v = e1[k // 2]
        return jnp.stack([v[0], v[0], v[1], v[1]], axis=0)

    p1 = Held(p1_ref, -1)
    wide = {k: prolonged(k) for k in range(-2, 18)}
    hold_T(wide, p1, range(-1, 17), 1, inside0)
    for k in range(16):
        v = smooth(p1[k - 1], p1[k], p1[k + 1], 1) + base0_ref[k]
        for q in range(4):
            pot_out[k, pl.ds(q, 8, stride=4), :] = v[q]


def final_part(far, mine, base0, base1):
    vmem = pl.BlockSpec(memory_space=pltpu.VMEM)
    return pl.pallas_call(
        final_kernel,
        out_shape=jax.ShapeDtypeStruct((16, 32, 128), F32),
        in_specs=[vmem] * 4,
        out_specs=vmem,
        scratch_shapes=[
            pltpu.VMEM((64, 8, 128), F32), pltpu.VMEM((54, 8, 128), F32),
            pltpu.VMEM((52, 8, 128), F32), pltpu.VMEM((18, 4, 8, 128), F32),
        ],
        compiler_params=pltpu.CompilerParams(vmem_limit_bytes=32 * 2**20),
        name="final",
    )(far, mine, base0, base1)


def on_device(orbitals, spin_group, occupation, potential_guess):
    applied = guess_part(potential_guess)
    parts = lax.all_to_all(density(spin_group, occupation, orbitals), "band", 0, 0)
    far, *held = far_part(parts, applied)
    rings = [
        [b * DOMS + (first + 8 * (b % 2) + i) % DOMS for i in range(RING)]
        for b in range(BANDS) for first in range(0, DOMS, RING)
    ]
    mine = lax.all_to_all(far, ("band", "dom"), 0, 0, axis_index_groups=rings)

    to_low, to_high, own0, own1, mag = near_part(potential_guess, *held)
    near_low = lax.ppermute(to_high, "dom", [(d, d + 1) for d in range(DOMS - 1)])
    near_high = lax.ppermute(to_low, "dom", [(d + 1, d) for d in range(DOMS - 1)])

    mine, near_low, near_high = lax.optimization_barrier((mine, near_low, near_high))
    other = lax.ppermute(mine, "band", [(b, b ^ 1) for b in range(BANDS)])
    base0, base1, magnetization = edge_part(near_low, near_high, own0, own1, mag)
    return final_part(other, mine, base0, base1), magnetization


def solution(mesh):
    placed = (P("band", "dom", None, None), P("band"), P("band"), P("dom", None, None))
    return jax.shard_map(
        on_device,
        mesh=mesh,
        in_specs=placed,
        out_specs=(P("dom", None, None), P("dom", None, None)),
        check_vma=False,
    )
```

time: 56 us -> 54.7 us (0.977)
  waiting for transfers between devices: 14.6 us -> 13.8 us
    pallas_call x2 -> x5, Pallas kernels: 5.68 us -> 5.53 us  [the longest x1 2.43 us: final_part(): pl.pallas_call(final_kernel, out_shape=jax.ShapeDtypeStruct((16, 32, 128)...]
  transfers between devices with their start and end apart: 5 -> 5, of which waited for: 4 -> 4; matrix products, arithmetic and copies ran while one was open for 0% -> 0% of each run, Pallas kernels for 0% -> 2%
where the time goes in v4:
time: 54.7 us; the launch traced here: 54.3 us
  starting transfers between devices  32.3 us (59%)
  waiting for transfers between devices  13.8 us (25%)
  Pallas kernels  7.55 us (14%)
  between operations  0.69 us (1%)
    all_to_all x1, starting transfers between devices, on_device(): mine = lax.all_to_all(far, ('band', 'dom'), 0, 0, axis_index_groups=rings)  16.3 us
    all_to_all x1, starting transfers between devices, on_device(): lax.all_to_all(density(spin_group, occupation, orbitals), 'band', 0, 0)  10.4 us
    all_to_all x1, waiting for transfers between devices, on_device(): lax.all_to_all(density(spin_group, occupation, orbitals), 'band', 0, 0)  9.29 us
    pallas_call x1, Pallas kernels, final_part(): pl.pallas_call(final_kernel, out_shape=jax.ShapeDtypeStruct((16, 32, 128)...  2.43 us
    ppermute x1, starting transfers between devices, on_device(): lax.ppermute(to_high, 'dom', [(d, d + 1) for d in range(DOMS - 1)])  2.19 us
    ppermute x1, starting transfers between devices, on_device(): other = lax.ppermute(mine, 'band', [(b, b ^ 1) for b in range(BANDS)])  2.13 us
    ppermute x1, waiting for transfers between devices, on_device(): lax.ppermute(to_high, 'dom', [(d, d + 1) for d in range(DOMS - 1)])  2.1 us
    ppermute x1, waiting for transfers between devices, on_device(): lax.ppermute(to_low, 'dom', [(d + 1, d) for d in range(DOMS - 1)])  2.05 us
  transfers between devices with their start and end apart: 5, of which 4 were waited for; matrix products, arithmetic and copies ran while one was open for 0% of the time, Pallas kernels for 2%

profile of v4, /device:TPU:1, one launch (start us, length us, event | category | flops | bytes accessed | tf_op | source)
XLA Modules:
  0.0 54.3 jit_solution(11909773764041234925)
XLA Ops:
  0.6 2.0 %density.1 = f32[8,128,128]{2,1,0:T(8,128)} custom-call(s32[8]{0:T(128)} %spin_hbm.1, s32[8]{0:T(128)} %occ_hbm.1, f32[8,8,16,64]{3,2,1,0:T(8,128)} %orb_hbm.1), custom_call_target="tpu_custom_call" | custom-call | tf_op jit(solution)/shard_map/density/pallas_call | solution.py:245
  2.7 0.0 copy-start
  2.7 10.4 %all-to-all-start = ((f32[8,128,128]{2,1,0:T(8,128)}), f32[8,128,128]{2,1,0:T(8,128)S(1)}, u32[]{:S(2)}, u32[]{:S(2)}) async-start(f32[8,128,128]{2,1,0:T(8,128)} %density.1), calls=%async_computation | async-start | bytes 1048576 | tf_op jit(solution)/shard_map/all_to_all | solution.py:551
  13.1 0.0 copy-done
  13.1 0.2 guess.1.applied_ref
  13.3 9.3 %all-to-all-done.part_ref = f32[8,128,128]{2,1,0:T(8,128)S(1)} async-done(((f32[8,128,128]{2,1,0:T(8,128)}), f32[8,128,128]{2,1,0:T(8,128)S(1)}, u32[]{:S(2)}, u32[]{:S(2)}) %all-to-all-start) | async-done | bytes 524320 | tf_op jit(solution)/shard_map/all_to_all | solution.py:551
  22.6 1.8 %far.1 = (f32[16,16,128]{2,1,0:T(8,128)}, f32[128,128]{1,0:T(8,128)S(1)}, f32[18,4,8,128]{3,2,1,0:T(8,128)S(1)}, f32[20,4,8,128]{3,2,1,0:T(8,128)S(1)}, f32[22,4...) custom-call(f32[8,128,128]{2,1,0:T(8,128)S(1)} %all-to-all-done.part, ...), custom_call_target="tpu_custom_call" | custom-call | tf_op jit(solution)/shard_map/far/pallas_call | solution.py:331
  24.4 16.3 %all-to-all-start.1 = ((f32[16,16,128]{2,1,0:T(8,128)}), f32[16,16,128]{2,1,0:T(8,128)S(1)}, u32[]{:S(2)}, u32[]{:S(2)}) async-start(f32[16,16,128]{2,1,0:T(8,128)} %get-tuple-element.21), calls=%async_computation.1 | async-start | bytes 262144 | tf_op jit(solution)/shard_map/all_to_all | solution.py:557
  40.7 0.3 near.1
  41.0 2.2 %collective-permute-start = (f32[26,8,128]{2,1,0:T(8,128)S(1)}, f32[26,8,128]{2,1,0:T(8,128)S(1)}, u32[]{:S(2)}, u32[]{:S(2)}) collective-permute-start(f32[26,8,128]{2,1,0:T(8,128)S(1)} %get-tuple-element.29), channel_id=1, source_target_pairs={{0,1},{1,2},{2,3},{3,4},{4,5},{5,6},{6,7},{7,8},{8,9},{9,10},{10,1... | collective-permute-start | bytes 319496 | tf_op jit(solution)/shard_map/ppermute | solution.py:560
  43.2 1.3 %collective-permute-start.1 = (f32[26,8,128]{2,1,0:T(8,128)S(1)}, f32[26,8,128]{2,1,0:T(8,128)S(1)}, u32[]{:S(2)}, u32[]{:S(2)}) collective-permute-start(f32[26,8,128]{2,1,0:T(8,128)S(1)} %get-tuple-element.30), channel_id=1, source_target_pairs={{1,0},{2,1},{3,2},{4,3},{5,4},{6,5},{7,6},{8,7},{9,8},{10,9},{11,1... | collective-permute-start | bytes 319496 | tf_op jit(solution)/shard_map/ppermute | solution.py:561
  44.5 2.1 %collective-permute-done.low_ref = f32[26,8,128]{2,1,0:T(8,128)S(1)} collective-permute-done((f32[26,8,128]{2,1,0:T(8,128)S(1)}, f32[26,8,128]{2,1,0:T(8,128)S(1)}, u32[]{:S(2)}, u32[]{:S(2)}) %collective-permute-start) | collective-permute-done | bytes 106528 | tf_op jit(solution)/shard_map/ppermute | solution.py:560
  46.6 2.1 %collective-permute-done.1.high_ref = f32[26,8,128]{2,1,0:T(8,128)S(1)} collective-permute-done((f32[26,8,128]{2,1,0:T(8,128)S(1)}, f32[26,8,128]{2,1,0:T(8,128)S(1)}, u32[]{:S(2)}, u32[]{:S(2)}) %collective-permute-start.1) | collective-permute-done | bytes 106528 | tf_op jit(solution)/shard_map/ppermute | solution.py:561
  48.7 0.0 all-to-all-done.1.mine_ref
  48.7 2.1 %collective-permute-start.2 = (f32[16,16,128]{2,1,0:T(8,128)S(1)}, f32[16,16,128]{2,1,0:T(8,128)S(1)}, u32[]{:S(2)}, u32[]{:S(2)}) collective-permute-start(f32[16,16,128]{2,1,0:T(8,128)S(1)} %all-to-all-done.1.mine_ref), channel_id=1, source_target_pairs={{0,64},{64,0},{128,192},{192,128},{256,320},{320,256},{384,448},{4... | collective-permute-start | bytes 393224 | tf_op jit(solution)/shard_map/ppermute | solution.py:564
  50.8 0.8 %edge.1 = (f32[16,4,8,128]{3,2,1,0:T(8,128)S(1)}, f32[10,2,8,128]{3,2,1,0:T(8,128)S(1)}, f32[16,32,128]{2,1,0:T(8,128)}) custom-call(f32[26,8,128]{2,1,0:T(8,128)S(1)} %collective-permute-done.low_ref, f32[26,8,128]{2,1,0:T(8,128)S(1)} %collective-permute-done.1.high_ref, f32[16,4,8,128]{3,2,1,0:T(8,128)S(1)} %get-tuple-element.34.own0_ref, ...), custom_call_target="tpu_custom_call" | custom-call | tf_op jit(solution)/shard_map/edge/pallas_call | solution.py:430
  51.6 0.3 collective-permute-done.2.far_ref
  51.9 2.4 %final.1 = f32[16,32,128]{2,1,0:T(8,128)} custom-call(f32[16,16,128]{2,1,0:T(8,128)S(1)} %collective-permute-done.2.far_ref, f32[16,16,128]{2,1,0:T(8,128)S(1)} %all-to-all-done.1.mine_ref, f32[16,4,8,128]{3,2,1,0:T(8,128)S(1)} %get-tuple-element.37.base0_ref, f32[10,2,8,128]{3,2,1,0:T(8,128)S(1)} %get-tuple-element.38.base1_ref), custom_call_target="tpu_custom_call" | custom-call | tf_op jit(solution)/shard_map/final/pallas_call | solution.py:535
Async XLA Ops:
  2.7 10.4 %copy-start = (f32[16,32,128]{2,1,0:T(8,128)S(1)}, f32[16,32,128]{2,1,0:T(8,128)}, u32[]{:S(2)}) copy-start(f32[16,32,128]{2,1,0:T(8,128)} %guess_ref.3) | copy-start | bytes 786436
  2.7 19.9 %all-to-all-start = ((f32[8,128,128]{2,1,0:T(8,128)}), f32[8,128,128]{2,1,0:T(8,128)S(1)}, u32[]{:S(2)}, u32[]{:S(2)}) async-start(f32[8,128,128]{2,1,0:T(8,128)} %density.1), calls=%async_computation | async-start | bytes 1048576 | tf_op jit(solution)/shard_map/all_to_all | solution.py:551
  24.4 24.2 %all-to-all-start.1 = ((f32[16,16,128]{2,1,0:T(8,128)}), f32[16,16,128]{2,1,0:T(8,128)S(1)}, u32[]{:S(2)}, u32[]{:S(2)}) async-start(f32[16,16,128]{2,1,0:T(8,128)} %get-tuple-element.21), calls=%async_computation.1 | async-start | bytes 262144 | tf_op jit(solution)/shard_map/all_to_all | solution.py:557
  41.0 5.6 %collective-permute-start = (f32[26,8,128]{2,1,0:T(8,128)S(1)}, f32[26,8,128]{2,1,0:T(8,128)S(1)}, u32[]{:S(2)}, u32[]{:S(2)}) collective-permute-start(f32[26,8,128]{2,1,0:T(8,128)S(1)} %get-tuple-element.29), channel_id=1, source_target_pairs={{0,1},{1,2},{2,3},{3,4},{4,5},{5,6},{6,7},{7,8},{8,9},{9,10},{10,1... | collective-permute-start | bytes 319496 | tf_op jit(solution)/shard_map/ppermute | solution.py:560
  43.2 5.4 %collective-permute-start.1 = (f32[26,8,128]{2,1,0:T(8,128)S(1)}, f32[26,8,128]{2,1,0:T(8,128)S(1)}, u32[]{:S(2)}, u32[]{:S(2)}) collective-permute-start(f32[26,8,128]{2,1,0:T(8,128)S(1)} %get-tuple-element.30), channel_id=1, source_target_pairs={{1,0},{2,1},{3,2},{4,3},{5,4},{6,5},{7,6},{8,7},{9,8},{10,9},{11,1... | collective-permute-start | bytes 319496 | tf_op jit(solution)/shard_map/ppermute | solution.py:561
  48.7 3.2 %collective-permute-start.2 = (f32[16,16,128]{2,1,0:T(8,128)S(1)}, f32[16,16,128]{2,1,0:T(8,128)S(1)}, u32[]{:S(2)}, u32[]{:S(2)}) collective-permute-start(f32[16,16,128]{2,1,0:T(8,128)S(1)} %all-to-all-done.1.mine_ref), channel_id=1, source_target_pairs={{0,64},{64,0},{128,192},{192,128},{256,320},{320,256},{384,448},{4... | collective-permute-start | bytes 393224 | tf_op jit(solution)/shard_map/ppermute | solution.py:564

commit v5 on v4

--- a/solution.py
+++ b/solution.py
@@ -12,6 +12,8 @@
 DOMS = 64
 REACH = 7
 RING = 16
+ROWS = 96
+ROOT = 11
 ALPHA = 1.0 / 9.0
 SOURCE_SCALE = 0.6
 F32 = jnp.float32
@@ -117,15 +119,16 @@
         held.put(k, mask(k, got))
 
 
-def refine_matrix(rows, columns):
-    row = lax.broadcasted_iota(jnp.int32, (rows, columns), 0)
-    col = lax.broadcasted_iota(jnp.int32, (rows, columns), 1)
-    cell, spin = row & 63, row >> 6
-    fine, half = col & 127, col >> 7
-    own = fine >> 1
-    other = jnp.where((fine & 1) == 0, own - 1, own + 1)
-    value = jnp.where(cell == own, 0.75, jnp.where(cell == other, 0.25, 0.0))
-    return jnp.where((spin == 1) & (half == 1), -value, value)
+def refine_z(coarse):
+    row = lax.broadcasted_iota(jnp.int32, (128, 256), 0)
+    col = lax.broadcasted_iota(jnp.int32, (128, 256), 1)
+    own = col >> 1
+    other = jnp.where((col & 1) == 0, own - 1, own + 1)
+    inside = (other >> 6) == (col >> 7)
+    matrix = jnp.where(row == own, 0.75, jnp.where((row == other) & inside, 0.25, 0.0))
+    return jnp.dot(
+        coarse, matrix, precision=lax.Precision.HIGHEST, preferred_element_type=F32
+    )
 
 
 def refine_y(pair):
@@ -150,13 +153,6 @@
             term = factor * coarse[j]
             total = term if total is None else total + term
     return total
-
-
-def refine_z(coarse, columns):
-    return jnp.dot(
-        coarse, refine_matrix(coarse.shape[1], columns),
-        precision=lax.Precision.HIGHEST, preferred_element_type=F32,
-    )
 
 
 def masks(dom):
@@ -234,9 +230,22 @@
             square = orb_ref[k, x] * orb_ref[k, x]
             ups[x] = ups[x] + up * square
             downs[x] = downs[x] + down * square
-    for x in range(8):
-        own_ref[pl.ds(16 * x, 16), :] = jnp.concatenate([ups[x], downs[x]], axis=-1)
-    for copy in copy_all(own_ref, part_hbm, BANDS, sems):
+    for core in range(2):
+        for i in range(4):
+            own_ref[core, pl.ds(16 * i, 16), :] = jnp.concatenate(
+                [ups[i] + downs[i], ups[i + 4] + downs[i + 4]], axis=-1
+            )
+        for i in range(2):
+            one, two = 4 * core + i, 4 * core + i + 2
+            own_ref[core, pl.ds(64 + 16 * i, 16), :] = jnp.concatenate(
+                [ups[one] - downs[one], ups[two] - downs[two]], axis=-1
+            )
+    copies = [
+        pltpu.make_async_copy(own_ref.at[b % 2], part_hbm.at[b], sems.at[b]) for b in range(BANDS)
+    ]
+    for copy in copies:
+        copy.start()
+    for copy in copies:
         copy.wait()
 
 
@@ -244,12 +253,12 @@
     hbm = pl.BlockSpec(memory_space=pltpu.HBM)
     return pl.pallas_call(
         density_kernel,
-        out_shape=jax.ShapeDtypeStruct((BANDS, 128, 128), F32),
+        out_shape=jax.ShapeDtypeStruct((BANDS, ROWS, 128), F32),
         in_specs=[hbm] * 3,
         out_specs=hbm,
         scratch_shapes=[
             pltpu.SMEM((8,), jnp.int32), pltpu.SMEM((8,), jnp.int32),
-            pltpu.VMEM((8, 8, 16, 64), F32), pltpu.VMEM((128, 128), F32),
+            pltpu.VMEM((8, 8, 16, 64), F32), pltpu.VMEM((2, ROWS, 128), F32),
             pltpu.SemaphoreType.DMA((10,)),
         ],
         compiler_params=pltpu.CompilerParams(vmem_limit_bytes=60 * 2**20),
@@ -285,22 +294,24 @@
 
 
 def far_kernel(
-    part_ref, applied_ref, far_hbm, minus_ref, d_ref, t_ref, r_ref, b1_ref, t1_ref, r1_ref,
-    sum_ref, wide_ref, far_ref, sems,
+    part_ref, applied_ref, far_hbm, halo_ref, minus_ref,
+    d_ref, t_ref, r_ref, b1_ref, t1_ref, r1_ref, sum_ref, wide_ref, far_ref, sems,
 ):
     inside0, inside1 = masks(lax.axis_index("dom"))
-    for x in range(8):
-        rows = pl.ds(16 * x, 16)
+    for i in range(ROWS // 16):
+        rows = pl.ds(16 * i, 16)
         total = part_ref[0, rows, :]
         for band in range(1, BANDS):
             total = total + part_ref[band, rows, :]
         sum_ref[rows, :] = total
-    wide = refine_z(sum_ref[...], 256)
-    wide_ref[...] = wide[:, :128]
-    minus_ref[...] = wide[:, 128:]
+    wide = refine_z(sum_ref[...])
+    for half in range(2):
+        wide_ref[half] = wide[:64, 128 * half:128 * half + 128]
+        minus_ref[pl.ds(32 * half, 32), :] = wide[64:, 128 * half:128 * half + 128]
     plus = []
     for x in range(8):
-        pair = [wide_ref[pl.ds(16 * x + p, 8, stride=2), :] for p in range(2)]
+        start = 16 * (x % 4)
+        pair = [wide_ref[x // 4, pl.ds(start + p, 8, stride=2), :] for p in range(2)]
         plus.append(SOURCE_SCALE * refine_y(pair))
     d, t, r = Held(d_ref, -1), Held(t_ref, -2), Held(r_ref, -3)
     for k in range(-1, 17):
@@ -321,7 +332,32 @@
             v = 0.5 * pair_z(v[0] + v[1], 2)
             packed = v if packed is None else jnp.where(lane == p, v, packed)
         far_ref[pl.ds(8 * group, 8), :] = packed
-    for copy in copy_all(far_ref, far_hbm, RING, sems):
+    copies = copy_all(far_ref, far_hbm, RING, sems)
+
+    core = lax.axis_index("band") % 2
+    even = (lanes_of((8, 128)) & 1) == 0
+
+    def edges(first0, first1, plane):
+        for k in range(4):
+            halo_ref[pl.ds(4 * k, 4)] = geometric(d, t, r, first0 + k, 1)
+        for pair in range(3):
+            one = geometric(b1, t1, r1, first1 + 2 * pair, 2)
+            two = geometric(b1, t1, r1, first1 + 2 * pair + 1, 2)
+            for q in range(2):
+                halo_ref[16 + 2 * pair + q] = jnp.where(even, one[q], two[q])
+        start = 32 * (plane // 2) + 16 * (plane % 2)
+        pair = [minus_ref[pl.ds(start + p, 8, stride=2), :] for p in range(2)]
+        halo_ref[pl.ds(22, 4)] = 0.25 * refine_y(pair)
+
+    @pl.when(core == 0)
+    def _():
+        edges(-4, -5, 0)
+
+    @pl.when(core == 1)
+    def _():
+        edges(16, 7, 3)
+
+    for copy in copies:
         copy.wait()
 
 
@@ -331,14 +367,14 @@
     return pl.pallas_call(
         far_kernel,
         out_shape=(
-            shape(RING, 16, 128), shape(128, 128),
+            shape(RING, 16, 128), shape(26, 8, 128), shape(64, 128),
             shape(18, 4, 8, 128), shape(20, 4, 8, 128), shape(22, 4, 8, 128),
             shape(12, 2, 8, 128), shape(14, 2, 8, 128), shape(16, 2, 8, 128),
         ),
         in_specs=[vmem, vmem],
-        out_specs=(pl.BlockSpec(memory_space=pltpu.HBM),) + (vmem,) * 7,
+        out_specs=(pl.BlockSpec(memory_space=pltpu.HBM),) + (vmem,) * 8,
         scratch_shapes=[
-            pltpu.VMEM((128, 128), F32), pltpu.VMEM((128, 128), F32),
+            pltpu.VMEM((ROWS, 128), F32), pltpu.VMEM((2, 64, 128), F32),
             pltpu.VMEM((16, 128), F32), pltpu.SemaphoreType.DMA((RING,)),
         ],
         compiler_params=pltpu.CompilerParams(vmem_limit_bytes=32 * 2**20),
@@ -353,31 +389,15 @@
 
 
 def near_kernel(
-    guess_ref, minus_ref, d_ref, t_ref, r_ref, b1_ref, t1_ref, r1_ref,
-    low_ref, high_ref, own0_ref, own1_ref, mag_ref,
+    guess_ref, d_ref, t_ref, r_ref, b1_ref, t1_ref, r1_ref, own0_ref, own1_ref,
 ):
     d, t, r = Given(d_ref, -1), Given(t_ref, -2), Given(r_ref, -3)
     b1, t1, r1 = Given(b1_ref, -2), Given(t1_ref, -3), Given(r1_ref, -4)
-    minus = []
-    for x in range(8):
-        minus.append(refine_y([minus_ref[pl.ds(16 * x + p, 8, stride=2), :] for p in range(2)]))
     guess = guess_planes(guess_ref)
-    for k in range(4):
-        low_ref[pl.ds(4 * k, 4)] = geometric(d, t, r, k - 4, 1)
-        high_ref[pl.ds(4 * k, 4)] = geometric(d, t, r, k + 16, 1)
-    low_ref[pl.ds(22, 4)] = refine_x(minus, -1)
-    high_ref[pl.ds(22, 4)] = refine_x(minus, 16)
-    f1 = {k: geometric(b1, t1, r1, k, 2) for k in range(-5, 13)}
     for k in range(-1, 9):
-        own1_ref[k + 1] = f1[k]
-    even = (lanes_of((8, 128)) & 1) == 0
-    for pair in range(3):
-        for q in range(2):
-            low_ref[16 + 2 * pair + q] = jnp.where(even, f1[2 * pair - 5][q], f1[2 * pair - 4][q])
-            high_ref[16 + 2 * pair + q] = jnp.where(even, f1[2 * pair + 7][q], f1[2 * pair + 8][q])
+        own1_ref[k + 1] = geometric(b1, t1, r1, k, 2)
     for k in range(16):
         own0_ref[k] = geometric(d, t, r, k, 1) + guess(k)
-        mag_ref[k] = refine_x(minus, k)
 
 
 def near_part(guess, *held):
@@ -385,63 +405,84 @@
     shape = lambda *s: jax.ShapeDtypeStruct(s, F32)
     return pl.pallas_call(
         near_kernel,
-        out_shape=(
-            shape(26, 8, 128), shape(26, 8, 128),
-            shape(16, 4, 8, 128), shape(10, 2, 8, 128), shape(16, 4, 8, 128),
-        ),
-        in_specs=[vmem] * 8,
-        out_specs=(vmem,) * 5,
+        out_shape=(shape(16, 4, 8, 128), shape(10, 2, 8, 128)),
+        in_specs=[vmem] * 7,
+        out_specs=(vmem,) * 2,
         compiler_params=pltpu.CompilerParams(vmem_limit_bytes=32 * 2**20),
         cost_estimate=pl.CostEstimate(flops=10**6, bytes_accessed=2**20, transcendentals=0),
         name="near",
     )(guess, *held)
 
 
-def edge_kernel(low_ref, high_ref, own0_ref, own1_ref, mag_ref, base0_ref, base1_ref, mag_out):
-    even = (lanes_of((8, 128)) & 1) == 0
-    extra = {}
-    for ref, first in ((low_ref, -1), (high_ref, 3)):
-        for pair in range(3):
-            both = [ref[16 + 2 * pair + q] for q in range(2)]
-            one = jnp.stack([jnp.where(even, v, pltpu.roll(v, 1, 1)) for v in both], axis=0)
-            two = jnp.stack([jnp.where(even, pltpu.roll(v, 127, 1), v) for v in both], axis=0)
-            for k, v in ((first + 2 * pair, one), (first + 2 * pair + 1, two)):
-                extra[k] = extra[k] + v if k in extra else v
-    for k in range(-1, 9):
-        base1_ref[k + 1] = own1_ref[k + 1] + extra[k]
+def ring_place():
+    dom, core = lax.axis_index("dom"), lax.axis_index("band") % 2
+    ring, spot = dom // RING, dom % RING
+    aligned = RING * ring
+    shifted = aligned + jnp.where(spot >= RING // 2, RING // 2, -(RING // 2))
+    return dom, core, spot, jnp.where(core == 0, aligned, shifted)
+
+
+def ring_slot(at, core):
+    first = jnp.where(core == 0, ROOT, ROOT - RING // 2)
+    return (at - first + RING) % RING
+
+
+def pack_kernel(mine_ref, halo_ref, minus_ref, out_ref):
+    _, core, spot, _ = ring_place()
+    start = jnp.where((spot < RING // 2) == (core == 0), RING // 2, 0)
+    for i in range(RING // 2):
+        slot = ring_slot(start + i, core)
+        for half in range(2):
+            out_ref[34 + 2 * i + half] = mine_ref[slot, pl.ds(8 * half, 8), :]
+    out_ref[pl.ds(0, 26)] = halo_ref[...]
+    for j in range(4):
+        for p in range(2):
+            out_ref[26 + 2 * j + p] = minus_ref[pl.ds(16 * j + p, 8, stride=2), :]
+
+
+def pack(mine, halo, minus):
+    vmem = pl.BlockSpec(memory_space=pltpu.VMEM)
+    return pl.pallas_call(
+        pack_kernel,
+        out_shape=jax.ShapeDtypeStruct((50, 8, 128), F32),
+        in_specs=[vmem] * 3,
+        out_specs=vmem,
+        compiler_params=pltpu.CompilerParams(vmem_limit_bytes=32 * 2**20),
+        name="pack",
+    )(mine, halo, minus)
+
+
+def final_kernel(
+    mine_ref, swapped_ref, halo_ref, minus_ref, own0_ref, own1_ref, pot_hbm, mag_hbm,
+    b2_ref, t2_ref, r2_ref, p1_ref, pot_ref, mag_ref, sems,
+):
+    dom, core, spot, own_first = ring_place()
+    lower = core == 0
+
+    def high(i):
+        return jnp.where(lower, halo_ref[i], swapped_ref[i])
+
+    def low(i):
+        return jnp.where(lower, swapped_ref[i], halo_ref[i])
+
+    minus = []
+    for x in range(8):
+        j = x % 4
+        pair = []
+        for p in range(2):
+            own = minus_ref[pl.ds(16 * j + p, 8, stride=2), :]
+            pair.append(jnp.where(lower == (x < 4), own, swapped_ref[26 + 2 * j + p]))
+        minus.append(refine_y(pair))
     for k in range(16):
-        v, mag = own0_ref[k], mag_ref[k]
-        if k < 4:
-            v = v + low_ref[pl.ds(4 * k, 4)]
-        if k >= 12:
-            v = v + high_ref[pl.ds(4 * (k - 12), 4)]
-        base0_ref[k] = v
+        mag = refine_x(minus, k)
         if k == 0:
-            mag = mag + low_ref[pl.ds(22, 4)]
+            mag = mag + low(pl.ds(22, 4))
         if k == 15:
-            mag = mag + high_ref[pl.ds(22, 4)]
+            mag = mag + high(pl.ds(22, 4))
         for q in range(4):
-            mag_out[k, pl.ds(q, 8, stride=4), :] = mag[q]
-
-
-def edge_part(low, high, own0, own1, mag):
-    vmem = pl.BlockSpec(memory_space=pltpu.VMEM)
-    shape = lambda *s: jax.ShapeDtypeStruct(s, F32)
-    return pl.pallas_call(
-        edge_kernel,
-        out_shape=(shape(16, 4, 8, 128), shape(10, 2, 8, 128), shape(16, 32, 128)),
-        in_specs=[vmem] * 5,
-        out_specs=(vmem,) * 3,
-        compiler_params=pltpu.CompilerParams(vmem_limit_bytes=32 * 2**20),
-        name="edge",
-    )(low, high, own0, own1, mag)
-
-
-def final_kernel(
-    far_ref, mine_ref, base0_ref, base1_ref, pot_out,
-    b2_ref, t2_ref, r2_ref, p1_ref,
-):
-    dom = lax.axis_index("dom")
+            mag_ref[k, pl.ds(q, 8, stride=4), :] = mag[q]
+    copies = [pltpu.make_async_copy(mag_ref, mag_hbm, sems.at[4])]
+    copies[0].start()
 
     def masked(count):
         first, last = -dom * count, (DOMS - dom) * count
@@ -453,19 +494,20 @@
         return mask
 
     lane = lanes_of((8, 128)) & 3
-    core = lax.axis_index("band") % 2
-    ring, spot = dom // RING, dom % RING
-    even_first = RING * ring
-    odd_first = even_first + jnp.where(spot >= RING // 2, RING // 2, -(RING // 2))
+    aligned = dom - spot
+    swapped_first = aligned + jnp.where(
+        spot < RING // 2, jnp.where(lower, -(RING // 2), RING // 2), jnp.where(lower, RING, 0)
+    )
 
     def vector(i, half):
         wanted = dom - REACH + i
-        at = wanted - even_first
-        in_even = (at >= 0) & (at < RING)
-        at = jnp.clip(jnp.where(in_even, at, wanted - odd_first), 0, RING - 1)
-        rows = pl.ds(8 * half, 8)
-        held = in_even == (core == 0)
-        v = jnp.where(held, mine_ref[at, rows, :], far_ref[at, rows, :])
+        at = wanted - own_first
+        held = (at >= 0) & (at < RING)
+        slot = ring_slot(jnp.clip(at, 0, RING - 1), core)
+        extra = jnp.clip(wanted - swapped_first, 0, RING // 2 - 1)
+        v = jnp.where(
+            held, mine_ref[slot, pl.ds(8 * half, 8), :], swapped_ref[34 + 2 * extra + half]
+        )
         return jnp.where((wanted >= 0) & (wanted < DOMS), v, 0.0)
 
     b2, t2, r2 = Held(b2_ref, -30), Held(t2_ref, -25), Held(r2_ref, -24)
@@ -515,7 +557,15 @@
     spread = {k: jnp.stack([e2[k // 2]] * 2, axis=0) for k in range(-4, 12)}
     v1 = run_T(spread, range(-2, 10), 2, 1, inside1)
     w1 = run_T(v1, range(-1, 9), 2, 1)
-    e1 = {k: inside1(k, w1[k] + base1_ref[k + 1]) for k in range(-1, 9)}
+    even = (lanes_of((8, 128)) & 1) == 0
+    for side, first in ((low, -1), (high, 3)):
+        for pair in range(3):
+            both = [side(16 + 2 * pair + q) for q in range(2)]
+            one = jnp.stack([jnp.where(even, v, pltpu.roll(v, 1, 1)) for v in both], axis=0)
+            two = jnp.stack([jnp.where(even, pltpu.roll(v, 127, 1), v) for v in both], axis=0)
+            for k, v in ((first + 2 * pair, one), (first + 2 * pair + 1, two)):
+                w1[k] = w1[k] + v
+    e1 = {k: inside1(k, w1[k] + own1_ref[k + 1]) for k in range(-1, 9)}
 
     def prolonged(k):
         v = e1[k // 2]
@@ -525,45 +575,62 @@
     wide = {k: prolonged(k) for k in range(-2, 18)}
     hold_T(wide, p1, range(-1, 17), 1, inside0)
     for k in range(16):
-        v = smooth(p1[k - 1], p1[k], p1[k + 1], 1) + base0_ref[k]
+        v = smooth(p1[k - 1], p1[k], p1[k + 1], 1) + own0_ref[k]
+        if k < 4:
+            v = v + low(pl.ds(4 * k, 4))
+        if k >= 12:
+            v = v + high(pl.ds(4 * (k - 12), 4))
         for q in range(4):
-            pot_out[k, pl.ds(q, 8, stride=4), :] = v[q]
-
-
-def final_part(far, mine, base0, base1):
+            pot_ref[k, pl.ds(q, 8, stride=4), :] = v[q]
+        if k % 4 == 3:
+            part = pl.ds(k - 3, 4)
+            copies.append(pltpu.make_async_copy(pot_ref.at[part], pot_hbm.at[part], sems.at[k // 4]))
+            copies[-1].start()
+    for copy in copies:
+        copy.wait()
+
+
+def final_part(*operands):
     vmem = pl.BlockSpec(memory_space=pltpu.VMEM)
+    hbm = pl.BlockSpec(memory_space=pltpu.HBM)
+    shape = lambda *s: jax.ShapeDtypeStruct(s, F32)
     return pl.pallas_call(
         final_kernel,
-        out_shape=jax.ShapeDtypeStruct((16, 32, 128), F32),
-        in_specs=[vmem] * 4,
-        out_specs=vmem,
+        out_shape=(shape(16, 32, 128), shape(16, 32, 128)),
+        in_specs=[vmem] * 6,
+        out_specs=(hbm, hbm),
         scratch_shapes=[
             pltpu.VMEM((64, 8, 128), F32), pltpu.VMEM((54, 8, 128), F32),
             pltpu.VMEM((52, 8, 128), F32), pltpu.VMEM((18, 4, 8, 128), F32),
+            pltpu.VMEM((16, 32, 128), F32), pltpu.VMEM((16, 32, 128), F32),
+            pltpu.SemaphoreType.DMA((5,)),
         ],
         compiler_params=pltpu.CompilerParams(vmem_limit_bytes=32 * 2**20),
         name="final",
-    )(far, mine, base0, base1)
+    )(*operands)
 
 
 def on_device(orbitals, spin_group, occupation, potential_guess):
     applied = guess_part(potential_guess)
     parts = lax.all_to_all(density(spin_group, occupation, orbitals), "band", 0, 0)
-    far, *held = far_part(parts, applied)
+    far, to_send, minus, *held = far_part(parts, applied)
     rings = [
-        [b * DOMS + (first + 8 * (b % 2) + i) % DOMS for i in range(RING)]
+        [
+            b * DOMS + (first + 8 * (b % 2) + (ROOT - 8 * (b % 2) + i) % RING) % DOMS
+            for i in range(RING)
+        ]
         for b in range(BANDS) for first in range(0, DOMS, RING)
     ]
     mine = lax.all_to_all(far, ("band", "dom"), 0, 0, axis_index_groups=rings)
 
-    to_low, to_high, own0, own1, mag = near_part(potential_guess, *held)
-    near_low = lax.ppermute(to_high, "dom", [(d, d + 1) for d in range(DOMS - 1)])
-    near_high = lax.ppermute(to_low, "dom", [(d + 1, d) for d in range(DOMS - 1)])
-
-    mine, near_low, near_high = lax.optimization_barrier((mine, near_low, near_high))
-    other = lax.ppermute(mine, "band", [(b, b ^ 1) for b in range(BANDS)])
-    base0, base1, magnetization = edge_part(near_low, near_high, own0, own1, mag)
-    return final_part(other, mine, base0, base1), magnetization
+    edges = [
+        (b * DOMS + d + 1 - b % 2, b * DOMS + d + b % 2) for b in range(BANDS) for d in range(DOMS - 1)
+    ]
+    halo = lax.ppermute(to_send, ("band", "dom"), edges)
+    own0, own1 = near_part(potential_guess, *held)
+    swap = [(b, b ^ 1) for b in range(BANDS)]
+    swapped = lax.ppermute(pack(mine, halo, minus), "band", swap)
+    return final_part(mine, swapped, halo, minus, own0, own1)
 
 
 def solution(mesh):

time: 54.7 us -> 51.7 us (0.945)
  starting transfers between devices: 32.3 us -> 29.4 us
  Pallas kernels: 7.55 us -> 6.86 us
    all_to_all x1, waiting for transfers between devices: 0.01 us -> 3.4 us  [on_device(): mine = lax.all_to_all(far, ('band', 'dom'), 0, 0, axis_index_groups=rings)]
    all_to_all x1, starting transfers between devices: 16.3 us -> 13.6 us  [on_device(): mine = lax.all_to_all(far, ('band', 'dom'), 0, 0, axis_index_groups=rings)]
    ppermute x3 -> x2, waiting for transfers between devices: 4.49 us -> 3.06 us  [the longest x1 2.26 us: on_device(): halo = lax.ppermute(to_send, ('band', 'dom'), edges)]
    all_to_all x1, waiting for transfers between devices: 9.29 us -> 7.89 us  [on_device(): lax.all_to_all(density(spin_group, occupation, orbitals), 'band', 0, 0)]
    pallas_call x5, Pallas kernels: 7.35 us -> 6.66 us  [the longest x1 2.58 us: final_part(): pl.pallas_call(final_kernel, out_shape=(shape(16, 32, 128), shape(16, 32,...]
    ppermute x3 -> x2, starting transfers between devices: 5.62 us -> 5.43 us  [the longest x1 3.08 us: on_device(): halo = lax.ppermute(to_send, ('band', 'dom'), edges)]
  transfers between devices with their start and end apart: 5 -> 4, of which waited for: 4 -> 4; matrix products, arithmetic and copies ran while one was open for 0% -> 0% of each run, Pallas kernels for 2% -> 1%
where the time goes in v5:
time: 51.7 us; the launch traced here: 51.3 us
  starting transfers between devices  29.4 us (57%)
  waiting for transfers between devices  14.3 us (28%)
  Pallas kernels  6.86 us (13%)
  between operations  0.69 us (1%)
    all_to_all x1, starting transfers between devices, on_device(): mine = lax.all_to_all(far, ('band', 'dom'), 0, 0, axis_index_groups=rings)  13.6 us
    all_to_all x1, starting transfers between devices, on_device(): lax.all_to_all(density(spin_group, occupation, orbitals), 'band', 0, 0)  10.4 us
    all_to_all x1, waiting for transfers between devices, on_device(): lax.all_to_all(density(spin_group, occupation, orbitals), 'band', 0, 0)  7.89 us
    all_to_all x1, waiting for transfers between devices, on_device(): mine = lax.all_to_all(far, ('band', 'dom'), 0, 0, axis_index_groups=rings)  3.4 us
    ppermute x1, starting transfers between devices, on_device(): halo = lax.ppermute(to_send, ('band', 'dom'), edges)  3.08 us
    pallas_call x1, Pallas kernels, final_part(): pl.pallas_call(final_kernel, out_shape=(shape(16, 32, 128), shape(16, 32,...  2.58 us
    ppermute x1, starting transfers between devices, on_device(): swapped = lax.ppermute(pack(mine, halo, minus), 'band', swap)  2.35 us
    ppermute x1, waiting for transfers between devices, on_device(): halo = lax.ppermute(to_send, ('band', 'dom'), edges)  2.26 us
  transfers between devices with their start and end apart: 4, of which 4 were waited for; matrix products, arithmetic and copies ran while one was open for 0% of the time, Pallas kernels for 1%

profile of v5, /device:TPU:1, one launch (start us, length us, event | category | flops | bytes accessed | tf_op | source)
XLA Modules:
  0.0 51.3 jit_solution(16351545392591922582)
XLA Ops:
  0.6 2.0 %density.1 = f32[8,96,128]{2,1,0:T(8,128)} custom-call(s32[8]{0:T(128)} %spin_hbm.1, s32[8]{0:T(128)} %occ_hbm.1, f32[8,8,16,64]{3,2,1,0:T(8,128)} %orb_hbm.1), custom_call_target="tpu_custom_call" | custom-call | tf_op jit(solution)/shard_map/density/pallas_call | solution.py:254
  2.6 0.0 copy-start
  2.6 10.4 %all-to-all-start = ((f32[8,96,128]{2,1,0:T(8,128)}), f32[8,96,128]{2,1,0:T(8,128)S(1)}, u32[]{:S(2)}, u32[]{:S(2)}) async-start(f32[8,96,128]{2,1,0:T(8,128)} %density.1), calls=%async_computation | async-start | bytes 786432 | tf_op jit(solution)/shard_map/all_to_all | solution.py:615
  13.0 0.0 copy-done
  13.0 0.2 guess.1.applied_ref
  13.2 7.9 %all-to-all-done.part_ref = f32[8,96,128]{2,1,0:T(8,128)S(1)} async-done(((f32[8,96,128]{2,1,0:T(8,128)}), f32[8,96,128]{2,1,0:T(8,128)S(1)}, u32[]{:S(2)}, u32[]{:S(2)}) %all-to-all-start) | async-done | bytes 393248 | tf_op jit(solution)/shard_map/all_to_all | solution.py:615
  21.1 1.8 %far.1 = (f32[16,16,128]{2,1,0:T(8,128)}, f32[26,8,128]{2,1,0:T(8,128)S(1)}, f32[64,128]{1,0:T(8,128)S(1)}, f32[18,4,8,128]{3,2,1,0:T(8,128)S(1)}, f32[20,4,8,12...) custom-call(f32[8,96,128]{2,1,0:T(8,128)S(1)} %all-to-all-done.part_, ...), custom_call_target="tpu_custom_call" | custom-call | tf_op jit(solution)/shard_map/far/pallas_call | solution.py:367
  22.9 13.6 %all-to-all-start.1 = ((f32[16,16,128]{2,1,0:T(8,128)}), f32[16,16,128]{2,1,0:T(8,128)S(1)}, u32[]{:S(2)}, u32[]{:S(2)}) async-start(f32[16,16,128]{2,1,0:T(8,128)} %get-tuple-element.13), calls=%async_computation.1 | async-start | bytes 262144 | tf_op jit(solution)/shard_map/all_to_all | solution.py:624
  36.5 3.1 %collective-permute-start = (f32[26,8,128]{2,1,0:T(8,128)S(1)}, f32[26,8,128]{2,1,0:T(8,128)S(1)}, u32[]{:S(2)}, u32[]{:S(2)}) collective-permute-start(f32[26,8,128]{2,1,0:T(8,128)S(1)} %get-tuple-element.14), channel_id=1, source_target_pairs={{1,0},{2,1},{3,2},{4,3},{5,4},{6,5},{7,6},{8,7},{9,8},{10,9},{11,1... | collective-permute-start | bytes 319496 | tf_op jit(solution)/shard_map/ppermute | solution.py:629
  39.6 2.3 %collective-permute-done.halo_ref = f32[26,8,128]{2,1,0:T(8,128)S(1)} collective-permute-done((f32[26,8,128]{2,1,0:T(8,128)S(1)}, f32[26,8,128]{2,1,0:T(8,128)S(1)}, u32[]{:S(2)}, u32[]{:S(2)}) %collective-permute-start) | collective-permute-done | bytes 106528 | tf_op jit(solution)/shard_map/ppermute | solution.py:629
  41.9 3.4 %all-to-all-done.1.mine_ref = f32[16,16,128]{2,1,0:T(8,128)S(1)} async-done(((f32[16,16,128]{2,1,0:T(8,128)}), f32[16,16,128]{2,1,0:T(8,128)S(1)}, u32[]{:S(2)}, u32[]{:S(2)}) %all-to-all-start.1) | async-done | bytes 131104 | tf_op jit(solution)/shard_map/all_to_all | solution.py:624
  45.3 2.4 %collective-permute-start.1 = (f32[50,8,128]{2,1,0:T(8,128)S(1)}, f32[50,8,128]{2,1,0:T(8,128)S(1)}, u32[]{:S(2)}, u32[]{:S(2)}) collective-permute-start(f32[50,8,128]{2,1,0:T(8,128)S(1)} %pack.1), channel_id=1, source_target_pairs={{0,64},{64,0},{128,192},{192,128},{256,320},{320,256},{384,448},{4... | collective-permute-start | bytes 614408 | tf_op jit(solution)/shard_map/ppermute | solution.py:632
  47.7 0.3 near.1
  47.9 0.8 %collective-permute-done.1.swapped_ref = f32[50,8,128]{2,1,0:T(8,128)S(1)} collective-permute-done((f32[50,8,128]{2,1,0:T(8,128)S(1)}, f32[50,8,128]{2,1,0:T(8,128)S(1)}, u32[]{:S(2)}, u32[]{:S(2)}) %collective-permute-start.1) | collective-permute-done | bytes 204832 | tf_op jit(solution)/shard_map/ppermute | solution.py:632
  48.7 2.6 %final.1 = (f32[16,32,128]{2,1,0:T(8,128)}, f32[16,32,128]{2,1,0:T(8,128)}) custom-call(f32[16,16,128]{2,1,0:T(8,128)S(1)} %all-to-all-done.1.mine_ref, f32[50,8,128]{2,1,0:T(8,128)S(1)} %collective-permute-done.1.swapped_ref, f32[26,8,128]{2,1,0:T(8,128)S(1)} %collective-permute-done.halo_ref, f32[64,128]{1,0:T(8,128)S(1)} %get-tuple-element.15.minus_ref, ...), custom_call_target="tpu_custom_call" | custom-call | tf_op jit(solution)/shard_map/final/pallas_call | solution.py:597
  (1 shorter events, 0.0 us)
Async XLA Ops:
  2.6 10.4 %copy-start = (f32[16,32,128]{2,1,0:T(8,128)S(1)}, f32[16,32,128]{2,1,0:T(8,128)}, u32[]{:S(2)}) copy-start(f32[16,32,128]{2,1,0:T(8,128)} %guess_ref.3) | copy-start | bytes 786436
  2.6 18.5 %all-to-all-start = ((f32[8,96,128]{2,1,0:T(8,128)}), f32[8,96,128]{2,1,0:T(8,128)S(1)}, u32[]{:S(2)}, u32[]{:S(2)}) async-start(f32[8,96,128]{2,1,0:T(8,128)} %density.1), calls=%async_computation | async-start | bytes 786432 | tf_op jit(solution)/shard_map/all_to_all | solution.py:615
  22.9 22.4 %all-to-all-start.1 = ((f32[16,16,128]{2,1,0:T(8,128)}), f32[16,16,128]{2,1,0:T(8,128)S(1)}, u32[]{:S(2)}, u32[]{:S(2)}) async-start(f32[16,16,128]{2,1,0:T(8,128)} %get-tuple-element.13), calls=%async_computation.1 | async-start | bytes 262144 | tf_op jit(solution)/shard_map/all_to_all | solution.py:624
  36.5 5.4 %collective-permute-start = (f32[26,8,128]{2,1,0:T(8,128)S(1)}, f32[26,8,128]{2,1,0:T(8,128)S(1)}, u32[]{:S(2)}, u32[]{:S(2)}) collective-permute-start(f32[26,8,128]{2,1,0:T(8,128)S(1)} %get-tuple-element.14), channel_id=1, source_target_pairs={{1,0},{2,1},{3,2},{4,3},{5,4},{6,5},{7,6},{8,7},{9,8},{10,9},{11,1... | collective-permute-start | bytes 319496 | tf_op jit(solution)/shard_map/ppermute | solution.py:629
  45.3 3.4 %collective-permute-start.1 = (f32[50,8,128]{2,1,0:T(8,128)S(1)}, f32[50,8,128]{2,1,0:T(8,128)S(1)}, u32[]{:S(2)}, u32[]{:S(2)}) collective-permute-start(f32[50,8,128]{2,1,0:T(8,128)S(1)} %pack.1), channel_id=1, source_target_pairs={{0,64},{64,0},{128,192},{192,128},{256,320},{320,256},{384,448},{4... | collective-permute-start | bytes 614408 | tf_op jit(solution)/shard_map/ppermute | solution.py:632

commit v6 on v5

--- a/solution.py
+++ b/solution.py
@@ -209,7 +209,7 @@
 
 
 def density_kernel(
-    spin_hbm, occ_hbm, orb_hbm, part_hbm, spin_ref, occ_ref, orb_ref, own_ref, sems,
+    spin_hbm, occ_hbm, orb_hbm, part_ref, spin_ref, occ_ref, orb_ref, plane_ref, sems,
 ):
     loads = [
         pltpu.make_async_copy(spin_hbm, spin_ref, sems.at[8]),
@@ -230,23 +230,21 @@
             square = orb_ref[k, x] * orb_ref[k, x]
             ups[x] = ups[x] + up * square
             downs[x] = downs[x] + down * square
-    for core in range(2):
-        for i in range(4):
-            own_ref[core, pl.ds(16 * i, 16), :] = jnp.concatenate(
-                [ups[i] + downs[i], ups[i + 4] + downs[i + 4]], axis=-1
-            )
-        for i in range(2):
-            one, two = 4 * core + i, 4 * core + i + 2
-            own_ref[core, pl.ds(64 + 16 * i, 16), :] = jnp.concatenate(
-                [ups[one] - downs[one], ups[two] - downs[two]], axis=-1
-            )
-    copies = [
-        pltpu.make_async_copy(own_ref.at[b % 2], part_hbm.at[b], sems.at[b]) for b in range(BANDS)
-    ]
-    for copy in copies:
-        copy.start()
-    for copy in copies:
-        copy.wait()
+    for x in range(8):
+        plane_ref[x] = ups[x] + downs[x]
+        plane_ref[8 + x] = ups[x] - downs[x]
+
+    def halves(plane):
+        return jnp.concatenate(
+            [plane_ref[plane, pl.ds(p, 8, stride=2), :] for p in range(2)], axis=-1
+        )
+
+    for x in range(8):
+        total, difference = halves(x), halves(8 + x)
+        for b in range(BANDS):
+            part_ref[b, pl.ds(8 * x, 8), :] = total
+            if b % 2 == x // 4:
+                part_ref[b, pl.ds(64 + 8 * (x % 4), 8), :] = difference
 
 
 def density(spin_group, occupation, orbitals):
@@ -255,19 +253,38 @@
         density_kernel,
         out_shape=jax.ShapeDtypeStruct((BANDS, ROWS, 128), F32),
         in_specs=[hbm] * 3,
-        out_specs=hbm,
+        out_specs=pl.BlockSpec(memory_space=pltpu.VMEM),
         scratch_shapes=[
             pltpu.SMEM((8,), jnp.int32), pltpu.SMEM((8,), jnp.int32),
-            pltpu.VMEM((8, 8, 16, 64), F32), pltpu.VMEM((2, ROWS, 128), F32),
+            pltpu.VMEM((8, 8, 16, 64), F32), pltpu.VMEM((16, 16, 64), F32),
             pltpu.SemaphoreType.DMA((10,)),
         ],
-        compiler_params=pltpu.CompilerParams(vmem_limit_bytes=60 * 2**20),
+        compiler_params=pltpu.CompilerParams(vmem_limit_bytes=57 * 2**20),
         name="density",
     )(spin_group, occupation, orbitals)
 
 
-def guess_kernel(guess_ref, out_ref):
-    inside0, _ = masks(lax.axis_index("dom"))
+def plane_pair(wide, plane):
+    rows = wide[8 * plane:8 * plane + 8]
+    return rows[:, :128], rows[:, 128:]
+
+
+def far_kernel(
+    part_ref, guess_ref, far_hbm, halo_ref, minus_ref,
+    d_ref, t_ref, r_ref, b1_ref, t1_ref, r1_ref, sum_ref, far_ref, sems,
+):
+    inside0, inside1 = masks(lax.axis_index("dom"))
+    for i in range(ROWS // 16):
+        rows = pl.ds(16 * i, 16)
+        total = part_ref[0, rows, :]
+        for band in range(1, BANDS):
+            total = total + part_ref[band, rows, :]
+        sum_ref[rows, :] = total
+    wide = refine_z(sum_ref[...])
+    plus = [SOURCE_SCALE * refine_y(plane_pair(wide, x)) for x in range(8)]
+    for j in range(4):
+        minus_ref[2 * j], minus_ref[2 * j + 1] = plane_pair(wide, 8 + j)
+    d, t, r = Held(d_ref, -1), Held(t_ref, -2), Held(r_ref, -3)
     guess = guess_planes(guess_ref)
     for k in range(-1, 17):
         v, low, high = guess(k), guess(k - 1), guess(k + 1)
@@ -277,45 +294,9 @@
         for side in (low, high):
             if side is not None:
                 around = side if around is None else around + side
-        out_ref[k + 1] = inside0(k, around - 6.0 * v if v is not None else around)
-
-
-def guess_part(guess):
-    vmem = pl.BlockSpec(memory_space=pltpu.VMEM)
-    return pl.pallas_call(
-        guess_kernel,
-        out_shape=jax.ShapeDtypeStruct((18, 4, 8, 128), F32),
-        in_specs=[vmem],
-        out_specs=vmem,
-        compiler_params=pltpu.CompilerParams(vmem_limit_bytes=32 * 2**20),
-        cost_estimate=pl.CostEstimate(flops=10**6, bytes_accessed=2**19, transcendentals=0),
-        name="guess",
-    )(guess)
-
-
-def far_kernel(
-    part_ref, applied_ref, far_hbm, halo_ref, minus_ref,
-    d_ref, t_ref, r_ref, b1_ref, t1_ref, r1_ref, sum_ref, wide_ref, far_ref, sems,
-):
-    inside0, inside1 = masks(lax.axis_index("dom"))
-    for i in range(ROWS // 16):
-        rows = pl.ds(16 * i, 16)
-        total = part_ref[0, rows, :]
-        for band in range(1, BANDS):
-            total = total + part_ref[band, rows, :]
-        sum_ref[rows, :] = total
-    wide = refine_z(sum_ref[...])
-    for half in range(2):
-        wide_ref[half] = wide[:64, 128 * half:128 * half + 128]
-        minus_ref[pl.ds(32 * half, 32), :] = wide[64:, 128 * half:128 * half + 128]
-    plus = []
-    for x in range(8):
-        start = 16 * (x % 4)
-        pair = [wide_ref[x // 4, pl.ds(start + p, 8, stride=2), :] for p in range(2)]
-        plus.append(SOURCE_SCALE * refine_y(pair))
-    d, t, r = Held(d_ref, -1), Held(t_ref, -2), Held(r_ref, -3)
-    for k in range(-1, 17):
-        d.put(k, inside0(k, refine_x(plus, k)) + applied_ref[k + 1])
+        if v is not None:
+            around = around - 6.0 * v
+        d.put(k, inside0(k, refine_x(plus, k) + around))
     hold_T(d, t, range(-2, 18), 1, inside0)
     hold_T(t, r, range(-3, 19), 1, inside0)
     b1, t1, r1 = Held(b1_ref, -2), Held(t1_ref, -3), Held(r1_ref, -4)
@@ -345,9 +326,7 @@
             two = geometric(b1, t1, r1, first1 + 2 * pair + 1, 2)
             for q in range(2):
                 halo_ref[16 + 2 * pair + q] = jnp.where(even, one[q], two[q])
-        start = 32 * (plane // 2) + 16 * (plane % 2)
-        pair = [minus_ref[pl.ds(start + p, 8, stride=2), :] for p in range(2)]
-        halo_ref[pl.ds(22, 4)] = 0.25 * refine_y(pair)
+        halo_ref[pl.ds(22, 4)] = 0.25 * refine_y((minus_ref[2 * plane], minus_ref[2 * plane + 1]))
 
     @pl.when(core == 0)
     def _():
@@ -361,25 +340,24 @@
         copy.wait()
 
 
-def far_part(parts, applied):
+def far_part(parts, guess):
     vmem = pl.BlockSpec(memory_space=pltpu.VMEM)
     shape = lambda *s: jax.ShapeDtypeStruct(s, F32)
     return pl.pallas_call(
         far_kernel,
         out_shape=(
-            shape(RING, 16, 128), shape(26, 8, 128), shape(64, 128),
+            shape(RING, 16, 128), shape(26, 8, 128), shape(8, 8, 128),
             shape(18, 4, 8, 128), shape(20, 4, 8, 128), shape(22, 4, 8, 128),
             shape(12, 2, 8, 128), shape(14, 2, 8, 128), shape(16, 2, 8, 128),
         ),
         in_specs=[vmem, vmem],
         out_specs=(pl.BlockSpec(memory_space=pltpu.HBM),) + (vmem,) * 8,
         scratch_shapes=[
-            pltpu.VMEM((ROWS, 128), F32), pltpu.VMEM((2, 64, 128), F32),
-            pltpu.VMEM((16, 128), F32), pltpu.SemaphoreType.DMA((RING,)),
+            pltpu.VMEM((ROWS, 128), F32), pltpu.VMEM((16, 128), F32), pltpu.SemaphoreType.DMA((RING,)),
         ],
         compiler_params=pltpu.CompilerParams(vmem_limit_bytes=32 * 2**20),
         name="far",
-    )(parts, applied)
+    )(parts, guess)
 
 
 class Given(Held):
@@ -414,37 +392,19 @@
     )(guess, *held)
 
 
-def ring_place():
-    dom, core = lax.axis_index("dom"), lax.axis_index("band") % 2
-    ring, spot = dom // RING, dom % RING
-    aligned = RING * ring
-    shifted = aligned + jnp.where(spot >= RING // 2, RING // 2, -(RING // 2))
-    return dom, core, spot, jnp.where(core == 0, aligned, shifted)
-
-
-def ring_slot(at, core):
-    first = jnp.where(core == 0, ROOT, ROOT - RING // 2)
-    return (at - first + RING) % RING
-
-
 def pack_kernel(mine_ref, halo_ref, minus_ref, out_ref):
-    _, core, spot, _ = ring_place()
-    start = jnp.where((spot < RING // 2) == (core == 0), RING // 2, 0)
-    for i in range(RING // 2):
-        slot = ring_slot(start + i, core)
+    out_ref[pl.ds(0, 26)] = halo_ref[...]
+    out_ref[pl.ds(26, 8)] = minus_ref[...]
+    for i in range(RING):
         for half in range(2):
-            out_ref[34 + 2 * i + half] = mine_ref[slot, pl.ds(8 * half, 8), :]
-    out_ref[pl.ds(0, 26)] = halo_ref[...]
-    for j in range(4):
-        for p in range(2):
-            out_ref[26 + 2 * j + p] = minus_ref[pl.ds(16 * j + p, 8, stride=2), :]
+            out_ref[34 + 2 * i + half] = mine_ref[i, pl.ds(8 * half, 8), :]
 
 
 def pack(mine, halo, minus):
     vmem = pl.BlockSpec(memory_space=pltpu.VMEM)
     return pl.pallas_call(
         pack_kernel,
-        out_shape=jax.ShapeDtypeStruct((50, 8, 128), F32),
+        out_shape=jax.ShapeDtypeStruct((66, 8, 128), F32),
         in_specs=[vmem] * 3,
         out_specs=vmem,
         compiler_params=pltpu.CompilerParams(vmem_limit_bytes=32 * 2**20),
@@ -456,8 +416,8 @@
     mine_ref, swapped_ref, halo_ref, minus_ref, own0_ref, own1_ref, pot_hbm, mag_hbm,
     b2_ref, t2_ref, r2_ref, p1_ref, pot_ref, mag_ref, sems,
 ):
-    dom, core, spot, own_first = ring_place()
-    lower = core == 0
+    dom = lax.axis_index("dom")
+    lower = lax.axis_index("band") % 2 == 0
 
     def high(i):
         return jnp.where(lower, halo_ref[i], swapped_ref[i])
@@ -470,7 +430,7 @@
         j = x % 4
         pair = []
         for p in range(2):
-            own = minus_ref[pl.ds(16 * j + p, 8, stride=2), :]
+            own = minus_ref[2 * j + p]
             pair.append(jnp.where(lower == (x < 4), own, swapped_ref[26 + 2 * j + p]))
         minus.append(refine_y(pair))
     for k in range(16):
@@ -494,19 +454,18 @@
         return mask
 
     lane = lanes_of((8, 128)) & 3
-    aligned = dom - spot
-    swapped_first = aligned + jnp.where(
-        spot < RING // 2, jnp.where(lower, -(RING // 2), RING // 2), jnp.where(lower, RING, 0)
-    )
+    spot = dom % RING
+    first = dom - spot
+    other_first = first + jnp.where(spot < RING // 2, -(RING // 2), RING // 2)
 
     def vector(i, half):
         wanted = dom - REACH + i
-        at = wanted - own_first
-        held = (at >= 0) & (at < RING)
-        slot = ring_slot(jnp.clip(at, 0, RING - 1), core)
-        extra = jnp.clip(wanted - swapped_first, 0, RING // 2 - 1)
+        at = wanted - first
+        aligned = (at >= 0) & (at < RING)
+        at = jnp.clip(jnp.where(aligned, at, wanted - other_first), 0, RING - 1)
+        slot = (at + RING - jnp.where(aligned, ROOT, ROOT - RING // 2)) % RING
         v = jnp.where(
-            held, mine_ref[slot, pl.ds(8 * half, 8), :], swapped_ref[34 + 2 * extra + half]
+            aligned == lower, mine_ref[slot, pl.ds(8 * half, 8), :], swapped_ref[34 + 2 * slot + half]
         )
         return jnp.where((wanted >= 0) & (wanted < DOMS), v, 0.0)
 
@@ -611,16 +570,15 @@
 
 
 def on_device(orbitals, spin_group, occupation, potential_guess):
-    applied = guess_part(potential_guess)
     parts = lax.all_to_all(density(spin_group, occupation, orbitals), "band", 0, 0)
-    far, to_send, minus, *held = far_part(parts, applied)
-    rings = [
-        [
-            b * DOMS + (first + 8 * (b % 2) + (ROOT - 8 * (b % 2) + i) % RING) % DOMS
-            for i in range(RING)
-        ]
-        for b in range(BANDS) for first in range(0, DOMS, RING)
-    ]
+    far, to_send, minus, *held = far_part(parts, potential_guess)
+    rings = []
+    for b in range(BANDS):
+        half = RING // 2 * (b % 2)
+        for first in range(half, DOMS - half, RING):
+            rings.append([b * DOMS + first + (ROOT - half + i) % RING for i in range(RING)])
+    for first in (0, 4, DOMS - 8, DOMS - 4):
+        rings.append([b * DOMS + first + i for b in range(1, BANDS, 2) for i in range(4)])
     mine = lax.all_to_all(far, ("band", "dom"), 0, 0, axis_index_groups=rings)
 
     edges = [

time: 51.7 us -> 49.6 us (0.959)
  blocking collectives: 0 us -> 18.5 us
  starting transfers between devices: 29.4 us -> 18.4 us
  waiting for transfers between devices: 14.3 us -> 4.93 us
    all_to_all x0 -> x1, blocking collectives: none -> 18.5 us  [on_device(): lax.all_to_all(density(spin_group, occupation, orbitals), 'band', 0, 0)]
    all_to_all x1 -> x0, starting transfers between devices: 10.4 us -> none  [on_device(): lax.all_to_all(density(spin_group, occupation, orbitals), 'band', 0, 0)]
    all_to_all x1, starting transfers between devices: 13.6 us -> 3.52 us  [on_device(): mine = lax.all_to_all(far, ('band', 'dom'), 0, 0, axis_index_groups=rings)]
    ppermute x1, starting transfers between devices: 2.35 us -> 11.7 us  [on_device(): swapped = lax.ppermute(pack(mine, halo, minus), 'band', swap)]
    all_to_all x1 -> x0, waiting for transfers between devices: 7.89 us -> none  [on_device(): lax.all_to_all(density(spin_group, occupation, orbitals), 'band', 0, 0)]
    all_to_all x1, waiting for transfers between devices: 3.4 us -> 2.35 us  [on_device(): mine = lax.all_to_all(far, ('band', 'dom'), 0, 0, axis_index_groups=rings)]
    ppermute x1, waiting for transfers between devices: 2.26 us -> 1.69 us  [on_device(): halo = lax.ppermute(to_send, ('band', 'dom'), edges)]
  transfers between devices with their start and end apart: 4 -> 3, of which waited for: 4 -> 3; matrix products, arithmetic and copies ran while one was open for 0% -> 0% of each run, Pallas kernels for 1% -> 1%
where the time goes in v6:
time: 49.6 us; the launch traced here: 49.1 us
  blocking collectives  18.5 us (37%)
  starting transfers between devices  18.4 us (37%)
  Pallas kernels  6.65 us (13%)
  waiting for transfers between devices  4.93 us (10%)
  between operations  0.69 us (1%)
    all_to_all x1, blocking collectives, on_device(): lax.all_to_all(density(spin_group, occupation, orbitals), 'band', 0, 0)  18.5 us
    ppermute x1, starting transfers between devices, on_device(): swapped = lax.ppermute(pack(mine, halo, minus), 'band', swap)  11.7 us
    all_to_all x1, starting transfers between devices, on_device(): mine = lax.all_to_all(far, ('band', 'dom'), 0, 0, axis_index_groups=rings)  3.52 us
    ppermute x1, starting transfers between devices, on_device(): halo = lax.ppermute(to_send, ('band', 'dom'), edges)  3.14 us
    pallas_call x1, Pallas kernels, final_part(): pl.pallas_call(final_kernel, out_shape=(shape(16, 32, 128), shape(16, 32,...  2.59 us
    all_to_all x1, waiting for transfers between devices, on_device(): mine = lax.all_to_all(far, ('band', 'dom'), 0, 0, axis_index_groups=rings)  2.35 us
    pallas_call x1, Pallas kernels, density(): pl.pallas_call(density_kernel, out_shape=jax.ShapeDtypeStruct((BANDS, ROW...  2.02 us
    pallas_call x1, Pallas kernels, far_part(): pl.pallas_call(far_kernel, out_shape=(shape(RING, 16, 128), shape(26, 8,...  1.76 us
  transfers between devices with their start and end apart: 3, of which 3 were waited for; matrix products, arithmetic and copies ran while one was open for 0% of the time, Pallas kernels for 1%

profile of v6, /device:TPU:1, one launch (start us, length us, event | category | flops | bytes accessed | tf_op | source)
XLA Modules:
  0.0 49.1 jit_solution(14032799522719115297)
XLA Ops:
  0.6 2.0 %density.1 = f32[8,96,128]{2,1,0:T(8,128)} custom-call(s32[8]{0:T(128)} %spin_hbm.1, s32[8]{0:T(128)} %occ_hbm.1, f32[8,8,16,64]{3,2,1,0:T(8,128)} %orb_hbm.1), custom_call_target="tpu_custom_call" | custom-call | tf_op jit(solution)/shard_map/density/pallas_call | solution.py:252
  2.7 0.0 copy-start
  2.7 18.5 %all_to_all.10.part_ref = f32[8,96,128]{2,1,0:T(8,128)S(1)} all-to-all(f32[8,96,128]{2,1,0:T(8,128)} %density.1), channel_id=1, replica_groups=mesh['band'=8,'dom'=64] {'band'}, dimensions={0} | all-to-all | bytes 786432 | tf_op jit(solution)/shard_map/all_to_all | solution.py:573
  21.1 0.0 copy-done
  21.1 1.8 %far.1 = (f32[16,16,128]{2,1,0:T(8,128)}, f32[26,8,128]{2,1,0:T(8,128)S(1)}, f32[8,8,128]{2,1,0:T(8,128)S(1)}, f32[18,4,8,128]{3,2,1,0:T(8,128)S(1)}, f32[20,4,8...) custom-call(f32[8,96,128]{2,1,0:T(8,128)S(1)} %all_to_all.10.part_re, ...), custom_call_target="tpu_custom_call" | custom-call | tf_op jit(solution)/shard_map/far/pallas_call | solution.py:346
  22.9 3.5 %all-to-all-start.1 = ((f32[16,16,128]{2,1,0:T(8,128)}), f32[16,16,128]{2,1,0:T(8,128)S(1)}, u32[]{:S(2)}, u32[]{:S(2)}) async-start(f32[16,16,128]{2,1,0:T(8,128)} %get-tuple-element.13), calls=%async_computation.1 | async-start | bytes 262144 | tf_op jit(solution)/shard_map/all_to_all | solution.py:582
  26.4 3.1 %collective-permute-start = (f32[26,8,128]{2,1,0:T(8,128)S(1)}, f32[26,8,128]{2,1,0:T(8,128)S(1)}, u32[]{:S(2)}, u32[]{:S(2)}) collective-permute-start(f32[26,8,128]{2,1,0:T(8,128)S(1)} %get-tuple-element.14), channel_id=1, source_target_pairs={{1,0},{2,1},{3,2},{4,3},{5,4},{6,5},{7,6},{8,7},{9,8},{10,9},{11,1... | collective-permute-start | bytes 319496 | tf_op jit(solution)/shard_map/ppermute | solution.py:587
  29.6 1.7 %collective-permute-done.halo_ref = f32[26,8,128]{2,1,0:T(8,128)S(1)} collective-permute-done((f32[26,8,128]{2,1,0:T(8,128)S(1)}, f32[26,8,128]{2,1,0:T(8,128)S(1)}, u32[]{:S(2)}, u32[]{:S(2)}) %collective-permute-start) | collective-permute-done | bytes 106528 | tf_op jit(solution)/shard_map/ppermute | solution.py:587
  31.3 2.3 %all-to-all-done.1.mine_ref = f32[16,16,128]{2,1,0:T(8,128)S(1)} async-done(((f32[16,16,128]{2,1,0:T(8,128)}), f32[16,16,128]{2,1,0:T(8,128)S(1)}, u32[]{:S(2)}, u32[]{:S(2)}) %all-to-all-start.1) | async-done | bytes 131104 | tf_op jit(solution)/shard_map/all_to_all | solution.py:582
  33.6 11.7 %collective-permute-start.1 = (f32[66,8,128]{2,1,0:T(8,128)S(1)}, f32[66,8,128]{2,1,0:T(8,128)S(1)}, u32[]{:S(2)}, u32[]{:S(2)}) collective-permute-start(f32[66,8,128]{2,1,0:T(8,128)S(1)} %pack.1), channel_id=1, source_target_pairs={{0,64},{64,0},{128,192},{192,128},{256,320},{320,256},{384,448},{4... | collective-permute-start | bytes 811016 | tf_op jit(solution)/shard_map/ppermute | solution.py:590
  45.3 0.3 near.1
  45.6 0.9 %collective-permute-done.1.swapped_ref = f32[66,8,128]{2,1,0:T(8,128)S(1)} collective-permute-done((f32[66,8,128]{2,1,0:T(8,128)S(1)}, f32[66,8,128]{2,1,0:T(8,128)S(1)}, u32[]{:S(2)}, u32[]{:S(2)}) %collective-permute-start.1) | collective-permute-done | bytes 270368 | tf_op jit(solution)/shard_map/ppermute | solution.py:590
  46.5 2.6 %final.1 = (f32[16,32,128]{2,1,0:T(8,128)}, f32[16,32,128]{2,1,0:T(8,128)}) custom-call(f32[16,16,128]{2,1,0:T(8,128)S(1)} %all-to-all-done.1.mine_ref, f32[66,8,128]{2,1,0:T(8,128)S(1)} %collective-permute-done.1.swapped_ref, f32[26,8,128]{2,1,0:T(8,128)S(1)} %collective-permute-done.halo_ref, f32[8,8,128]{2,1,0:T(8,128)S(1)} %get-tuple-element.15.minus_ref, ...), custom_call_target="tpu_custom_call" | custom-call | tf_op jit(solution)/shard_map/final/pallas_call | solution.py:556
  (1 shorter events, 0.0 us)
Async XLA Ops:
  2.7 18.5 %copy-start = (f32[16,32,128]{2,1,0:T(8,128)S(1)}, f32[16,32,128]{2,1,0:T(8,128)}, u32[]{:S(2)}) copy-start(f32[16,32,128]{2,1,0:T(8,128)} %guess_ref.3) | copy-start | bytes 786436
  22.9 10.7 %all-to-all-start.1 = ((f32[16,16,128]{2,1,0:T(8,128)}), f32[16,16,128]{2,1,0:T(8,128)S(1)}, u32[]{:S(2)}, u32[]{:S(2)}) async-start(f32[16,16,128]{2,1,0:T(8,128)} %get-tuple-element.13), calls=%async_computation.1 | async-start | bytes 262144 | tf_op jit(solution)/shard_map/all_to_all | solution.py:582
  26.4 4.8 %collective-permute-start = (f32[26,8,128]{2,1,0:T(8,128)S(1)}, f32[26,8,128]{2,1,0:T(8,128)S(1)}, u32[]{:S(2)}, u32[]{:S(2)}) collective-permute-start(f32[26,8,128]{2,1,0:T(8,128)S(1)} %get-tuple-element.14), channel_id=1, source_target_pairs={{1,0},{2,1},{3,2},{4,3},{5,4},{6,5},{7,6},{8,7},{9,8},{10,9},{11,1... | collective-permute-start | bytes 319496 | tf_op jit(solution)/shard_map/ppermute | solution.py:587
  33.6 12.8 %collective-permute-start.1 = (f32[66,8,128]{2,1,0:T(8,128)S(1)}, f32[66,8,128]{2,1,0:T(8,128)S(1)}, u32[]{:S(2)}, u32[]{:S(2)}) collective-permute-start(f32[66,8,128]{2,1,0:T(8,128)S(1)} %pack.1), channel_id=1, source_target_pairs={{0,64},{64,0},{128,192},{192,128},{256,320},{320,256},{384,448},{4... | collective-permute-start | bytes 811016 | tf_op jit(solution)/shard_map/ppermute | solution.py:590

commit v7 on v6

--- a/solution.py
+++ b/solution.py
@@ -259,7 +259,7 @@
             pltpu.VMEM((8, 8, 16, 64), F32), pltpu.VMEM((16, 16, 64), F32),
             pltpu.SemaphoreType.DMA((10,)),
         ],
-        compiler_params=pltpu.CompilerParams(vmem_limit_bytes=57 * 2**20),
+        compiler_params=pltpu.CompilerParams(vmem_limit_bytes=40 * 2**20),
         name="density",
     )(spin_group, occupation, orbitals)
 
@@ -270,8 +270,8 @@
 
 
 def far_kernel(
-    part_ref, guess_ref, far_hbm, halo_ref, minus_ref,
-    d_ref, t_ref, r_ref, b1_ref, t1_ref, r1_ref, sum_ref, far_ref, sems,
+    part_ref, guess_ref, far_ref, halo_ref, minus_ref,
+    d_ref, t_ref, r_ref, b1_ref, t1_ref, r1_ref, sum_ref,
 ):
     inside0, inside1 = masks(lax.axis_index("dom"))
     for i in range(ROWS // 16):
@@ -312,8 +312,8 @@
             v = r1[2 * k] + r1[2 * k + 1]
             v = 0.5 * pair_z(v[0] + v[1], 2)
             packed = v if packed is None else jnp.where(lane == p, v, packed)
-        far_ref[pl.ds(8 * group, 8), :] = packed
-    copies = copy_all(far_ref, far_hbm, RING, sems)
+        for i in range(RING):
+            far_ref[i, pl.ds(8 * group, 8), :] = packed
 
     core = lax.axis_index("band") % 2
     even = (lanes_of((8, 128)) & 1) == 0
@@ -335,9 +335,6 @@
     @pl.when(core == 1)
     def _():
         edges(16, 7, 3)
-
-    for copy in copies:
-        copy.wait()
 
 
 def far_part(parts, guess):
@@ -351,10 +348,8 @@
             shape(12, 2, 8, 128), shape(14, 2, 8, 128), shape(16, 2, 8, 128),
         ),
         in_specs=[vmem, vmem],
-        out_specs=(pl.BlockSpec(memory_space=pltpu.HBM),) + (vmem,) * 8,
-        scratch_shapes=[
-            pltpu.VMEM((ROWS, 128), F32), pltpu.VMEM((16, 128), F32), pltpu.SemaphoreType.DMA((RING,)),
-        ],
+        out_specs=(vmem,) * 9,
+        scratch_shapes=[pltpu.VMEM((ROWS, 128), F32)],
         compiler_params=pltpu.CompilerParams(vmem_limit_bytes=32 * 2**20),
         name="far",
     )(parts, guess)
@@ -570,6 +565,9 @@
 
 
 def on_device(orbitals, spin_group, occupation, potential_guess):
+    orbitals, spin_group, occupation = (
+        pltpu.with_memory_space_constraint(v, pltpu.HBM) for v in (orbitals, spin_group, occupation)
+    )
     parts = lax.all_to_all(density(spin_group, occupation, orbitals), "band", 0, 0)
     far, to_send, minus, *held = far_part(parts, potential_guess)
     rings = []

time: 49.6 us -> 48.6 us (0.980)
  blocking collectives: 18.5 us -> 17.5 us
  Pallas kernels: 6.65 us -> 5.88 us
  starting transfers between devices: 18.4 us -> 19 us
    all_to_all x1, blocking collectives: 18.5 us -> 17.5 us  [on_device(): lax.all_to_all(density(spin_group, occupation, orbitals), 'band', 0, 0)]
    pallas_call x1, Pallas kernels: 2.02 us -> 1.27 us  [density(): pl.pallas_call(density_kernel, out_shape=jax.ShapeDtypeStruct((BANDS, ROW...]
    ppermute x1, starting transfers between devices: 11.7 us -> 12.4 us  [on_device(): swapped = lax.ppermute(pack(mine, halo, minus), 'band', swap)]
where the time goes in v7:
time: 48.6 us; the launch traced here: 48 us
  starting transfers between devices  19 us (39%)
  blocking collectives  17.5 us (36%)
  Pallas kernels  5.88 us (12%)
  waiting for transfers between devices  4.93 us (10%)
  between operations  0.68 us (1%)
    all_to_all x1, blocking collectives, on_device(): lax.all_to_all(density(spin_group, occupation, orbitals), 'band', 0, 0)  17.5 us
    ppermute x1, starting transfers between devices, on_device(): swapped = lax.ppermute(pack(mine, halo, minus), 'band', swap)  12.4 us
    all_to_all x1, starting transfers between devices, on_device(): mine = lax.all_to_all(far, ('band', 'dom'), 0, 0, axis_index_groups=rings)  3.51 us
    ppermute x1, starting transfers between devices, on_device(): halo = lax.ppermute(to_send, ('band', 'dom'), edges)  3.14 us
    pallas_call x1, Pallas kernels, final_part(): pl.pallas_call(final_kernel, out_shape=(shape(16, 32, 128), shape(16, 32,...  2.59 us
    all_to_all x1, waiting for transfers between devices, on_device(): mine = lax.all_to_all(far, ('band', 'dom'), 0, 0, axis_index_groups=rings)  2.35 us
    pallas_call x1, Pallas kernels, far_part(): pl.pallas_call(far_kernel, out_shape=(shape(RING, 16, 128), shape(26, 8,...  1.75 us
    ppermute x1, waiting for transfers between devices, on_device(): halo = lax.ppermute(to_send, ('band', 'dom'), edges)  1.69 us
  transfers between devices with their start and end apart: 3, of which 3 were waited for; matrix products, arithmetic and copies ran while one was open for 0% of the time, Pallas kernels for 1%

profile of v7, /device:TPU:1, one launch (start us, length us, event | category | flops | bytes accessed | tf_op | source)
XLA Modules:
  0.0 48.0 jit_solution(16827728541000617150)
XLA Ops:
  0.6 1.3 %density.1 = f32[8,96,128]{2,1,0:T(8,128)S(1)} custom-call(s32[8]{0:T(128)} %spin_hbm.1, s32[8]{0:T(128)} %occ_hbm.1, f32[8,8,16,64]{3,2,1,0:T(8,128)} %orb_hbm.1), custom_call_target="tpu_custom_call" | custom-call | tf_op jit(solution)/shard_map/density/pallas_call | solution.py:252
  1.9 0.0 copy-start
  1.9 17.5 %all_to_all.10.part_ref = f32[8,96,128]{2,1,0:T(8,128)S(1)} all-to-all(f32[8,96,128]{2,1,0:T(8,128)S(1)} %density.1), channel_id=1, replica_groups=mesh['band'=8,'dom'=64] {'band'}, dimensions={0} | all-to-all | bytes 786432 | tf_op jit(solution)/shard_map/all_to_all | solution.py:571
  19.4 0.0 copy-done
  19.4 1.8 %far.1 = (f32[16,16,128]{2,1,0:T(8,128)}, f32[26,8,128]{2,1,0:T(8,128)S(1)}, f32[8,8,128]{2,1,0:T(8,128)S(1)}, f32[18,4,8,128]{3,2,1,0:T(8,128)S(1)}, f32[20,4,8...) custom-call(f32[8,96,128]{2,1,0:T(8,128)S(1)} %all_to_all.10.part_re, ...), custom_call_target="tpu_custom_call" | custom-call | tf_op jit(solution)/shard_map/far/pallas_call | solution.py:343
  21.1 3.5 %all-to-all-start.1 = ((f32[16,16,128]{2,1,0:T(8,128)}), f32[16,16,128]{2,1,0:T(8,128)S(1)}, u32[]{:S(2)}, u32[]{:S(2)}) async-start(f32[16,16,128]{2,1,0:T(8,128)} %get-tuple-element.13), calls=%async_computation.1 | async-start | bytes 262144 | tf_op jit(solution)/shard_map/all_to_all | solution.py:580
  24.7 3.1 %collective-permute-start = (f32[26,8,128]{2,1,0:T(8,128)S(1)}, f32[26,8,128]{2,1,0:T(8,128)S(1)}, u32[]{:S(2)}, u32[]{:S(2)}) collective-permute-start(f32[26,8,128]{2,1,0:T(8,128)S(1)} %get-tuple-element.14), channel_id=1, source_target_pairs={{1,0},{2,1},{3,2},{4,3},{5,4},{6,5},{7,6},{8,7},{9,8},{10,9},{11,1... | collective-permute-start | bytes 319496 | tf_op jit(solution)/shard_map/ppermute | solution.py:585
  27.8 1.7 %collective-permute-done.halo_ref = f32[26,8,128]{2,1,0:T(8,128)S(1)} collective-permute-done((f32[26,8,128]{2,1,0:T(8,128)S(1)}, f32[26,8,128]{2,1,0:T(8,128)S(1)}, u32[]{:S(2)}, u32[]{:S(2)}) %collective-permute-start) | collective-permute-done | bytes 106528 | tf_op jit(solution)/shard_map/ppermute | solution.py:585
  29.5 2.3 %all-to-all-done.1.mine_ref = f32[16,16,128]{2,1,0:T(8,128)S(1)} async-done(((f32[16,16,128]{2,1,0:T(8,128)}), f32[16,16,128]{2,1,0:T(8,128)S(1)}, u32[]{:S(2)}, u32[]{:S(2)}) %all-to-all-start.1) | async-done | bytes 131104 | tf_op jit(solution)/shard_map/all_to_all | solution.py:580
  31.9 12.4 %collective-permute-start.1 = (f32[66,8,128]{2,1,0:T(8,128)S(1)}, f32[66,8,128]{2,1,0:T(8,128)S(1)}, u32[]{:S(2)}, u32[]{:S(2)}) collective-permute-start(f32[66,8,128]{2,1,0:T(8,128)S(1)} %pack.1), channel_id=1, source_target_pairs={{0,64},{64,0},{128,192},{192,128},{256,320},{320,256},{384,448},{4... | collective-permute-start | bytes 811016 | tf_op jit(solution)/shard_map/ppermute | solution.py:588
  44.3 0.3 near.1
  44.5 0.9 %collective-permute-done.1.swapped_ref = f32[66,8,128]{2,1,0:T(8,128)S(1)} collective-permute-done((f32[66,8,128]{2,1,0:T(8,128)S(1)}, f32[66,8,128]{2,1,0:T(8,128)S(1)}, u32[]{:S(2)}, u32[]{:S(2)}) %collective-permute-start.1) | collective-permute-done | bytes 270368 | tf_op jit(solution)/shard_map/ppermute | solution.py:588
  45.4 2.6 %final.1 = (f32[16,32,128]{2,1,0:T(8,128)}, f32[16,32,128]{2,1,0:T(8,128)}) custom-call(f32[16,16,128]{2,1,0:T(8,128)S(1)} %all-to-all-done.1.mine_ref, f32[66,8,128]{2,1,0:T(8,128)S(1)} %collective-permute-done.1.swapped_ref, f32[26,8,128]{2,1,0:T(8,128)S(1)} %collective-permute-done.halo_ref, f32[8,8,128]{2,1,0:T(8,128)S(1)} %get-tuple-element.15.minus_ref, ...), custom_call_target="tpu_custom_call" | custom-call | tf_op jit(solution)/shard_map/final/pallas_call | solution.py:551
  (1 shorter events, 0.0 us)
Async XLA Ops:
  1.9 17.5 %copy-start = (f32[16,32,128]{2,1,0:T(8,128)S(1)}, f32[16,32,128]{2,1,0:T(8,128)}, u32[]{:S(2)}) copy-start(f32[16,32,128]{2,1,0:T(8,128)} %guess_ref.3) | copy-start | bytes 786436
  21.1 10.7 %all-to-all-start.1 = ((f32[16,16,128]{2,1,0:T(8,128)}), f32[16,16,128]{2,1,0:T(8,128)S(1)}, u32[]{:S(2)}, u32[]{:S(2)}) async-start(f32[16,16,128]{2,1,0:T(8,128)} %get-tuple-element.13), calls=%async_computation.1 | async-start | bytes 262144 | tf_op jit(solution)/shard_map/all_to_all | solution.py:580
  24.7 4.8 %collective-permute-start = (f32[26,8,128]{2,1,0:T(8,128)S(1)}, f32[26,8,128]{2,1,0:T(8,128)S(1)}, u32[]{:S(2)}, u32[]{:S(2)}) collective-permute-start(f32[26,8,128]{2,1,0:T(8,128)S(1)} %get-tuple-element.14), channel_id=1, source_target_pairs={{1,0},{2,1},{3,2},{4,3},{5,4},{6,5},{7,6},{8,7},{9,8},{10,9},{11,1... | collective-permute-start | bytes 319496 | tf_op jit(solution)/shard_map/ppermute | solution.py:585
  31.9 13.5 %collective-permute-start.1 = (f32[66,8,128]{2,1,0:T(8,128)S(1)}, f32[66,8,128]{2,1,0:T(8,128)S(1)}, u32[]{:S(2)}, u32[]{:S(2)}) collective-permute-start(f32[66,8,128]{2,1,0:T(8,128)S(1)} %pack.1), channel_id=1, source_target_pairs={{0,64},{64,0},{128,192},{192,128},{256,320},{320,256},{384,448},{4... | collective-permute-start | bytes 811016 | tf_op jit(solution)/shard_map/ppermute | solution.py:588

commit v8 on v7

--- a/solution.py
+++ b/solution.py
@@ -168,7 +168,7 @@
             return v
         return mask
 
-    return masked(15), masked(7)
+    return masked(15), masked(7), masked(3)
 
 
 def guess_planes(guess_ref):
@@ -270,10 +270,10 @@
 
 
 def far_kernel(
-    part_ref, guess_ref, far_ref, halo_ref, minus_ref,
+    part_ref, guess_ref, far_ref, halo_ref, minus_ref, b2_ref,
     d_ref, t_ref, r_ref, b1_ref, t1_ref, r1_ref, sum_ref,
 ):
-    inside0, inside1 = masks(lax.axis_index("dom"))
+    inside0, inside1, inside2 = masks(lax.axis_index("dom"))
     for i in range(ROWS // 16):
         rows = pl.ds(16 * i, 16)
         total = part_ref[0, rows, :]
@@ -304,19 +304,45 @@
         b1.put(k, restricted(r, k))
     hold_T(b1, t1, range(-3, 11), 2, inside1)
     hold_T(t1, r1, range(-4, 12), 2, inside1)
-    lane = lanes_of((8, 128)) & 3
+    b2 = {}
+    for k in range(-2, 6):
+        v = r1[2 * k] + r1[2 * k + 1]
+        b2[k] = 0.5 * pair_z(v[0] + v[1], 2)
+        b2_ref[k + 2] = b2[k]
+    t2 = run_T(b2, range(-3, 7), 4, mask=inside2)
+    r2 = run_T(t2, range(-4, 8), 4, mask=inside2)
+    b3 = [0.5 * pair_y(pair_z(r2[2 * k] + r2[2 * k + 1], 4), 1) for k in range(-2, 4)]
+
+    lane, row = lanes_of((8, 128)), rows_of((8, 128))
+    parity = row & 1
+    common = b3[0]
+    for n in range(1, 4):
+        here = ((lane & 7) == 3 + 4 * (n % 2)) & (parity == n // 2)
+        common = jnp.where(here, b3[n], common)
+    above, below = common, common
+    for p in range(3):
+        above = jnp.where((lane & 3) == p, b2[3 + p], above)
+        below = jnp.where((lane & 3) == p, b2[p - 2], below)
+    line = lanes_of((1, 128)) & 7
+    last = b3[4][0:1]
+    for n in (4, 5):
+        for y in range(4):
+            last = jnp.where(line == 4 * (n - 4) + y, b3[n][2 * y:2 * y + 1], last)
+    core = lax.axis_index("band") % 2
+    half = RING // 2 * core
+    me = (lax.axis_index("dom") + half) % RING
+    for i in range(RING):
+        target = (ROOT - half + i) % RING
+        far_ref[pl.ds(9 * i, 8), :] = jnp.where(target > me, above, below)
+        far_ref[pl.ds(9 * i + 8, 1), :] = last
+
     for group in range(2):
-        packed = None
-        for p in range(4):
-            k = 4 * group + p - 2
-            v = r1[2 * k] + r1[2 * k + 1]
-            v = 0.5 * pair_z(v[0] + v[1], 2)
-            packed = v if packed is None else jnp.where(lane == p, v, packed)
-        for i in range(RING):
-            far_ref[i, pl.ds(8 * group, 8), :] = packed
-
-    core = lax.axis_index("band") % 2
-    even = (lanes_of((8, 128)) & 1) == 0
+        packed = b2[4 * group - 2]
+        for p in range(1, 4):
+            packed = jnp.where((lane & 3) == p, b2[4 * group - 2 + p], packed)
+        halo_ref[26 + group] = packed
+
+    even = (lane & 1) == 0
 
     def edges(first0, first1, plane):
         for k in range(4):
@@ -343,12 +369,12 @@
     return pl.pallas_call(
         far_kernel,
         out_shape=(
-            shape(RING, 16, 128), shape(26, 8, 128), shape(8, 8, 128),
+            shape(9 * RING, 128), shape(28, 8, 128), shape(8, 8, 128), shape(8, 8, 128),
             shape(18, 4, 8, 128), shape(20, 4, 8, 128), shape(22, 4, 8, 128),
             shape(12, 2, 8, 128), shape(14, 2, 8, 128), shape(16, 2, 8, 128),
         ),
         in_specs=[vmem, vmem],
-        out_specs=(vmem,) * 9,
+        out_specs=(vmem,) * 10,
         scratch_shapes=[pltpu.VMEM((ROWS, 128), F32)],
         compiler_params=pltpu.CompilerParams(vmem_limit_bytes=32 * 2**20),
         name="far",
@@ -388,18 +414,18 @@
 
 
 def pack_kernel(mine_ref, halo_ref, minus_ref, out_ref):
-    out_ref[pl.ds(0, 26)] = halo_ref[...]
-    out_ref[pl.ds(26, 8)] = minus_ref[...]
+    out_ref[pl.ds(0, 28)] = halo_ref[...]
+    out_ref[pl.ds(28, 8)] = minus_ref[...]
     for i in range(RING):
-        for half in range(2):
-            out_ref[34 + 2 * i + half] = mine_ref[i, pl.ds(8 * half, 8), :]
+        out_ref[36 + 2 * i] = mine_ref[pl.ds(9 * i, 8), :]
+        out_ref[37 + 2 * i, pl.ds(0, 1), :] = mine_ref[pl.ds(9 * i + 8, 1), :]
 
 
 def pack(mine, halo, minus):
     vmem = pl.BlockSpec(memory_space=pltpu.VMEM)
     return pl.pallas_call(
         pack_kernel,
-        out_shape=jax.ShapeDtypeStruct((66, 8, 128), F32),
+        out_shape=jax.ShapeDtypeStruct((36 + 2 * RING, 8, 128), F32),
         in_specs=[vmem] * 3,
         out_specs=vmem,
         compiler_params=pltpu.CompilerParams(vmem_limit_bytes=32 * 2**20),
@@ -408,25 +434,25 @@
 
 
 def final_kernel(
-    mine_ref, swapped_ref, halo_ref, minus_ref, own0_ref, own1_ref, pot_hbm, mag_hbm,
-    b2_ref, t2_ref, r2_ref, p1_ref, pot_ref, mag_ref, sems,
+    packed_ref, swapped_ref, mine2_ref, own0_ref, own1_ref, pot_hbm, mag_hbm,
+    p1_ref, pot_ref, mag_ref, sems,
 ):
     dom = lax.axis_index("dom")
     lower = lax.axis_index("band") % 2 == 0
 
     def high(i):
-        return jnp.where(lower, halo_ref[i], swapped_ref[i])
+        return jnp.where(lower, packed_ref[i], swapped_ref[i])
 
     def low(i):
-        return jnp.where(lower, swapped_ref[i], halo_ref[i])
+        return jnp.where(lower, swapped_ref[i], packed_ref[i])
 
     minus = []
     for x in range(8):
         j = x % 4
         pair = []
         for p in range(2):
-            own = minus_ref[2 * j + p]
-            pair.append(jnp.where(lower == (x < 4), own, swapped_ref[26 + 2 * j + p]))
+            own = packed_ref[28 + 2 * j + p]
+            pair.append(jnp.where(lower == (x < 4), own, swapped_ref[28 + 2 * j + p]))
         minus.append(refine_y(pair))
     for k in range(16):
         mag = refine_x(minus, k)
@@ -448,42 +474,55 @@
             return jnp.where(ok, v, 0.0)
         return mask
 
-    lane = lanes_of((8, 128)) & 3
+    lane, row = lanes_of((8, 128)), rows_of((8, 128))
     spot = dom % RING
     first = dom - spot
     other_first = first + jnp.where(spot < RING // 2, -(RING // 2), RING // 2)
-
-    def vector(i, half):
-        wanted = dom - REACH + i
+    body, last = {}, {}
+    for step in range(-REACH, REACH + 1):
+        wanted = dom + step
         at = wanted - first
         aligned = (at >= 0) & (at < RING)
         at = jnp.clip(jnp.where(aligned, at, wanted - other_first), 0, RING - 1)
         slot = (at + RING - jnp.where(aligned, ROOT, ROOT - RING // 2)) % RING
-        v = jnp.where(
-            aligned == lower, mine_ref[slot, pl.ds(8 * half, 8), :], swapped_ref[34 + 2 * slot + half]
-        )
-        return jnp.where((wanted >= 0) & (wanted < DOMS), v, 0.0)
-
-    b2, t2, r2 = Held(b2_ref, -30), Held(t2_ref, -25), Held(r2_ref, -24)
-    for i in range(16):
-        packed = None
-        for part in ((i, 0), (i - 1, 1)):
-            if 0 <= part[0] < 15:
-                v = vector(*part)
-                packed = v if packed is None else packed + v
-        for p in range(4):
-            only = jnp.where(lane == p, packed, 0.0)
-            only = only + pltpu.roll(only, 1 if p % 2 == 0 else 127, 1)
-            only = only + pltpu.roll(only, 2 if p < 2 else 126, 1)
-            b2.put(4 * (i - REACH) - 2 + p, only)
+        there = (wanted >= 0) & (wanted < DOMS)
+        for part, ref in ((0, body), (1, last)):
+            rows = pl.ds(0, 1 if part else 8)
+            v = jnp.where(
+                aligned == lower,
+                packed_ref[36 + 2 * slot + part, rows, :],
+                swapped_ref[36 + 2 * slot + part, rows, :],
+            )
+            ref[step] = jnp.where(there, v, 0.0)
+
+    def unpack4(v, p):
+        return pair_z(pair_z(jnp.where((lane & 3) == p, v, 0.0), 1), 2)
+
     inside2, inside3, inside4 = masked(4), masked(2), masked(1)
-    hold_T(b2, t2, range(-25, 29), 4, inside2)
-    hold_T(t2, r2, range(-24, 28), 4, lambda k, v: v)
+    b2 = {k: mine2_ref[k + 2] for k in range(-2, 6)}
+    below, above = [low(26), low(27)], [high(26), high(27)]
+    for n in range(7):
+        up, down = n - 5, n + 2
+        v = unpack4(below[(n + 1) // 4], (n + 1) % 4)
+        if n < 3:
+            v = v + unpack4(body[-2], n)
+        b2[up] = b2[up] + v if up in b2 else v
+        v = unpack4(above[n // 4], n % 4)
+        if n > 3:
+            v = v + unpack4(body[2], n - 4)
+        b2[down] = b2[down] + v if down in b2 else v
+    t2 = run_T(b2, range(-4, 8), 4, mask=inside2)
+    r2 = run_T(t2, range(-2, 6), 4)
 
     b3 = {}
-    for k in range(-12, 14):
-        v = pair_y(pair_z(r2[2 * k] + r2[2 * k + 1], 4), 1)
-        b3[k] = inside3(k, 0.5 * v)
+    for pair in range(-6, 7):
+        both = jnp.where((row & 1) == 0, body[pair + 1], body[pair])
+        both = pair_y(jnp.where((lane & 3) == 3, both, 0.0), 1)
+        tail = jnp.broadcast_to(last[pair - 1], (8, 128))
+        for n in range(2):
+            v = jnp.where((lane & 7) == 4 * n + 3, both, 0.0)
+            v = v + jnp.where((lane & 7) == 4 * n + (row >> 1), tail, 0.0)
+            b3[2 * pair + n] = pair_z(pair_z(pair_z(v, 1), 2), 4)
     t3 = run_T(b3, range(-11, 13), 8, 2, inside3)
     r3 = run_T(t3, range(-10, 12), 8, 2)
 
@@ -551,11 +590,10 @@
     return pl.pallas_call(
         final_kernel,
         out_shape=(shape(16, 32, 128), shape(16, 32, 128)),
-        in_specs=[vmem] * 6,
+        in_specs=[vmem] * 5,
         out_specs=(hbm, hbm),
         scratch_shapes=[
-            pltpu.VMEM((64, 8, 128), F32), pltpu.VMEM((54, 8, 128), F32),
-            pltpu.VMEM((52, 8, 128), F32), pltpu.VMEM((18, 4, 8, 128), F32),
+            pltpu.VMEM((18, 4, 8, 128), F32),
             pltpu.VMEM((16, 32, 128), F32), pltpu.VMEM((16, 32, 128), F32),
             pltpu.SemaphoreType.DMA((5,)),
         ],
@@ -569,7 +607,7 @@
         pltpu.with_memory_space_constraint(v, pltpu.HBM) for v in (orbitals, spin_group, occupation)
     )
     parts = lax.all_to_all(density(spin_group, occupation, orbitals), "band", 0, 0)
-    far, to_send, minus, *held = far_part(parts, potential_guess)
+    far, to_send, minus, mine2, *held = far_part(parts, potential_guess)
     rings = []
     for b in range(BANDS):
         half = RING // 2 * (b % 2)
@@ -577,7 +615,9 @@
             rings.append([b * DOMS + first + (ROOT - half + i) % RING for i in range(RING)])
     for first in (0, 4, DOMS - 8, DOMS - 4):
         rings.append([b * DOMS + first + i for b in range(1, BANDS, 2) for i in range(4)])
-    mine = lax.all_to_all(far, ("band", "dom"), 0, 0, axis_index_groups=rings)
+    mine = lax.all_to_all(
+        far.reshape(RING, 9 * 128), ("band", "dom"), 0, 0, axis_index_groups=rings
+    ).reshape(9 * RING, 128)
 
     edges = [
         (b * DOMS + d + 1 - b % 2, b * DOMS + d + b % 2) for b in range(BANDS) for d in range(DOMS - 1)
@@ -585,8 +625,9 @@
     halo = lax.ppermute(to_send, ("band", "dom"), edges)
     own0, own1 = near_part(potential_guess, *held)
     swap = [(b, b ^ 1) for b in range(BANDS)]
-    swapped = lax.ppermute(pack(mine, halo, minus), "band", swap)
-    return final_part(mine, swapped, halo, minus, own0, own1)
+    packed = pack(mine, halo, minus)
+    swapped = lax.ppermute(packed, "band", swap)
+    return final_part(packed, swapped, mine2, own0, own1)
 
 
 def solution(mesh):

time: 48.6 us -> 48.2 us (level)
  no operation moved by 1% of the time
where the time goes in v8:
time: 48.2 us; the launch traced here: 47.9 us
  starting transfers between devices  18.7 us (39%)
  blocking collectives  17.5 us (36%)
  Pallas kernels  6.36 us (13%)
  waiting for transfers between devices  4.7 us (10%)
  between operations  0.68 us (1%)
    all_to_all x1, blocking collectives, on_device(): lax.all_to_all(density(spin_group, occupation, orbitals), 'band', 0, 0)  17.5 us
    ppermute x1, starting transfers between devices, on_device(): swapped = lax.ppermute(packed, 'band', swap)  12 us
    all_to_all x1, starting transfers between devices, on_device(): lax.all_to_all(far.reshape(RING, 9 * 128), ('band', 'dom'), 0, 0, axis_in...  3.5 us
    ppermute x1, starting transfers between devices, on_device(): halo = lax.ppermute(to_send, ('band', 'dom'), edges)  3.14 us
    pallas_call x1, Pallas kernels, final_part(): pl.pallas_call(final_kernel, out_shape=(shape(16, 32, 128), shape(16, 32,...  2.85 us
    all_to_all x1, waiting for transfers between devices, on_device(): lax.all_to_all(far.reshape(RING, 9 * 128), ('band', 'dom'), 0, 0, axis_in...  2.04 us
    pallas_call x1, Pallas kernels, far_part(): pl.pallas_call(far_kernel, out_shape=(shape(9 * RING, 128), shape(28, 8,...  1.96 us
    ppermute x1, waiting for transfers between devices, on_device(): halo = lax.ppermute(to_send, ('band', 'dom'), edges)  1.77 us
  transfers between devices with their start and end apart: 3, of which 3 were waited for; matrix products, arithmetic and copies ran while one was open for 0% of the time, Pallas kernels for 1%

profile of v8, /device:TPU:1, one launch (start us, length us, event | category | flops | bytes accessed | tf_op | source)
XLA Modules:
  0.0 47.9 jit_solution(8373543966470578955)
XLA Ops:
  0.6 1.3 %density.1 = f32[8,96,128]{2,1,0:T(8,128)S(1)} custom-call(s32[8]{0:T(128)} %spin_hbm.1, s32[8]{0:T(128)} %occ_hbm.1, f32[8,8,16,64]{3,2,1,0:T(8,128)} %orb_hbm.1), custom_call_target="tpu_custom_call" | custom-call | tf_op jit(solution)/shard_map/density/pallas_call | solution.py:252
  1.9 0.0 copy-start
  1.9 17.5 %all_to_all.14.part_ref = f32[8,96,128]{2,1,0:T(8,128)S(1)} all-to-all(f32[8,96,128]{2,1,0:T(8,128)S(1)} %density.1), channel_id=1, replica_groups=mesh['band'=8,'dom'=64] {'band'}, dimensions={0} | all-to-all | bytes 786432 | tf_op jit(solution)/shard_map/all_to_all | solution.py:609
  19.4 0.0 copy-done
  19.4 2.0 %far.1 = (f32[144,128]{1,0:T(8,128)}, f32[28,8,128]{2,1,0:T(8,128)S(1)}, f32[8,8,128]{2,1,0:T(8,128)S(1)}, f32[8,8,128]{2,1,0:T(8,128)S(1)}, f32[18,4,8,128]{3,2...) custom-call(f32[8,96,128]{2,1,0:T(8,128)S(1)} %all_to_all.14.part_re, ...), custom_call_target="tpu_custom_call" | custom-call | tf_op jit(solution)/shard_map/far/pallas_call | solution.py:369
  21.4 3.5 %all-to-all-start.1 = ((f32[16,1,1152]{2,1,0:T(1,128)}), f32[16,1,1152]{2,1,0:T(1,128)S(1)}, u32[]{:S(2)}, u32[]{:S(2)}) async-start(f32[16,1,1152]{2,1,0:T(1,128)} %bitcast), calls=%async_computation.1 | async-start | bytes 147456 | tf_op jit(solution)/shard_map/all_to_all | solution.py:618
  24.9 3.1 %collective-permute-start = (f32[28,8,128]{2,1,0:T(8,128)S(1)}, f32[28,8,128]{2,1,0:T(8,128)S(1)}, u32[]{:S(2)}, u32[]{:S(2)}) collective-permute-start(f32[28,8,128]{2,1,0:T(8,128)S(1)} %get-tuple-element.15), channel_id=1, source_target_pairs={{1,0},{2,1},{3,2},{4,3},{5,4},{6,5},{7,6},{8,7},{9,8},{10,9},{11,1... | collective-permute-start | bytes 344072 | tf_op jit(solution)/shard_map/ppermute | solution.py:625
  28.0 1.8 %collective-permute-done.halo_ref = f32[28,8,128]{2,1,0:T(8,128)S(1)} collective-permute-done((f32[28,8,128]{2,1,0:T(8,128)S(1)}, f32[28,8,128]{2,1,0:T(8,128)S(1)}, u32[]{:S(2)}, u32[]{:S(2)}) %collective-permute-start) | collective-permute-done | bytes 114720 | tf_op jit(solution)/shard_map/ppermute | solution.py:625
  29.8 2.0 %all-to-all-done.1 = f32[16,1,1152]{2,1,0:T(1,128)S(1)} async-done(((f32[16,1,1152]{2,1,0:T(1,128)}), f32[16,1,1152]{2,1,0:T(1,128)S(1)}, u32[]{:S(2)}, u32[]{:S(2)}) %all-to-all-start.1) | async-done | bytes 73760 | tf_op jit(solution)/shard_map/all_to_all | solution.py:618
  31.9 12.0 %collective-permute-start.1 = (f32[68,8,128]{2,1,0:T(8,128)S(1)}, f32[68,8,128]{2,1,0:T(8,128)S(1)}, u32[]{:S(2)}, u32[]{:S(2)}) collective-permute-start(f32[68,8,128]{2,1,0:T(8,128)S(1)} %pack.1.packed_ref), channel_id=1, source_target_pairs={{0,64},{64,0},{128,192},{192,128},{256,320},{320,256},{384,448},{4... | collective-permute-start | bytes 835592 | tf_op jit(solution)/shard_map/ppermute | solution.py:629
  43.9 0.3 near.1
  44.1 0.9 %collective-permute-done.1.swapped_ref = f32[68,8,128]{2,1,0:T(8,128)S(1)} collective-permute-done((f32[68,8,128]{2,1,0:T(8,128)S(1)}, f32[68,8,128]{2,1,0:T(8,128)S(1)}, u32[]{:S(2)}, u32[]{:S(2)}) %collective-permute-start.1) | collective-permute-done | bytes 278560 | tf_op jit(solution)/shard_map/ppermute | solution.py:629
  45.0 2.8 %final.1 = (f32[16,32,128]{2,1,0:T(8,128)}, f32[16,32,128]{2,1,0:T(8,128)}) custom-call(f32[68,8,128]{2,1,0:T(8,128)S(1)} %pack.1.packed_ref, f32[68,8,128]{2,1,0:T(8,128)S(1)} %collective-permute-done.1.swapped_ref, f32[8,8,128]{2,1,0:T(8,128)S(1)} %get-tuple-element.17.mine2_ref, f32[16,4,8,128]{3,2,1,0:T(8,128)S(1)} %get-tuple-element.24.own0_ref, ...), custom_call_target="tpu_custom_call" | custom-call | tf_op jit(solution)/shard_map/final/pallas_call | solution.py:590
  (1 shorter events, 0.0 us)
Async XLA Ops:
  1.9 17.5 %copy-start = (f32[16,32,128]{2,1,0:T(8,128)S(1)}, f32[16,32,128]{2,1,0:T(8,128)}, u32[]{:S(2)}) copy-start(f32[16,32,128]{2,1,0:T(8,128)} %guess_ref.3) | copy-start | bytes 786436
  21.4 10.5 %all-to-all-start.1 = ((f32[16,1,1152]{2,1,0:T(1,128)}), f32[16,1,1152]{2,1,0:T(1,128)S(1)}, u32[]{:S(2)}, u32[]{:S(2)}) async-start(f32[16,1,1152]{2,1,0:T(1,128)} %bitcast), calls=%async_computation.1 | async-start | bytes 147456 | tf_op jit(solution)/shard_map/all_to_all | solution.py:618
  24.9 4.9 %collective-permute-start = (f32[28,8,128]{2,1,0:T(8,128)S(1)}, f32[28,8,128]{2,1,0:T(8,128)S(1)}, u32[]{:S(2)}, u32[]{:S(2)}) collective-permute-start(f32[28,8,128]{2,1,0:T(8,128)S(1)} %get-tuple-element.15), channel_id=1, source_target_pairs={{1,0},{2,1},{3,2},{4,3},{5,4},{6,5},{7,6},{8,7},{9,8},{10,9},{11,1... | collective-permute-start | bytes 344072 | tf_op jit(solution)/shard_map/ppermute | solution.py:625
  31.9 13.2 %collective-permute-start.1 = (f32[68,8,128]{2,1,0:T(8,128)S(1)}, f32[68,8,128]{2,1,0:T(8,128)S(1)}, u32[]{:S(2)}, u32[]{:S(2)}) collective-permute-start(f32[68,8,128]{2,1,0:T(8,128)S(1)} %pack.1.packed_ref), channel_id=1, source_target_pairs={{0,64},{64,0},{128,192},{192,128},{256,320},{320,256},{384,448},{4... | collective-permute-start | bytes 835592 | tf_op jit(solution)/shard_map/ppermute | solution.py:629

commit v9 on v8

--- a/solution.py
+++ b/solution.py
@@ -496,21 +496,20 @@
             ref[step] = jnp.where(there, v, 0.0)
 
     def unpack4(v, p):
-        return pair_z(pair_z(jnp.where((lane & 3) == p, v, 0.0), 1), 2)
+        v = jnp.where((lane & 3) == p, v, 0.0)
+        v = v + pltpu.roll(v, 1 if p % 2 == 0 else 127, 1)
+        return v + pltpu.roll(v, 2 if p < 2 else 126, 1)
 
     inside2, inside3, inside4 = masked(4), masked(2), masked(1)
     b2 = {k: mine2_ref[k + 2] for k in range(-2, 6)}
-    below, above = [low(26), low(27)], [high(26), high(27)]
-    for n in range(7):
-        up, down = n - 5, n + 2
-        v = unpack4(below[(n + 1) // 4], (n + 1) % 4)
-        if n < 3:
-            v = v + unpack4(body[-2], n)
-        b2[up] = b2[up] + v if up in b2 else v
-        v = unpack4(above[n // 4], n % 4)
-        if n > 3:
-            v = v + unpack4(body[2], n - 4)
-        b2[down] = b2[down] + v if down in b2 else v
+    tiles = (
+        (-5, 3, pltpu.roll(low(26), 127, 1) + body[-2]), (-2, 4, low(27)),
+        (2, 4, high(26)), (6, 3, high(27) + body[2]),
+    )
+    for start, count, tile in tiles:
+        for p in range(count):
+            k, v = start + p, unpack4(tile, p)
+            b2[k] = b2[k] + v if k in b2 else v
     t2 = run_T(b2, range(-4, 8), 4, mask=inside2)
     r2 = run_T(t2, range(-2, 6), 4)
 
@@ -547,9 +546,22 @@
     e2 = {k: inside2(k, w2[k] + ALPHA * (b2[k] + t2[k] + r2[k])) for k in range(-2, 6)}
 
     inside1, inside0 = masked(8), masked(16)
-    spread = {k: jnp.stack([e2[k // 2]] * 2, axis=0) for k in range(-4, 12)}
-    v1 = run_T(spread, range(-2, 10), 2, 1, inside1)
-    w1 = run_T(v1, range(-1, 9), 2, 1)
+    sides, base = {}, {}
+    for i in range(-1, 5):
+        v = e2[i]
+        sides[i] = sides_z(v, 2) + v + jnp.stack([from_below(v), from_above(v)], axis=0)
+        base[i] = v * (1.0 / 3.0) + sides[i] * ALPHA
+    v1, w1 = {}, {}
+    for k in range(-2, 10):
+        i, j = k // 2, k // 2 + (1 if k % 2 else -1)
+        v1[k] = inside1(k, base[i] + (e2[i] + e2[j]) * ALPHA)
+    for i in range(-1, 5):
+        around = sides_y(base[i], 1) + sides_z(base[i], 2)
+        for k in (2 * i, 2 * i + 1):
+            j = i + (1 if k % 2 else -1)
+            if -1 <= k < 9:
+                total = around + (sides[i] + sides[j]) * ALPHA + v1[k - 1] + v1[k + 1]
+                w1[k] = v1[k] * (1.0 / 3.0) + total * ALPHA
     even = (lanes_of((8, 128)) & 1) == 0
     for side, first in ((low, -1), (high, 3)):
         for pair in range(3):
@@ -560,15 +572,29 @@
                 w1[k] = w1[k] + v
     e1 = {k: inside1(k, w1[k] + own1_ref[k + 1]) for k in range(-1, 9)}
 
-    def prolonged(k):
-        v = e1[k // 2]
-        return jnp.stack([v[0], v[0], v[1], v[1]], axis=0)
-
+    wide, sides, base = {}, {}, {}
+    for i in range(-1, 9):
+        one, two = e1[i][0], e1[i][1]
+        wide[i] = jnp.stack([one, one, two, two], axis=0)
+        z_one, z_two, both = sides_z(one, 1), sides_z(two, 1), one + two
+        sides[i] = jnp.stack(
+            [
+                z_one + one + from_below(two), z_one + both,
+                z_two + both, z_two + two + from_above(one),
+            ],
+            axis=0,
+        )
+        base[i] = wide[i] * (1.0 / 3.0) + sides[i] * ALPHA
     p1 = Held(p1_ref, -1)
-    wide = {k: prolonged(k) for k in range(-2, 18)}
-    hold_T(wide, p1, range(-1, 17), 1, inside0)
+    for k in range(-1, 17):
+        i, j = k // 2, k // 2 + (1 if k % 2 else -1)
+        p1.put(k, inside0(k, base[i] + (wide[i] + wide[j]) * ALPHA))
     for k in range(16):
-        v = smooth(p1[k - 1], p1[k], p1[k + 1], 1) + own0_ref[k]
+        i, j = k // 2, k // 2 + (1 if k % 2 else -1)
+        if k % 2 == 0:
+            around = sides_y(base[i], 1) + sides_z(base[i], 1)
+        total = around + (sides[i] + sides[j]) * ALPHA + p1[k - 1] + p1[k + 1]
+        v = p1[k] * (1.0 / 3.0) + total * ALPHA + own0_ref[k]
         if k < 4:
             v = v + low(pl.ds(4 * k, 4))
         if k >= 12:

time: 48.2 us -> 47.9 us (level)
  no operation moved by 1% of the time
where the time goes in v9:
time: 47.9 us; the launch traced here: 47.5 us
  starting transfers between devices  18.7 us (39%)
  blocking collectives  17.5 us (37%)
  Pallas kernels  6.03 us (13%)
  waiting for transfers between devices  4.7 us (10%)
  between operations  0.68 us (1%)
    all_to_all x1, blocking collectives, on_device(): lax.all_to_all(density(spin_group, occupation, orbitals), 'band', 0, 0)  17.5 us
    ppermute x1, starting transfers between devices, on_device(): swapped = lax.ppermute(packed, 'band', swap)  12 us
    all_to_all x1, starting transfers between devices, on_device(): lax.all_to_all(far.reshape(RING, 9 * 128), ('band', 'dom'), 0, 0, axis_in...  3.5 us
    ppermute x1, starting transfers between devices, on_device(): halo = lax.ppermute(to_send, ('band', 'dom'), edges)  3.14 us
    pallas_call x1, Pallas kernels, final_part(): pl.pallas_call(final_kernel, out_shape=(shape(16, 32, 128), shape(16, 32,...  2.52 us
    all_to_all x1, waiting for transfers between devices, on_device(): lax.all_to_all(far.reshape(RING, 9 * 128), ('band', 'dom'), 0, 0, axis_in...  2.04 us
    pallas_call x1, Pallas kernels, far_part(): pl.pallas_call(far_kernel, out_shape=(shape(9 * RING, 128), shape(28, 8,...  1.96 us
    ppermute x1, waiting for transfers between devices, on_device(): halo = lax.ppermute(to_send, ('band', 'dom'), edges)  1.77 us
  transfers between devices with their start and end apart: 3, of which 3 were waited for; matrix products, arithmetic and copies ran while one was open for 0% of the time, Pallas kernels for 1%

profile of v9, /device:TPU:1, one launch (start us, length us, event | category | flops | bytes accessed | tf_op | source)
XLA Modules:
  0.0 47.5 jit_solution(1484567766919868771)
XLA Ops:
  0.6 1.3 %density.1 = f32[8,96,128]{2,1,0:T(8,128)S(1)} custom-call(s32[8]{0:T(128)} %spin_hbm.1, s32[8]{0:T(128)} %occ_hbm.1, f32[8,8,16,64]{3,2,1,0:T(8,128)} %orb_hbm.1), custom_call_target="tpu_custom_call" | custom-call | tf_op jit(solution)/shard_map/density/pallas_call | solution.py:252
  1.9 0.0 copy-start
  1.9 17.5 %all_to_all.14.part_ref = f32[8,96,128]{2,1,0:T(8,128)S(1)} all-to-all(f32[8,96,128]{2,1,0:T(8,128)S(1)} %density.1), channel_id=1, replica_groups=mesh['band'=8,'dom'=64] {'band'}, dimensions={0} | all-to-all | bytes 786432 | tf_op jit(solution)/shard_map/all_to_all | solution.py:635
  19.4 0.0 copy-done
  19.4 2.0 %far.1 = (f32[144,128]{1,0:T(8,128)}, f32[28,8,128]{2,1,0:T(8,128)S(1)}, f32[8,8,128]{2,1,0:T(8,128)S(1)}, f32[8,8,128]{2,1,0:T(8,128)S(1)}, f32[18,4,8,128]{3,2...) custom-call(f32[8,96,128]{2,1,0:T(8,128)S(1)} %all_to_all.14.part_re, ...), custom_call_target="tpu_custom_call" | custom-call | tf_op jit(solution)/shard_map/far/pallas_call | solution.py:369
  21.4 3.5 %all-to-all-start.1 = ((f32[16,1,1152]{2,1,0:T(1,128)}), f32[16,1,1152]{2,1,0:T(1,128)S(1)}, u32[]{:S(2)}, u32[]{:S(2)}) async-start(f32[16,1,1152]{2,1,0:T(1,128)} %bitcast), calls=%async_computation.1 | async-start | bytes 147456 | tf_op jit(solution)/shard_map/all_to_all | solution.py:644
  24.9 3.1 %collective-permute-start = (f32[28,8,128]{2,1,0:T(8,128)S(1)}, f32[28,8,128]{2,1,0:T(8,128)S(1)}, u32[]{:S(2)}, u32[]{:S(2)}) collective-permute-start(f32[28,8,128]{2,1,0:T(8,128)S(1)} %get-tuple-element.15), channel_id=1, source_target_pairs={{1,0},{2,1},{3,2},{4,3},{5,4},{6,5},{7,6},{8,7},{9,8},{10,9},{11,1... | collective-permute-start | bytes 344072 | tf_op jit(solution)/shard_map/ppermute | solution.py:651
  28.0 1.8 %collective-permute-done.halo_ref = f32[28,8,128]{2,1,0:T(8,128)S(1)} collective-permute-done((f32[28,8,128]{2,1,0:T(8,128)S(1)}, f32[28,8,128]{2,1,0:T(8,128)S(1)}, u32[]{:S(2)}, u32[]{:S(2)}) %collective-permute-start) | collective-permute-done | bytes 114720 | tf_op jit(solution)/shard_map/ppermute | solution.py:651
  29.8 2.0 %all-to-all-done.1 = f32[16,1,1152]{2,1,0:T(1,128)S(1)} async-done(((f32[16,1,1152]{2,1,0:T(1,128)}), f32[16,1,1152]{2,1,0:T(1,128)S(1)}, u32[]{:S(2)}, u32[]{:S(2)}) %all-to-all-start.1) | async-done | bytes 73760 | tf_op jit(solution)/shard_map/all_to_all | solution.py:644
  31.9 12.0 %collective-permute-start.1 = (f32[68,8,128]{2,1,0:T(8,128)S(1)}, f32[68,8,128]{2,1,0:T(8,128)S(1)}, u32[]{:S(2)}, u32[]{:S(2)}) collective-permute-start(f32[68,8,128]{2,1,0:T(8,128)S(1)} %pack.1.packed_ref), channel_id=1, source_target_pairs={{0,64},{64,0},{128,192},{192,128},{256,320},{320,256},{384,448},{4... | collective-permute-start | bytes 835592 | tf_op jit(solution)/shard_map/ppermute | solution.py:655
  43.9 0.3 near.1
  44.1 0.9 %collective-permute-done.1.swapped_ref = f32[68,8,128]{2,1,0:T(8,128)S(1)} collective-permute-done((f32[68,8,128]{2,1,0:T(8,128)S(1)}, f32[68,8,128]{2,1,0:T(8,128)S(1)}, u32[]{:S(2)}, u32[]{:S(2)}) %collective-permute-start.1) | collective-permute-done | bytes 278560 | tf_op jit(solution)/shard_map/ppermute | solution.py:655
  45.0 2.5 %final.1 = (f32[16,32,128]{2,1,0:T(8,128)}, f32[16,32,128]{2,1,0:T(8,128)}) custom-call(f32[68,8,128]{2,1,0:T(8,128)S(1)} %pack.1.packed_ref, f32[68,8,128]{2,1,0:T(8,128)S(1)} %collective-permute-done.1.swapped_ref, f32[8,8,128]{2,1,0:T(8,128)S(1)} %get-tuple-element.17.mine2_ref, f32[16,4,8,128]{3,2,1,0:T(8,128)S(1)} %get-tuple-element.24.own0_ref, ...), custom_call_target="tpu_custom_call" | custom-call | tf_op jit(solution)/shard_map/final/pallas_call | solution.py:616
  (1 shorter events, 0.0 us)
Async XLA Ops:
  1.9 17.5 %copy-start = (f32[16,32,128]{2,1,0:T(8,128)S(1)}, f32[16,32,128]{2,1,0:T(8,128)}, u32[]{:S(2)}) copy-start(f32[16,32,128]{2,1,0:T(8,128)} %guess_ref.3) | copy-start | bytes 786436
  21.4 10.5 %all-to-all-start.1 = ((f32[16,1,1152]{2,1,0:T(1,128)}), f32[16,1,1152]{2,1,0:T(1,128)S(1)}, u32[]{:S(2)}, u32[]{:S(2)}) async-start(f32[16,1,1152]{2,1,0:T(1,128)} %bitcast), calls=%async_computation.1 | async-start | bytes 147456 | tf_op jit(solution)/shard_map/all_to_all | solution.py:644
  24.9 4.9 %collective-permute-start = (f32[28,8,128]{2,1,0:T(8,128)S(1)}, f32[28,8,128]{2,1,0:T(8,128)S(1)}, u32[]{:S(2)}, u32[]{:S(2)}) collective-permute-start(f32[28,8,128]{2,1,0:T(8,128)S(1)} %get-tuple-element.15), channel_id=1, source_target_pairs={{1,0},{2,1},{3,2},{4,3},{5,4},{6,5},{7,6},{8,7},{9,8},{10,9},{11,1... | collective-permute-start | bytes 344072 | tf_op jit(solution)/shard_map/ppermute | solution.py:651
  31.9 13.2 %collective-permute-start.1 = (f32[68,8,128]{2,1,0:T(8,128)S(1)}, f32[68,8,128]{2,1,0:T(8,128)S(1)}, u32[]{:S(2)}, u32[]{:S(2)}) collective-permute-start(f32[68,8,128]{2,1,0:T(8,128)S(1)} %pack.1.packed_ref), channel_id=1, source_target_pairs={{0,64},{64,0},{128,192},{192,128},{256,320},{320,256},{384,448},{4... | collective-permute-start | bytes 835592 | tf_op jit(solution)/shard_map/ppermute | solution.py:655

commit v10 on v9

--- a/solution.py
+++ b/solution.py
@@ -270,8 +270,8 @@
 
 
 def far_kernel(
-    part_ref, guess_ref, far_ref, halo_ref, minus_ref, b2_ref,
-    d_ref, t_ref, r_ref, b1_ref, t1_ref, r1_ref, sum_ref,
+    part_ref, guess_ref, far_hbm, halo_ref, minus_ref, b2_ref,
+    d_ref, t_ref, r_ref, b1_ref, t1_ref, r1_ref, sum_ref, far_ref, sem,
 ):
     inside0, inside1, inside2 = masks(lax.axis_index("dom"))
     for i in range(ROWS // 16):
@@ -335,12 +335,14 @@
         target = (ROOT - half + i) % RING
         far_ref[pl.ds(9 * i, 8), :] = jnp.where(target > me, above, below)
         far_ref[pl.ds(9 * i + 8, 1), :] = last
+    copy = pltpu.make_async_copy(far_ref, far_hbm, sem)
+    copy.start()
 
     for group in range(2):
         packed = b2[4 * group - 2]
         for p in range(1, 4):
             packed = jnp.where((lane & 3) == p, b2[4 * group - 2 + p], packed)
-        halo_ref[26 + group] = packed
+        halo_ref[24 + group] = packed
 
     even = (lane & 1) == 0
 
@@ -352,7 +354,7 @@
             two = geometric(b1, t1, r1, first1 + 2 * pair + 1, 2)
             for q in range(2):
                 halo_ref[16 + 2 * pair + q] = jnp.where(even, one[q], two[q])
-        halo_ref[pl.ds(22, 4)] = 0.25 * refine_y((minus_ref[2 * plane], minus_ref[2 * plane + 1]))
+        halo_ref[22], halo_ref[23] = minus_ref[2 * plane], minus_ref[2 * plane + 1]
 
     @pl.when(core == 0)
     def _():
@@ -361,6 +363,8 @@
     @pl.when(core == 1)
     def _():
         edges(16, 7, 3)
+
+    copy.wait()
 
 
 def far_part(parts, guess):
@@ -369,13 +373,15 @@
     return pl.pallas_call(
         far_kernel,
         out_shape=(
-            shape(9 * RING, 128), shape(28, 8, 128), shape(8, 8, 128), shape(8, 8, 128),
+            shape(9 * RING, 128), shape(26, 8, 128), shape(8, 8, 128), shape(8, 8, 128),
             shape(18, 4, 8, 128), shape(20, 4, 8, 128), shape(22, 4, 8, 128),
             shape(12, 2, 8, 128), shape(14, 2, 8, 128), shape(16, 2, 8, 128),
         ),
         in_specs=[vmem, vmem],
-        out_specs=(vmem,) * 10,
-        scratch_shapes=[pltpu.VMEM((ROWS, 128), F32)],
+        out_specs=(pl.BlockSpec(memory_space=pltpu.HBM),) + (vmem,) * 9,
+        scratch_shapes=[
+            pltpu.VMEM((ROWS, 128), F32), pltpu.VMEM((9 * RING, 128), F32), pltpu.SemaphoreType.DMA,
+        ],
         compiler_params=pltpu.CompilerParams(vmem_limit_bytes=32 * 2**20),
         name="far",
     )(parts, guess)
@@ -414,18 +420,18 @@
 
 
 def pack_kernel(mine_ref, halo_ref, minus_ref, out_ref):
-    out_ref[pl.ds(0, 28)] = halo_ref[...]
-    out_ref[pl.ds(28, 8)] = minus_ref[...]
+    out_ref[pl.ds(0, 26)] = halo_ref[...]
+    out_ref[pl.ds(26, 8)] = minus_ref[...]
     for i in range(RING):
-        out_ref[36 + 2 * i] = mine_ref[pl.ds(9 * i, 8), :]
-        out_ref[37 + 2 * i, pl.ds(0, 1), :] = mine_ref[pl.ds(9 * i + 8, 1), :]
+        out_ref[34 + i] = mine_ref[pl.ds(9 * i, 8), :]
+        out_ref[50 + i // 8, pl.ds(i % 8, 1), :] = mine_ref[pl.ds(9 * i + 8, 1), :]
 
 
 def pack(mine, halo, minus):
     vmem = pl.BlockSpec(memory_space=pltpu.VMEM)
     return pl.pallas_call(
         pack_kernel,
-        out_shape=jax.ShapeDtypeStruct((36 + 2 * RING, 8, 128), F32),
+        out_shape=jax.ShapeDtypeStruct((52, 8, 128), F32),
         in_specs=[vmem] * 3,
         out_specs=vmem,
         compiler_params=pltpu.CompilerParams(vmem_limit_bytes=32 * 2**20),
@@ -451,15 +457,15 @@
         j = x % 4
         pair = []
         for p in range(2):
-            own = packed_ref[28 + 2 * j + p]
-            pair.append(jnp.where(lower == (x < 4), own, swapped_ref[28 + 2 * j + p]))
+            own = packed_ref[26 + 2 * j + p]
+            pair.append(jnp.where(lower == (x < 4), own, swapped_ref[26 + 2 * j + p]))
         minus.append(refine_y(pair))
     for k in range(16):
         mag = refine_x(minus, k)
         if k == 0:
-            mag = mag + low(pl.ds(22, 4))
+            mag = mag + 0.25 * refine_y((low(22), low(23)))
         if k == 15:
-            mag = mag + high(pl.ds(22, 4))
+            mag = mag + 0.25 * refine_y((high(22), high(23)))
         for q in range(4):
             mag_ref[k, pl.ds(q, 8, stride=4), :] = mag[q]
     copies = [pltpu.make_async_copy(mag_ref, mag_hbm, sems.at[4])]
@@ -486,13 +492,9 @@
         at = jnp.clip(jnp.where(aligned, at, wanted - other_first), 0, RING - 1)
         slot = (at + RING - jnp.where(aligned, ROOT, ROOT - RING // 2)) % RING
         there = (wanted >= 0) & (wanted < DOMS)
-        for part, ref in ((0, body), (1, last)):
-            rows = pl.ds(0, 1 if part else 8)
-            v = jnp.where(
-                aligned == lower,
-                packed_ref[36 + 2 * slot + part, rows, :],
-                swapped_ref[36 + 2 * slot + part, rows, :],
-            )
+        places = ((body, 34 + slot, pl.ds(0, 8)), (last, 50 + slot // 8, pl.ds(slot % 8, 1)))
+        for ref, tile, rows in places:
+            v = jnp.where(aligned == lower, packed_ref[tile, rows, :], swapped_ref[tile, rows, :])
             ref[step] = jnp.where(there, v, 0.0)
 
     def unpack4(v, p):
@@ -503,8 +505,8 @@
     inside2, inside3, inside4 = masked(4), masked(2), masked(1)
     b2 = {k: mine2_ref[k + 2] for k in range(-2, 6)}
     tiles = (
-        (-5, 3, pltpu.roll(low(26), 127, 1) + body[-2]), (-2, 4, low(27)),
-        (2, 4, high(26)), (6, 3, high(27) + body[2]),
+        (-5, 3, pltpu.roll(low(24), 127, 1) + body[-2]), (-2, 4, low(25)),
+        (2, 4, high(24)), (6, 3, high(25) + body[2]),
     )
     for start, count, tile in tiles:
         for p in range(count):

time: 47.9 us -> 47.6 us (level)
  no operation moved by 1% of the time
where the time goes in v10:
time: 47.6 us; the launch traced here: 47.3 us
  starting transfers between devices  18.6 us (39%)
  blocking collectives  17.5 us (37%)
  Pallas kernels  5.92 us (12%)
  waiting for transfers between devices  4.61 us (10%)
  between operations  0.69 us (1%)
    all_to_all x1, blocking collectives, on_device(): lax.all_to_all(density(spin_group, occupation, orbitals), 'band', 0, 0)  17.5 us
    ppermute x1, starting transfers between devices, on_device(): swapped = lax.ppermute(packed, 'band', swap)  11.9 us
    all_to_all x1, starting transfers between devices, on_device(): lax.all_to_all(far.reshape(RING, 9 * 128), ('band', 'dom'), 0, 0, axis_in...  3.52 us
    ppermute x1, starting transfers between devices, on_device(): halo = lax.ppermute(to_send, ('band', 'dom'), edges)  3.14 us
    pallas_call x1, Pallas kernels, final_part(): pl.pallas_call(final_kernel, out_shape=(shape(16, 32, 128), shape(16, 32,...  2.52 us
    all_to_all x1, waiting for transfers between devices, on_device(): lax.all_to_all(far.reshape(RING, 9 * 128), ('band', 'dom'), 0, 0, axis_in...  2.12 us
    pallas_call x1, Pallas kernels, far_part(): pl.pallas_call(far_kernel, out_shape=(shape(9 * RING, 128), shape(26, 8,...  1.85 us
    ppermute x1, waiting for transfers between devices, on_device(): halo = lax.ppermute(to_send, ('band', 'dom'), edges)  1.69 us
  transfers between devices with their start and end apart: 3, of which 3 were waited for; matrix products, arithmetic and copies ran while one was open for 0% of the time, Pallas kernels for 1%

profile of v10, /device:TPU:1, one launch (start us, length us, event | category | flops | bytes accessed | tf_op | source)
XLA Modules:
  0.0 47.3 jit_solution(1546037535070323208)
XLA Ops:
  0.6 1.3 %density.1 = f32[8,96,128]{2,1,0:T(8,128)S(1)} custom-call(s32[8]{0:T(128)} %spin_hbm.1, s32[8]{0:T(128)} %occ_hbm.1, f32[8,8,16,64]{3,2,1,0:T(8,128)} %orb_hbm.1), custom_call_target="tpu_custom_call" | custom-call | tf_op jit(solution)/shard_map/density/pallas_call | solution.py:252
  1.9 0.0 copy-start
  1.9 17.5 %all_to_all.14.part_ref = f32[8,96,128]{2,1,0:T(8,128)S(1)} all-to-all(f32[8,96,128]{2,1,0:T(8,128)S(1)} %density.1), channel_id=1, replica_groups=mesh['band'=8,'dom'=64] {'band'}, dimensions={0} | all-to-all | bytes 786432 | tf_op jit(solution)/shard_map/all_to_all | solution.py:637
  19.4 0.0 copy-done
  19.4 1.8 %far.1 = (f32[144,128]{1,0:T(8,128)}, f32[26,8,128]{2,1,0:T(8,128)S(1)}, f32[8,8,128]{2,1,0:T(8,128)S(1)}, f32[8,8,128]{2,1,0:T(8,128)S(1)}, f32[18,4,8,128]{3,2...) custom-call(f32[8,96,128]{2,1,0:T(8,128)S(1)} %all_to_all.14.part_re, ...), custom_call_target="tpu_custom_call" | custom-call | tf_op jit(solution)/shard_map/far/pallas_call | solution.py:373
  21.3 3.5 %all-to-all-start.1 = ((f32[16,1,1152]{2,1,0:T(1,128)}), f32[16,1,1152]{2,1,0:T(1,128)S(1)}, u32[]{:S(2)}, u32[]{:S(2)}) async-start(f32[16,1,1152]{2,1,0:T(1,128)} %bitcast), calls=%async_computation.1 | async-start | bytes 147456 | tf_op jit(solution)/shard_map/all_to_all | solution.py:646
  24.8 3.1 %collective-permute-start = (f32[26,8,128]{2,1,0:T(8,128)S(1)}, f32[26,8,128]{2,1,0:T(8,128)S(1)}, u32[]{:S(2)}, u32[]{:S(2)}) collective-permute-start(f32[26,8,128]{2,1,0:T(8,128)S(1)} %get-tuple-element.15), channel_id=1, source_target_pairs={{1,0},{2,1},{3,2},{4,3},{5,4},{6,5},{7,6},{8,7},{9,8},{10,9},{11,1... | collective-permute-start | bytes 319496 | tf_op jit(solution)/shard_map/ppermute | solution.py:653
  27.9 1.7 %collective-permute-done.halo_ref = f32[26,8,128]{2,1,0:T(8,128)S(1)} collective-permute-done((f32[26,8,128]{2,1,0:T(8,128)S(1)}, f32[26,8,128]{2,1,0:T(8,128)S(1)}, u32[]{:S(2)}, u32[]{:S(2)}) %collective-permute-start) | collective-permute-done | bytes 106528 | tf_op jit(solution)/shard_map/ppermute | solution.py:653
  29.6 2.1 %all-to-all-done.1 = f32[16,1,1152]{2,1,0:T(1,128)S(1)} async-done(((f32[16,1,1152]{2,1,0:T(1,128)}), f32[16,1,1152]{2,1,0:T(1,128)S(1)}, u32[]{:S(2)}, u32[]{:S(2)}) %all-to-all-start.1) | async-done | bytes 73760 | tf_op jit(solution)/shard_map/all_to_all | solution.py:646
  31.8 11.9 %collective-permute-start.1 = (f32[52,8,128]{2,1,0:T(8,128)S(1)}, f32[52,8,128]{2,1,0:T(8,128)S(1)}, u32[]{:S(2)}, u32[]{:S(2)}) collective-permute-start(f32[52,8,128]{2,1,0:T(8,128)S(1)} %pack.1.packed_ref), channel_id=1, source_target_pairs={{0,64},{64,0},{128,192},{192,128},{256,320},{320,256},{384,448},{4... | collective-permute-start | bytes 638984 | tf_op jit(solution)/shard_map/ppermute | solution.py:657
  43.7 0.3 near.1
  44.0 0.8 %collective-permute-done.1.swapped_ref = f32[52,8,128]{2,1,0:T(8,128)S(1)} collective-permute-done((f32[52,8,128]{2,1,0:T(8,128)S(1)}, f32[52,8,128]{2,1,0:T(8,128)S(1)}, u32[]{:S(2)}, u32[]{:S(2)}) %collective-permute-start.1) | collective-permute-done | bytes 213024 | tf_op jit(solution)/shard_map/ppermute | solution.py:657
  44.8 2.5 %final.1 = (f32[16,32,128]{2,1,0:T(8,128)}, f32[16,32,128]{2,1,0:T(8,128)}) custom-call(f32[52,8,128]{2,1,0:T(8,128)S(1)} %pack.1.packed_ref, f32[52,8,128]{2,1,0:T(8,128)S(1)} %collective-permute-done.1.swapped_ref, f32[8,8,128]{2,1,0:T(8,128)S(1)} %get-tuple-element.17.mine2_ref, f32[16,4,8,128]{3,2,1,0:T(8,128)S(1)} %get-tuple-element.24.own0_ref, ...), custom_call_target="tpu_custom_call" | custom-call | tf_op jit(solution)/shard_map/final/pallas_call | solution.py:618
  (1 shorter events, 0.0 us)
Async XLA Ops:
  1.9 17.5 %copy-start = (f32[16,32,128]{2,1,0:T(8,128)S(1)}, f32[16,32,128]{2,1,0:T(8,128)}, u32[]{:S(2)}) copy-start(f32[16,32,128]{2,1,0:T(8,128)} %guess_ref.3) | copy-start | bytes 786436
  21.3 10.5 %all-to-all-start.1 = ((f32[16,1,1152]{2,1,0:T(1,128)}), f32[16,1,1152]{2,1,0:T(1,128)S(1)}, u32[]{:S(2)}, u32[]{:S(2)}) async-start(f32[16,1,1152]{2,1,0:T(1,128)} %bitcast), calls=%async_computation.1 | async-start | bytes 147456 | tf_op jit(solution)/shard_map/all_to_all | solution.py:646
  24.8 4.8 %collective-permute-start = (f32[26,8,128]{2,1,0:T(8,128)S(1)}, f32[26,8,128]{2,1,0:T(8,128)S(1)}, u32[]{:S(2)}, u32[]{:S(2)}) collective-permute-start(f32[26,8,128]{2,1,0:T(8,128)S(1)} %get-tuple-element.15), channel_id=1, source_target_pairs={{1,0},{2,1},{3,2},{4,3},{5,4},{6,5},{7,6},{8,7},{9,8},{10,9},{11,1... | collective-permute-start | bytes 319496 | tf_op jit(solution)/shard_map/ppermute | solution.py:653
  31.8 13.0 %collective-permute-start.1 = (f32[52,8,128]{2,1,0:T(8,128)S(1)}, f32[52,8,128]{2,1,0:T(8,128)S(1)}, u32[]{:S(2)}, u32[]{:S(2)}) collective-permute-start(f32[52,8,128]{2,1,0:T(8,128)S(1)} %pack.1.packed_ref), channel_id=1, source_target_pairs={{0,64},{64,0},{128,192},{192,128},{256,320},{320,256},{384,448},{4... | collective-permute-start | bytes 638984 | tf_op jit(solution)/shard_map/ppermute | solution.py:657

commit v11 on v10

--- a/solution.py
+++ b/solution.py
@@ -452,6 +452,62 @@
     def low(i):
         return jnp.where(lower, swapped_ref[i], packed_ref[i])
 
+    def masked(count):
+        first, last = -dom * count, (DOMS - dom) * count
+        def mask(k, v):
+            if 0 <= k < count:
+                return v
+            ok = (k >= first) & (k < last)
+            return jnp.where(ok, v, 0.0)
+        return mask
+
+    lane, row = lanes_of((8, 128)), rows_of((8, 128))
+    spot = dom % RING
+    first = dom - spot
+    other_first = first + jnp.where(spot < RING // 2, -(RING // 2), RING // 2)
+    body, last = {}, {}
+    for step in range(-REACH, REACH + 1):
+        wanted = dom + step
+        at = wanted - first
+        aligned = (at >= 0) & (at < RING)
+        at = jnp.clip(jnp.where(aligned, at, wanted - other_first), 0, RING - 1)
+        slot = (at + RING - jnp.where(aligned, ROOT, ROOT - RING // 2)) % RING
+        there = (wanted >= 0) & (wanted < DOMS)
+        places = ((body, 34 + slot, pl.ds(0, 8)), (last, 50 + slot // 8, pl.ds(slot % 8, 1)))
+        for ref, tile, rows in places:
+            v = jnp.where(aligned == lower, packed_ref[tile, rows, :], swapped_ref[tile, rows, :])
+            ref[step] = jnp.where(there, v, 0.0)
+
+    def unpack4(v, p):
+        v = jnp.where((lane & 3) == p, v, 0.0)
+        v = v + pltpu.roll(v, 1 if p % 2 == 0 else 127, 1)
+        return v + pltpu.roll(v, 2 if p < 2 else 126, 1)
+
+    inside2, inside3, inside4 = masked(4), masked(2), masked(1)
+    b2 = {k: mine2_ref[k + 2] for k in range(-2, 6)}
+    tiles = (
+        (-5, 3, pltpu.roll(low(24), 127, 1) + body[-2]), (-2, 4, low(25)),
+        (2, 4, high(24)), (6, 3, high(25) + body[2]),
+    )
+    for start, count, tile in tiles:
+        for p in range(count):
+            k, v = start + p, unpack4(tile, p)
+            b2[k] = b2[k] + v if k in b2 else v
+    t2 = run_T(b2, range(-4, 8), 4, mask=inside2)
+    r2 = run_T(t2, range(-2, 6), 4)
+
+    b3 = {}
+    for pair in range(-6, 7):
+        both = jnp.where((row & 1) == 0, body[pair + 1], body[pair])
+        both = pair_y(jnp.where((lane & 3) == 3, both, 0.0), 1)
+        tail = jnp.broadcast_to(last[pair - 1], (8, 128))
+        for n in range(2):
+            v = jnp.where((lane & 7) == 4 * n + 3, both, 0.0)
+            v = v + jnp.where((lane & 7) == 4 * n + (row >> 1), tail, 0.0)
+            b3[2 * pair + n] = pair_z(pair_z(pair_z(v, 1), 2), 4)
+    t3 = run_T(b3, range(-11, 13), 8, 2, inside3)
+    r3 = run_T(t3, range(-10, 12), 8, 2)
+
     minus = []
     for x in range(8):
         j = x % 4
@@ -470,62 +526,6 @@
             mag_ref[k, pl.ds(q, 8, stride=4), :] = mag[q]
     copies = [pltpu.make_async_copy(mag_ref, mag_hbm, sems.at[4])]
     copies[0].start()
-
-    def masked(count):
-        first, last = -dom * count, (DOMS - dom) * count
-        def mask(k, v):
-            if 0 <= k < count:
-                return v
-            ok = (k >= first) & (k < last)
-            return jnp.where(ok, v, 0.0)
-        return mask
-
-    lane, row = lanes_of((8, 128)), rows_of((8, 128))
-    spot = dom % RING
-    first = dom - spot
-    other_first = first + jnp.where(spot < RING // 2, -(RING // 2), RING // 2)
-    body, last = {}, {}
-    for step in range(-REACH, REACH + 1):
-        wanted = dom + step
-        at = wanted - first
-        aligned = (at >= 0) & (at < RING)
-        at = jnp.clip(jnp.where(aligned, at, wanted - other_first), 0, RING - 1)
-        slot = (at + RING - jnp.where(aligned, ROOT, ROOT - RING // 2)) % RING
-        there = (wanted >= 0) & (wanted < DOMS)
-        places = ((body, 34 + slot, pl.ds(0, 8)), (last, 50 + slot // 8, pl.ds(slot % 8, 1)))
-        for ref, tile, rows in places:
-            v = jnp.where(aligned == lower, packed_ref[tile, rows, :], swapped_ref[tile, rows, :])
-            ref[step] = jnp.where(there, v, 0.0)
-
-    def unpack4(v, p):
-        v = jnp.where((lane & 3) == p, v, 0.0)
-        v = v + pltpu.roll(v, 1 if p % 2 == 0 else 127, 1)
-        return v + pltpu.roll(v, 2 if p < 2 else 126, 1)
-
-    inside2, inside3, inside4 = masked(4), masked(2), masked(1)
-    b2 = {k: mine2_ref[k + 2] for k in range(-2, 6)}
-    tiles = (
-        (-5, 3, pltpu.roll(low(24), 127, 1) + body[-2]), (-2, 4, low(25)),
-        (2, 4, high(24)), (6, 3, high(25) + body[2]),
-    )
-    for start, count, tile in tiles:
-        for p in range(count):
-            k, v = start + p, unpack4(tile, p)
-            b2[k] = b2[k] + v if k in b2 else v
-    t2 = run_T(b2, range(-4, 8), 4, mask=inside2)
-    r2 = run_T(t2, range(-2, 6), 4)
-
-    b3 = {}
-    for pair in range(-6, 7):
-        both = jnp.where((row & 1) == 0, body[pair + 1], body[pair])
-        both = pair_y(jnp.where((lane & 3) == 3, both, 0.0), 1)
-        tail = jnp.broadcast_to(last[pair - 1], (8, 128))
-        for n in range(2):
-            v = jnp.where((lane & 7) == 4 * n + 3, both, 0.0)
-            v = v + jnp.where((lane & 7) == 4 * n + (row >> 1), tail, 0.0)
-            b3[2 * pair + n] = pair_z(pair_z(pair_z(v, 1), 2), 4)
-    t3 = run_T(b3, range(-11, 13), 8, 2, inside3)
-    r3 = run_T(t3, range(-10, 12), 8, 2)
 
     b4 = {}
     for k in range(-5, 6):

time: 47.6 us -> 47.6 us (level)
  no operation moved by 1% of the time
where the time goes in v11:
time: 47.6 us; the launch traced here: 47.3 us
  starting transfers between devices  18.6 us (39%)
  blocking collectives  17.5 us (37%)
  Pallas kernels  5.92 us (12%)
  waiting for transfers between devices  4.61 us (10%)
  between operations  0.69 us (1%)
    all_to_all x1, blocking collectives, on_device(): lax.all_to_all(density(spin_group, occupation, orbitals), 'band', 0, 0)  17.5 us
    ppermute x1, starting transfers between devices, on_device(): swapped = lax.ppermute(packed, 'band', swap)  11.9 us
    all_to_all x1, starting transfers between devices, on_device(): lax.all_to_all(far.reshape(RING, 9 * 128), ('band', 'dom'), 0, 0, axis_in...  3.52 us
    ppermute x1, starting transfers between devices, on_device(): halo = lax.ppermute(to_send, ('band', 'dom'), edges)  3.14 us
    pallas_call x1, Pallas kernels, final_part(): pl.pallas_call(final_kernel, out_shape=(shape(16, 32, 128), shape(16, 32,...  2.52 us
    all_to_all x1, waiting for transfers between devices, on_device(): lax.all_to_all(far.reshape(RING, 9 * 128), ('band', 'dom'), 0, 0, axis_in...  2.12 us
    pallas_call x1, Pallas kernels, far_part(): pl.pallas_call(far_kernel, out_shape=(shape(9 * RING, 128), shape(26, 8,...  1.85 us
    ppermute x1, waiting for transfers between devices, on_device(): halo = lax.ppermute(to_send, ('band', 'dom'), edges)  1.69 us
  transfers between devices with their start and end apart: 3, of which 3 were waited for; matrix products, arithmetic and copies ran while one was open for 0% of the time, Pallas kernels for 1%

profile of v11, /device:TPU:1, one launch (start us, length us, event | category | flops | bytes accessed | tf_op | source)
XLA Modules:
  0.0 47.3 jit_solution(4898536303461284332)
XLA Ops:
  0.6 1.3 %density.1 = f32[8,96,128]{2,1,0:T(8,128)S(1)} custom-call(s32[8]{0:T(128)} %spin_hbm.1, s32[8]{0:T(128)} %occ_hbm.1, f32[8,8,16,64]{3,2,1,0:T(8,128)} %orb_hbm.1), custom_call_target="tpu_custom_call" | custom-call | tf_op jit(solution)/shard_map/density/pallas_call | solution.py:252
  1.9 0.0 copy-start
  1.9 17.5 %all_to_all.14.part_ref = f32[8,96,128]{2,1,0:T(8,128)S(1)} all-to-all(f32[8,96,128]{2,1,0:T(8,128)S(1)} %density.1), channel_id=1, replica_groups=mesh['band'=8,'dom'=64] {'band'}, dimensions={0} | all-to-all | bytes 786432 | tf_op jit(solution)/shard_map/all_to_all | solution.py:637
  19.4 0.0 copy-done
  19.4 1.8 %far.1 = (f32[144,128]{1,0:T(8,128)}, f32[26,8,128]{2,1,0:T(8,128)S(1)}, f32[8,8,128]{2,1,0:T(8,128)S(1)}, f32[8,8,128]{2,1,0:T(8,128)S(1)}, f32[18,4,8,128]{3,2...) custom-call(f32[8,96,128]{2,1,0:T(8,128)S(1)} %all_to_all.14.part_re, ...), custom_call_target="tpu_custom_call" | custom-call | tf_op jit(solution)/shard_map/far/pallas_call | solution.py:373
  21.3 3.5 %all-to-all-start.1 = ((f32[16,1,1152]{2,1,0:T(1,128)}), f32[16,1,1152]{2,1,0:T(1,128)S(1)}, u32[]{:S(2)}, u32[]{:S(2)}) async-start(f32[16,1,1152]{2,1,0:T(1,128)} %bitcast), calls=%async_computation.1 | async-start | bytes 147456 | tf_op jit(solution)/shard_map/all_to_all | solution.py:646
  24.8 3.1 %collective-permute-start = (f32[26,8,128]{2,1,0:T(8,128)S(1)}, f32[26,8,128]{2,1,0:T(8,128)S(1)}, u32[]{:S(2)}, u32[]{:S(2)}) collective-permute-start(f32[26,8,128]{2,1,0:T(8,128)S(1)} %get-tuple-element.15), channel_id=1, source_target_pairs={{1,0},{2,1},{3,2},{4,3},{5,4},{6,5},{7,6},{8,7},{9,8},{10,9},{11,1... | collective-permute-start | bytes 319496 | tf_op jit(solution)/shard_map/ppermute | solution.py:653
  27.9 1.7 %collective-permute-done.halo_ref = f32[26,8,128]{2,1,0:T(8,128)S(1)} collective-permute-done((f32[26,8,128]{2,1,0:T(8,128)S(1)}, f32[26,8,128]{2,1,0:T(8,128)S(1)}, u32[]{:S(2)}, u32[]{:S(2)}) %collective-permute-start) | collective-permute-done | bytes 106528 | tf_op jit(solution)/shard_map/ppermute | solution.py:653
  29.6 2.1 %all-to-all-done.1 = f32[16,1,1152]{2,1,0:T(1,128)S(1)} async-done(((f32[16,1,1152]{2,1,0:T(1,128)}), f32[16,1,1152]{2,1,0:T(1,128)S(1)}, u32[]{:S(2)}, u32[]{:S(2)}) %all-to-all-start.1) | async-done | bytes 73760 | tf_op jit(solution)/shard_map/all_to_all | solution.py:646
  31.8 11.9 %collective-permute-start.1 = (f32[52,8,128]{2,1,0:T(8,128)S(1)}, f32[52,8,128]{2,1,0:T(8,128)S(1)}, u32[]{:S(2)}, u32[]{:S(2)}) collective-permute-start(f32[52,8,128]{2,1,0:T(8,128)S(1)} %pack.1.packed_ref), channel_id=1, source_target_pairs={{0,64},{64,0},{128,192},{192,128},{256,320},{320,256},{384,448},{4... | collective-permute-start | bytes 638984 | tf_op jit(solution)/shard_map/ppermute | solution.py:657
  43.7 0.3 near.1
  44.0 0.8 %collective-permute-done.1.swapped_ref = f32[52,8,128]{2,1,0:T(8,128)S(1)} collective-permute-done((f32[52,8,128]{2,1,0:T(8,128)S(1)}, f32[52,8,128]{2,1,0:T(8,128)S(1)}, u32[]{:S(2)}, u32[]{:S(2)}) %collective-permute-start.1) | collective-permute-done | bytes 213024 | tf_op jit(solution)/shard_map/ppermute | solution.py:657
  44.8 2.5 %final.1 = (f32[16,32,128]{2,1,0:T(8,128)}, f32[16,32,128]{2,1,0:T(8,128)}) custom-call(f32[52,8,128]{2,1,0:T(8,128)S(1)} %pack.1.packed_ref, f32[52,8,128]{2,1,0:T(8,128)S(1)} %collective-permute-done.1.swapped_ref, f32[8,8,128]{2,1,0:T(8,128)S(1)} %get-tuple-element.17.mine2_ref, f32[16,4,8,128]{3,2,1,0:T(8,128)S(1)} %get-tuple-element.24.own0_ref, ...), custom_call_target="tpu_custom_call" | custom-call | tf_op jit(solution)/shard_map/final/pallas_call | solution.py:618
  (1 shorter events, 0.0 us)
Async XLA Ops:
  1.9 17.5 %copy-start = (f32[16,32,128]{2,1,0:T(8,128)S(1)}, f32[16,32,128]{2,1,0:T(8,128)}, u32[]{:S(2)}) copy-start(f32[16,32,128]{2,1,0:T(8,128)} %guess_ref.3) | copy-start | bytes 786436
  21.3 10.5 %all-to-all-start.1 = ((f32[16,1,1152]{2,1,0:T(1,128)}), f32[16,1,1152]{2,1,0:T(1,128)S(1)}, u32[]{:S(2)}, u32[]{:S(2)}) async-start(f32[16,1,1152]{2,1,0:T(1,128)} %bitcast), calls=%async_computation.1 | async-start | bytes 147456 | tf_op jit(solution)/shard_map/all_to_all | solution.py:646
  24.8 4.8 %collective-permute-start = (f32[26,8,128]{2,1,0:T(8,128)S(1)}, f32[26,8,128]{2,1,0:T(8,128)S(1)}, u32[]{:S(2)}, u32[]{:S(2)}) collective-permute-start(f32[26,8,128]{2,1,0:T(8,128)S(1)} %get-tuple-element.15), channel_id=1, source_target_pairs={{1,0},{2,1},{3,2},{4,3},{5,4},{6,5},{7,6},{8,7},{9,8},{10,9},{11,1... | collective-permute-start | bytes 319496 | tf_op jit(solution)/shard_map/ppermute | solution.py:653
  31.8 13.0 %collective-permute-start.1 = (f32[52,8,128]{2,1,0:T(8,128)S(1)}, f32[52,8,128]{2,1,0:T(8,128)S(1)}, u32[]{:S(2)}, u32[]{:S(2)}) collective-permute-start(f32[52,8,128]{2,1,0:T(8,128)S(1)} %pack.1.packed_ref), channel_id=1, source_target_pairs={{0,64},{64,0},{128,192},{192,128},{256,320},{320,256},{384,448},{4... | collective-permute-start | bytes 638984 | tf_op jit(solution)/shard_map/ppermute | solution.py:657

commit v12 on v10

--- a/solution.py
+++ b/solution.py
@@ -520,10 +520,12 @@
         both = jnp.where((row & 1) == 0, body[pair + 1], body[pair])
         both = pair_y(jnp.where((lane & 3) == 3, both, 0.0), 1)
         tail = jnp.broadcast_to(last[pair - 1], (8, 128))
-        for n in range(2):
-            v = jnp.where((lane & 7) == 4 * n + 3, both, 0.0)
-            v = v + jnp.where((lane & 7) == 4 * n + (row >> 1), tail, 0.0)
-            b3[2 * pair + n] = pair_z(pair_z(pair_z(v, 1), 2), 4)
+        spot8 = (lane & 7) - 4 * (row & 1)
+        v = jnp.where(spot8 == 3, both, 0.0) + jnp.where(spot8 == (row >> 1), tail, 0.0)
+        v = pair_z(pair_z(pair_z(v, 1), 2), 4)
+        even = (row & 1) == 0
+        w = jnp.where(even, pltpu.roll(v, 7, 0), pltpu.roll(v, 1, 0))
+        b3[2 * pair], b3[2 * pair + 1] = jnp.where(even, v, w), jnp.where(even, w, v)
     t3 = run_T(b3, range(-11, 13), 8, 2, inside3)
     r3 = run_T(t3, range(-10, 12), 8, 2)
 

time: 47.6 us -> 47.7 us (level)
  no operation moved by 1% of the time
where the time goes in v12:
time: 47.7 us; the launch traced here: 47.3 us
  starting transfers between devices  18.6 us (39%)
  blocking collectives  17.5 us (37%)
  Pallas kernels  5.97 us (13%)
  waiting for transfers between devices  4.61 us (10%)
  between operations  0.69 us (1%)
    all_to_all x1, blocking collectives, on_device(): lax.all_to_all(density(spin_group, occupation, orbitals), 'band', 0, 0)  17.5 us
    ppermute x1, starting transfers between devices, on_device(): swapped = lax.ppermute(packed, 'band', swap)  11.9 us
    all_to_all x1, starting transfers between devices, on_device(): lax.all_to_all(far.reshape(RING, 9 * 128), ('band', 'dom'), 0, 0, axis_in...  3.52 us
    ppermute x1, starting transfers between devices, on_device(): halo = lax.ppermute(to_send, ('band', 'dom'), edges)  3.14 us
    pallas_call x1, Pallas kernels, final_part(): pl.pallas_call(final_kernel, out_shape=(shape(16, 32, 128), shape(16, 32,...  2.57 us
    all_to_all x1, waiting for transfers between devices, on_device(): lax.all_to_all(far.reshape(RING, 9 * 128), ('band', 'dom'), 0, 0, axis_in...  2.12 us
    pallas_call x1, Pallas kernels, far_part(): pl.pallas_call(far_kernel, out_shape=(shape(9 * RING, 128), shape(26, 8,...  1.85 us
    ppermute x1, waiting for transfers between devices, on_device(): halo = lax.ppermute(to_send, ('band', 'dom'), edges)  1.69 us
  transfers between devices with their start and end apart: 3, of which 3 were waited for; matrix products, arithmetic and copies ran while one was open for 0% of the time, Pallas kernels for 1%

profile of v12, /device:TPU:1, one launch (start us, length us, event | category | flops | bytes accessed | tf_op | source)
XLA Modules:
  0.0 47.3 jit_solution(15706253404373141149)
XLA Ops:
  0.6 1.3 %density.1 = f32[8,96,128]{2,1,0:T(8,128)S(1)} custom-call(s32[8]{0:T(128)} %spin_hbm.1, s32[8]{0:T(128)} %occ_hbm.1, f32[8,8,16,64]{3,2,1,0:T(8,128)} %orb_hbm.1), custom_call_target="tpu_custom_call" | custom-call | tf_op jit(solution)/shard_map/density/pallas_call | solution.py:252
  1.9 0.0 copy-start
  1.9 17.5 %all_to_all.14.part_ref = f32[8,96,128]{2,1,0:T(8,128)S(1)} all-to-all(f32[8,96,128]{2,1,0:T(8,128)S(1)} %density.1), channel_id=1, replica_groups=mesh['band'=8,'dom'=64] {'band'}, dimensions={0} | all-to-all | bytes 786432 | tf_op jit(solution)/shard_map/all_to_all | solution.py:639
  19.4 0.0 copy-done
  19.4 1.8 %far.1 = (f32[144,128]{1,0:T(8,128)}, f32[26,8,128]{2,1,0:T(8,128)S(1)}, f32[8,8,128]{2,1,0:T(8,128)S(1)}, f32[8,8,128]{2,1,0:T(8,128)S(1)}, f32[18,4,8,128]{3,2...) custom-call(f32[8,96,128]{2,1,0:T(8,128)S(1)} %all_to_all.14.part_re, ...), custom_call_target="tpu_custom_call" | custom-call | tf_op jit(solution)/shard_map/far/pallas_call | solution.py:373
  21.3 3.5 %all-to-all-start.1 = ((f32[16,1,1152]{2,1,0:T(1,128)}), f32[16,1,1152]{2,1,0:T(1,128)S(1)}, u32[]{:S(2)}, u32[]{:S(2)}) async-start(f32[16,1,1152]{2,1,0:T(1,128)} %bitcast), calls=%async_computation.1 | async-start | bytes 147456 | tf_op jit(solution)/shard_map/all_to_all | solution.py:648
  24.8 3.1 %collective-permute-start = (f32[26,8,128]{2,1,0:T(8,128)S(1)}, f32[26,8,128]{2,1,0:T(8,128)S(1)}, u32[]{:S(2)}, u32[]{:S(2)}) collective-permute-start(f32[26,8,128]{2,1,0:T(8,128)S(1)} %get-tuple-element.15), channel_id=1, source_target_pairs={{1,0},{2,1},{3,2},{4,3},{5,4},{6,5},{7,6},{8,7},{9,8},{10,9},{11,1... | collective-permute-start | bytes 319496 | tf_op jit(solution)/shard_map/ppermute | solution.py:655
  27.9 1.7 %collective-permute-done.halo_ref = f32[26,8,128]{2,1,0:T(8,128)S(1)} collective-permute-done((f32[26,8,128]{2,1,0:T(8,128)S(1)}, f32[26,8,128]{2,1,0:T(8,128)S(1)}, u32[]{:S(2)}, u32[]{:S(2)}) %collective-permute-start) | collective-permute-done | bytes 106528 | tf_op jit(solution)/shard_map/ppermute | solution.py:655
  29.6 2.1 %all-to-all-done.1 = f32[16,1,1152]{2,1,0:T(1,128)S(1)} async-done(((f32[16,1,1152]{2,1,0:T(1,128)}), f32[16,1,1152]{2,1,0:T(1,128)S(1)}, u32[]{:S(2)}, u32[]{:S(2)}) %all-to-all-start.1) | async-done | bytes 73760 | tf_op jit(solution)/shard_map/all_to_all | solution.py:648
  31.8 11.9 %collective-permute-start.1 = (f32[52,8,128]{2,1,0:T(8,128)S(1)}, f32[52,8,128]{2,1,0:T(8,128)S(1)}, u32[]{:S(2)}, u32[]{:S(2)}) collective-permute-start(f32[52,8,128]{2,1,0:T(8,128)S(1)} %pack.1.packed_ref), channel_id=1, source_target_pairs={{0,64},{64,0},{128,192},{192,128},{256,320},{320,256},{384,448},{4... | collective-permute-start | bytes 638984 | tf_op jit(solution)/shard_map/ppermute | solution.py:659
  43.7 0.3 near.1
  44.0 0.8 %collective-permute-done.1.swapped_ref = f32[52,8,128]{2,1,0:T(8,128)S(1)} collective-permute-done((f32[52,8,128]{2,1,0:T(8,128)S(1)}, f32[52,8,128]{2,1,0:T(8,128)S(1)}, u32[]{:S(2)}, u32[]{:S(2)}) %collective-permute-start.1) | collective-permute-done | bytes 213024 | tf_op jit(solution)/shard_map/ppermute | solution.py:659
  44.8 2.6 %final.1 = (f32[16,32,128]{2,1,0:T(8,128)}, f32[16,32,128]{2,1,0:T(8,128)}) custom-call(f32[52,8,128]{2,1,0:T(8,128)S(1)} %pack.1.packed_ref, f32[52,8,128]{2,1,0:T(8,128)S(1)} %collective-permute-done.1.swapped_ref, f32[8,8,128]{2,1,0:T(8,128)S(1)} %get-tuple-element.17.mine2_ref, f32[16,4,8,128]{3,2,1,0:T(8,128)S(1)} %get-tuple-element.24.own0_ref, ...), custom_call_target="tpu_custom_call" | custom-call | tf_op jit(solution)/shard_map/final/pallas_call | solution.py:620
  (1 shorter events, 0.0 us)
Async XLA Ops:
  1.9 17.5 %copy-start = (f32[16,32,128]{2,1,0:T(8,128)S(1)}, f32[16,32,128]{2,1,0:T(8,128)}, u32[]{:S(2)}) copy-start(f32[16,32,128]{2,1,0:T(8,128)} %guess_ref.3) | copy-start | bytes 786436
  21.3 10.5 %all-to-all-start.1 = ((f32[16,1,1152]{2,1,0:T(1,128)}), f32[16,1,1152]{2,1,0:T(1,128)S(1)}, u32[]{:S(2)}, u32[]{:S(2)}) async-start(f32[16,1,1152]{2,1,0:T(1,128)} %bitcast), calls=%async_computation.1 | async-start | bytes 147456 | tf_op jit(solution)/shard_map/all_to_all | solution.py:648
  24.8 4.8 %collective-permute-start = (f32[26,8,128]{2,1,0:T(8,128)S(1)}, f32[26,8,128]{2,1,0:T(8,128)S(1)}, u32[]{:S(2)}, u32[]{:S(2)}) collective-permute-start(f32[26,8,128]{2,1,0:T(8,128)S(1)} %get-tuple-element.15), channel_id=1, source_target_pairs={{1,0},{2,1},{3,2},{4,3},{5,4},{6,5},{7,6},{8,7},{9,8},{10,9},{11,1... | collective-permute-start | bytes 319496 | tf_op jit(solution)/shard_map/ppermute | solution.py:655
  31.8 13.0 %collective-permute-start.1 = (f32[52,8,128]{2,1,0:T(8,128)S(1)}, f32[52,8,128]{2,1,0:T(8,128)S(1)}, u32[]{:S(2)}, u32[]{:S(2)}) collective-permute-start(f32[52,8,128]{2,1,0:T(8,128)S(1)} %pack.1.packed_ref), channel_id=1, source_target_pairs={{0,64},{64,0},{128,192},{192,128},{256,320},{320,256},{384,448},{4... | collective-permute-start | bytes 638984 | tf_op jit(solution)/shard_map/ppermute | solution.py:659
